TPU v7x, 128 devices: a whole 4x4x4 slice. The times are simulated.
128 devices in a mesh: dom: 8 (over z, x_lo), dp: 16 (over y, x_hi, core).
Axes of the slice: x: 4 (x_hi: 2, x_lo: 2; x = x_hi * 2 + x_lo), y: 4, z: 4, core: 2. Of those that a mesh axis runs over, the one named last changes fastest.
Arguments:
- state: bfloat16 [16, 8192, 512], P('dp', 'dom'), may hold values from -6 to 6
- blocks: bfloat16 [64, 4, 128, 128], P('dom'), may hold values from -0.25 to 0.25
- source: int32 [64, 4], P('dom'), may hold values from 0 to 11
- count: int32 [64], P('dom'), may hold values from 1 to 4, as said below
- cotangent: bfloat16 [16, 8192, 512], P('dp', 'dom'), may hold values from -6 to 6
- w_self: bfloat16 [3, 512, 512], replicated, may hold values from -0.25 to 0.25
- w_nbr: bfloat16 [3, 512, 512], replicated, may hold values from -0.25 to 0.25
Outputs:
- final_state: bfloat16 [16, 8192, 512], P('dp', 'dom')
- state_grad: bfloat16 [16, 8192, 512], P('dp', 'dom')
- self_grad: float32 [3, 512, 512], replicated
- nbr_grad: float32 [3, 512, 512], replicated
Inputs may be any that keep to these rules, and one draw needn't show every extreme that they name: `source`: index into the partition's extended tiles: the last 2 tiles of the previous partition (cyclically), then its own 8 tiles, then the first 2 tiles of the next partition. Slots at or past the count are unused.
All inputs are finite; a program needn't handle non-finite values.
Results may differ from a plain program's by a relative error of at most 0.015.
Values may be sent and summed in bfloat16 or wider, within the bound.
No kernel may reach another device: no remote copies, remote signals or barrier semaphores. Data moves between devices by JAX's collectives and lax.ppermute only.
A program may use at most 128 MiB of HBM per device.

v0:
```python
import math

import jax
import jax.numpy as jnp
from jax import lax
from jax.sharding import PartitionSpec as P

HALO = 2
LAYERS = 3


def with_halo(block, sides, width):
    for axis, dim in sides:
        count = lax.axis_size(axis)
        forward = [(i, i + 1) for i in range(count - 1)]
        forward.append((count - 1, 0))
        backward = [(target, source) for source, target in forward]
        low = lax.ppermute(
            lax.slice_in_dim(block, block.shape[dim] - width, None, axis=dim), axis, forward
        )
        high = lax.ppermute(lax.slice_in_dim(block, 0, width, axis=dim), axis, backward)
        block = jnp.concatenate([low, block, high], axis=dim)
    return block


def from_behind(block, axis, distance):
    devices = range(lax.axis_size(axis))
    route = [((i - distance) % len(devices), i) for i in devices]
    return lax.ppermute(block, axis, route)


def per_device(state, blocks, source, count, cotangent, w_self, w_nbr):
    tiles_dev, slots, tile_rows, _ = blocks.shape
    samples, node_rows, features = state.shape
    extent = tiles_dev + 2 * HALO
    rim_rows = HALO * tile_rows
    live_slots = (jnp.arange(slots, dtype=jnp.int32)[None, :] < count[:, None]).astype(jnp.bfloat16)
    weights_m = blocks * live_slots[:, :, None, None]
    chooser = (source[:, :, None] == jnp.arange(extent, dtype=jnp.int32)[None, None, :]).astype(
        jnp.float32
    )
    hidden = state
    inputs, aggregates, preacts = ([], [], [])
    for stratum in range(LAYERS):
        extended = with_halo(hidden, (("dom", 1),), rim_rows)
        ext_tiles = extended.reshape(samples, extent, tile_rows, features)
        gathered = jnp.take(ext_tiles, source, axis=1)
        aggregate = jnp.einsum(
            "tsab,ctsbf->ctaf", weights_m, gathered, preferred_element_type=jnp.float32
        )
        aggregate = aggregate.reshape(samples, node_rows, features).astype(jnp.bfloat16)
        preact = jnp.einsum(
            "crf,fg->crg", hidden, w_self[stratum], preferred_element_type=jnp.float32
        ) + jnp.einsum("crf,fg->crg", aggregate, w_nbr[stratum], preferred_element_type=jnp.float32)
        inputs.append(hidden)
        aggregates.append(aggregate)
        preacts.append(preact)
        hidden = (hidden.astype(jnp.float32) + jax.nn.silu(preact)).astype(jnp.bfloat16)
    grad_now = cotangent.astype(jnp.float32)
    self_parts, nbr_parts = ([], [])
    for stratum in reversed(range(LAYERS)):
        preact = preacts[stratum]
        sigmoid_pre = jax.nn.sigmoid(preact)
        grad_pre = (grad_now * sigmoid_pre * (1.0 + preact * (1.0 - sigmoid_pre))).astype(
            jnp.bfloat16
        )
        self_part = jnp.einsum(
            "crf,crg->fg", inputs[stratum], grad_pre, preferred_element_type=jnp.float32
        )
        nbr_part = jnp.einsum(
            "crf,crg->fg", aggregates[stratum], grad_pre, preferred_element_type=jnp.float32
        )
        self_parts.append(self_part)
        nbr_parts.append(nbr_part)
        grad_agg = jnp.einsum(
            "crg,fg->crf", grad_pre, w_nbr[stratum], preferred_element_type=jnp.float32
        ).astype(jnp.bfloat16)
        contrib = jnp.einsum(
            "tsba,ctaf->ctsbf",
            weights_m,
            grad_agg.reshape(samples, tiles_dev, tile_rows, features),
            preferred_element_type=jnp.float32,
        )
        ext_grad = jnp.einsum("tse,ctsbf->cebf", chooser, contrib, precision=lax.Precision.HIGHEST)
        ext_grad = ext_grad.reshape(samples, extent * tile_rows, features)
        left_rim = ext_grad[:, :rim_rows]
        right_rim = ext_grad[:, rim_rows + node_rows :]
        own_grad = ext_grad[:, rim_rows : rim_rows + node_rows]
        from_next = from_behind(left_rim.astype(jnp.bfloat16), "dom", -1).astype(left_rim.dtype)
        from_prev = from_behind(right_rim.astype(jnp.bfloat16), "dom", 1).astype(right_rim.dtype)
        own_grad = (
            own_grad
            + jnp.pad(from_prev, ((0, 0), (0, node_rows - rim_rows), (0, 0)))
            + jnp.pad(from_next, ((0, 0), (node_rows - rim_rows, 0), (0, 0)))
        )
        grad_now = (
            grad_now
            + jnp.einsum(
                "crg,fg->crf", grad_pre, w_self[stratum], preferred_element_type=jnp.float32
            )
            + own_grad
        )
    self_stack = jnp.stack(self_parts[::-1])
    nbr_stack = jnp.stack(nbr_parts[::-1])
    self_stack, nbr_stack = lax.psum((self_stack, nbr_stack), ("dom", "dp"))
    total_rows = samples * lax.axis_size("dp") * node_rows * lax.axis_size("dom")
    factor = 1.0 / math.sqrt(total_rows)
    return (hidden, grad_now.astype(jnp.bfloat16), self_stack * factor, nbr_stack * factor)


def solution(mesh):
    in_specs = (
        P("dp", "dom", None),
        P("dom", None, None, None),
        P("dom", None),
        P("dom"),
        P("dp", "dom", None),
        P(),
        P(),
    )
    out_specs = (P("dp", "dom", None), P("dp", "dom", None), P(), P())
    return jax.shard_map(
        per_device, mesh=mesh, in_specs=in_specs, out_specs=out_specs, check_vma=False
    )
```

profile of v0, /device:TPU:1, one launch (start us, length us, event | category | flops | bytes accessed | tf_op | source)
XLA Modules:
  0.0 345.9 jit_solution(836602939632191957)
XLA Ops:
  10.4 3.6 %collective-permute-start.1 = (bf16[1,256,512]{2,1,0:T(8,128)(2,1)S(1)}, bf16[1,256,512]{2,1,0:T(8,128)(2,1)S(1)}, u32[]{:S(2)}, u32[]{:S(2)}) collective-permute-start(bf16[1,256,512]{2,1,0:T(8,128)(2,1)S(1)} %get-tuple-element.28), channel_id=1, source_target_pairs={{16,0},{32,16},{48,32},{64,48},{80,64},{96,80},{112,96},{0,112},{1... | collective-permute-start | bytes 786440 | tf_op jit(solution)/shard_map/ppermute | solution.py:21
  15.5 3.4 fusion.55
  19.9 3.4 collective-permute-done.1
  23.5 2.8 gather_fusion
  26.3 3.5 bitcast_convert_fusion.2
  29.8 3.8 %fusion.25 = (bf16[1,1024,512]{2,1,0:T(8,128)(2,1)S(1)}, f32[1024,512]{1,0:T(8,128)}) fusion(bf16[1,1024,512]{2,1,0:T(8,128)(2,1)S(1)} %copy-done.2, f32[1024,512]{1,0:T(8,128)S(1)} %copy-done.11, bf16[1024,512]{1,0:T(8,128)(2,1)S(1)} %bitcast.283, bf16[3,512,512]{2,1,0:T(8,128)(2,1)} %param.15), kind=kOutput, calls=%fused_computation.52 | convolution fusion | flops 541065216 | bytes 7864320 | tf_op jit(solution)/shard_map/crf,fg->crg/dot_general | solution.py:54
  37.3 3.1 fusion.52
  42.1 4.9 %collective-permute-done.3 = bf16[1,256,512]{2,1,0:T(8,128)(2,1)S(1)} collective-permute-done((bf16[1,256,512]{2,1,0:T(8,128)(2,1)S(1)}, bf16[1,256,512]{2,1,0:T(8,128)(2,1)S(1)}, u32[]{:S(2)}, u32[]{:S(2)}) %collective-permute-start.3) | collective-permute-done | bytes 262176 | tf_op jit(solution)/shard_map/ppermute | solution.py:21
  47.0 2.8 gather_fusion.1
  49.9 3.5 bitcast_convert_fusion.1
  53.4 3.8 %fusion.24 = (bf16[1,1024,512]{2,1,0:T(8,128)(2,1)S(1)}, f32[1024,512]{1,0:T(8,128)}) fusion(bf16[1,1024,512]{2,1,0:T(8,128)(2,1)S(1)} %copy-done.5, f32[1024,512]{1,0:T(8,128)S(1)} %copy-done.13, bf16[1024,512]{1,0:T(8,128)(2,1)S(1)} %bitcast.285, bf16[3,512,512]{2,1,0:T(8,128)(2,1)} %param.15), kind=kOutput, calls=%fused_computation.49 | convolution fusion | flops 541065216 | bytes 7864320 | tf_op jit(solution)/shard_map/crf,fg->crg/dot_general | solution.py:54
  61.0 3.1 fusion.49
  64.6 4.7 %collective-permute-done.5 = bf16[1,256,512]{2,1,0:T(8,128)(2,1)S(1)} collective-permute-done((bf16[1,256,512]{2,1,0:T(8,128)(2,1)S(1)}, bf16[1,256,512]{2,1,0:T(8,128)(2,1)S(1)}, u32[]{:S(2)}, u32[]{:S(2)}) %collective-permute-start.5) | collective-permute-done | bytes 262176 | tf_op jit(solution)/shard_map/ppermute | solution.py:21
  69.4 2.8 gather_fusion.2
  72.2 3.5 bitcast_convert_fusion
  79.7 4.7 %convolution_bitcast_fusion.2 = f32[8,4,128,512]{2,3,1,0:T(8,128)} fusion(bf16[8,128,512,1]{2,1,3,0:T(8,128)(2,1)S(1)} %bitcast.281, bf16[8,4,128,128]{3,2,1,0:T(8,128)(2,1)S(1)} %copy-done, bf16[8,4]{1,0:T(8,128)(2,1)S(1)} %fusion.92), kind=kOutput, calls=%fused_computation.17 | convolution fusion | flops 538968064 | bytes 10485824 | tf_op jit(solution)/shard_map/tsba,ctaf->ctsbf/dot_general | solution.py:78
  84.4 10.3 %copy.40 = f32[8,4,128,512]{3,0,1,2:T(8,128)} copy(f32[8,4,128,512]{2,3,1,0:T(8,128)} %convolution_bitcast_fusion.2) | data formatting | bytes 16777216 | tf_op jit(solution)/shard_map/reshape.41
  94.7 5.9 %convolution_bitcast_fusion.5 = f32[1,12,128,512]{3,1,2,0:T(8,128)S(1)} fusion(f32[8,4,128,512]{3,0,1,2:T(8,128)} %copy.40, s32[8,4]{0,1:T(4,128)S(1)} %copy-done.18), kind=kOutput, calls=%fused_computation.24 | convolution fusion | flops 301990272 | bytes 11534464 | tf_op jit(solution)/shard_map/tse,ctsbf->cebf/dot_general | solution.py:84
  103.6 2.8 collective-permute-start.7
  110.0 3.7 %collective-permute-done.7 = bf16[1,256,512]{2,1,0:T(8,128)(2,1)S(1)} collective-permute-done((bf16[1,256,512]{2,1,0:T(8,128)(2,1)S(1)}, bf16[1,256,512]{2,1,0:T(8,128)(2,1)S(1)}, u32[]{:S(2)}, u32[]{:S(2)}) %collective-permute-start.7) | collective-permute-done | bytes 262176 | tf_op jit(solution)/shard_map/ppermute | solution.py:29
  119.3 4.7 %convolution_bitcast_fusion.1 = f32[8,4,128,512]{2,3,1,0:T(8,128)} fusion(bf16[8,128,512,1]{2,1,3,0:T(8,128)(2,1)S(1)} %bitcast.282, bf16[8,4,128,128]{3,2,1,0:T(8,128)(2,1)S(1)} %copy-done, bf16[8,4]{1,0:T(8,128)(2,1)S(1)} %fusion.92), kind=kOutput, calls=%fused_computation.16 | convolution fusion | flops 538968064 | bytes 10485824 | tf_op jit(solution)/shard_map/tsba,ctaf->ctsbf/dot_general | solution.py:78
  124.0 10.3 %copy.43 = f32[8,4,128,512]{3,0,1,2:T(8,128)} copy(f32[8,4,128,512]{2,3,1,0:T(8,128)} %convolution_bitcast_fusion.1) | data formatting | bytes 16777216 | tf_op jit(solution)/shard_map/reshape.49
  134.3 5.9 %convolution_bitcast_fusion.4 = f32[1,12,128,512]{3,1,2,0:T(8,128)S(1)} fusion(f32[8,4,128,512]{3,0,1,2:T(8,128)} %copy.43, s32[8,4]{0,1:T(4,128)S(1)} %copy-done.18), kind=kOutput, calls=%fused_computation.23 | convolution fusion | flops 301990272 | bytes 11534464 | tf_op jit(solution)/shard_map/tse,ctsbf->cebf/dot_general | solution.py:84
  142.3 3.8 %collective-permute-start.9 = (bf16[1,256,512]{2,1,0:T(8,128)(2,1)S(1)}, bf16[1,256,512]{2,1,0:T(8,128)(2,1)S(1)}, u32[]{:S(2)}, u32[]{:S(2)}) collective-permute-start(bf16[1,256,512]{2,1,0:T(8,128)(2,1)S(1)} %get-tuple-element.20), channel_id=1, source_target_pairs={{16,0},{32,16},{48,32},{64,48},{80,64},{96,80},{112,96},{0,112},{1... | collective-permute-start | bytes 786440 | tf_op jit(solution)/shard_map/ppermute | solution.py:29
  163.3 4.7 %convolution_bitcast_fusion = f32[8,4,128,512]{2,3,1,0:T(8,128)} fusion(bf16[8,128,512,1]{2,1,3,0:T(8,128)(2,1)S(1)} %bitcast.280, bf16[8,4,128,128]{3,2,1,0:T(8,128)(2,1)S(1)} %copy-done, bf16[8,4]{1,0:T(8,128)(2,1)S(1)} %fusion.92), kind=kOutput, calls=%fused_computation.15 | convolution fusion | flops 538968064 | bytes 10485824 | tf_op jit(solution)/shard_map/tsba,ctaf->ctsbf/dot_general | solution.py:78
  168.0 10.4 %copy.46 = f32[8,4,128,512]{3,0,1,2:T(8,128)} copy(f32[8,4,128,512]{2,3,1,0:T(8,128)} %convolution_bitcast_fusion) | data formatting | bytes 16777216 | tf_op jit(solution)/shard_map/reshape.57
  178.4 6.0 %convolution_bitcast_fusion.3 = f32[1,12,128,512]{3,1,2,0:T(8,128)S(1)} fusion(f32[8,4,128,512]{3,0,1,2:T(8,128)} %copy.46, s32[8,4]{0,1:T(4,128)S(1)} %copy-done.18), kind=kOutput, calls=%fused_computation.22 | convolution fusion | flops 301990272 | bytes 11534464 | tf_op jit(solution)/shard_map/tse,ctsbf->cebf/dot_general | solution.py:84
  186.6 4.1 %collective-permute-start.11 = (bf16[1,256,512]{2,1,0:T(8,128)(2,1)S(1)}, bf16[1,256,512]{2,1,0:T(8,128)(2,1)S(1)}, u32[]{:S(2)}, u32[]{:S(2)}) collective-permute-start(bf16[1,256,512]{2,1,0:T(8,128)(2,1)S(1)} %get-tuple-element.18), channel_id=1, source_target_pairs={{16,0},{32,16},{48,32},{64,48},{80,64},{96,80},{112,96},{0,112},{1... | collective-permute-start | bytes 786440 | tf_op jit(solution)/shard_map/ppermute | solution.py:29
  190.7 5.9 %collective-permute-done.10 = bf16[1,256,512]{2,1,0:T(8,128)(2,1)S(1)} collective-permute-done((bf16[1,256,512]{2,1,0:T(8,128)(2,1)S(1)}, bf16[1,256,512]{2,1,0:T(8,128)(2,1)S(1)}, u32[]{:S(2)}, u32[]{:S(2)}) %collective-permute-start.10) | collective-permute-done | bytes 262176 | tf_op jit(solution)/shard_map/ppermute | solution.py:29
  200.4 126.6 %all-reduce.9.cloned.1.call-done = (f32[3,512,512]{1,2,0:T(8,128)}, f32[3,512,512]{1,2,0:T(8,128)}) async-done(((f32[3,512,512]{1,2,0:T(8,128)}, f32[3,512,512]{1,2,0:T(8,128)}), (f32[3,512,512]{1,2,0:T(8,128)}, f32[3,512,512]{1,2,0:T(8,128)})) %all-reduce.9.cloned.1.call-update) | async-done | bytes 6291472 | tf_op jit(solution)/shard_map/psum | solution.py:105
  327.0 5.7 %broadcast_multiply_fusion = (f32[3,512,512]{1,2,0:T(8,128)}, f32[3,512,512]{1,2,0:T(8,128)S(1)}) fusion(f32[3,512,512]{1,2,0:T(8,128)} %get-tuple-element.14, f32[3,512,512]{1,2,0:T(8,128)} %get-tuple-element.13), kind=kLoop, calls=%fused_computation.66 | loop fusion | flops 1572864 | bytes 12582912 | tf_op jit(solution)/shard_map/mul | solution.py:108
  332.7 3.5 %copy.54 = f32[3,512,512]{2,1,0:T(8,128)} copy(f32[3,512,512]{1,2,0:T(8,128)} %get-tuple-element.37) | data formatting | bytes 6291456
  (127 shorter events, 59.5 us)
Async XLA Ops:
  7.2 319.8 %all-reduce.9.cloned.1.call-start = ((), (), s32[]{:S(2)}) async-start(), calls=%async_computation | async-start | bytes 12582912 | tf_op jit(solution)/shard_map/psum | solution.py:105
  8.3 10.7 %copy-start.19 = (s32[8]{0:T(128)S(1)}, s32[8]{0:T(128)}, u32[]{:S(2)}) copy-start(s32[8]{0:T(128)} %param.12) | copy-start | bytes 100
  8.3 15.1 %copy-start.1 = (bf16[1,1024,512]{2,1,0:T(8,128)(2,1)S(1)}, bf16[1,1024,512]{2,1,0:T(8,128)(2,1)}, u32[]{:S(2)}) copy-start(bf16[1,1024,512]{2,1,0:T(8,128)(2,1)} %param.9) | copy-start | bytes 3145732
  8.3 11.6 %collective-permute-start = (bf16[1,256,512]{2,1,0:T(8,128)(2,1)S(1)}, bf16[1,256,512]{2,1,0:T(8,128)(2,1)S(1)}, u32[]{:S(2)}, u32[]{:S(2)}) collective-permute-start(bf16[1,256,512]{2,1,0:T(8,128)(2,1)S(1)} %get-tuple-element.27), channel_id=1, source_target_pairs={{0,16},{16,32},{32,48},{48,64},{64,80},{80,96},{96,112},{112,0},{1... | collective-permute-start | bytes 786440 | tf_op jit(solution)/shard_map/ppermute | solution.py:18
  10.4 12.9 %collective-permute-start.1 = (bf16[1,256,512]{2,1,0:T(8,128)(2,1)S(1)}, bf16[1,256,512]{2,1,0:T(8,128)(2,1)S(1)}, u32[]{:S(2)}, u32[]{:S(2)}) collective-permute-start(bf16[1,256,512]{2,1,0:T(8,128)(2,1)S(1)} %get-tuple-element.28), channel_id=1, source_target_pairs={{16,0},{32,16},{48,32},{64,48},{80,64},{96,80},{112,96},{0,112},{1... | collective-permute-start | bytes 786440 | tf_op jit(solution)/shard_map/ppermute | solution.py:21
  29.8 3.8 %copy-start.23 = (bf16[8,512,128]{1,2,0:T(8,128)(2,1)}, bf16[8,512,128]{1,2,0:T(8,128)(2,1)S(1)}, u32[]{:S(2)}) copy-start(bf16[8,512,128]{1,2,0:T(8,128)(2,1)S(1)} %bitcast_convert_fusion.2) | copy-start | bytes 3145732
  33.6 13.3 %copy-start.4 = (bf16[1,1024,512]{2,1,0:T(8,128)(2,1)}, bf16[1,1024,512]{2,1,0:T(8,128)(2,1)S(1)}, u32[]{:S(2)}) copy-start(bf16[1,1024,512]{2,1,0:T(8,128)(2,1)S(1)} %get-tuple-element.29) | copy-start | bytes 3145732
  33.6 8.4 %collective-permute-start.2 = (bf16[1,256,512]{2,1,0:T(8,128)(2,1)S(1)}, bf16[1,256,512]{2,1,0:T(8,128)(2,1)S(1)}, u32[]{:S(2)}, u32[]{:S(2)}) collective-permute-start(bf16[1,256,512]{2,1,0:T(8,128)(2,1)S(1)} %get-tuple-element.25), channel_id=1, source_target_pairs={{0,16},{16,32},{32,48},{48,64},{64,80},{80,96},{96,112},{112,0},{1... | collective-permute-start | bytes 786440 | tf_op jit(solution)/shard_map/ppermute | solution.py:18
  34.9 12.0 %collective-permute-start.3 = (bf16[1,256,512]{2,1,0:T(8,128)(2,1)S(1)}, bf16[1,256,512]{2,1,0:T(8,128)(2,1)S(1)}, u32[]{:S(2)}, u32[]{:S(2)}) collective-permute-start(bf16[1,256,512]{2,1,0:T(8,128)(2,1)S(1)} %get-tuple-element.26), channel_id=1, source_target_pairs={{16,0},{32,16},{48,32},{64,48},{80,64},{96,80},{112,96},{0,112},{1... | collective-permute-start | bytes 786440 | tf_op jit(solution)/shard_map/ppermute | solution.py:21
  57.1 12.1 %copy-start.7 = (bf16[1,1024,512]{2,1,0:T(8,128)(2,1)}, bf16[1,1024,512]{2,1,0:T(8,128)(2,1)S(1)}, u32[]{:S(2)}) copy-start(bf16[1,1024,512]{2,1,0:T(8,128)(2,1)S(1)} %get-tuple-element.31) | copy-start | bytes 3145732
  57.2 7.4 %collective-permute-start.4 = (bf16[1,256,512]{2,1,0:T(8,128)(2,1)S(1)}, bf16[1,256,512]{2,1,0:T(8,128)(2,1)S(1)}, u32[]{:S(2)}, u32[]{:S(2)}) collective-permute-start(bf16[1,256,512]{2,1,0:T(8,128)(2,1)S(1)} %get-tuple-element.23), channel_id=1, source_target_pairs={{0,16},{16,32},{32,48},{48,64},{64,80},{80,96},{96,112},{112,0},{1... | collective-permute-start | bytes 786440 | tf_op jit(solution)/shard_map/ppermute | solution.py:18
  58.5 10.8 %collective-permute-start.5 = (bf16[1,256,512]{2,1,0:T(8,128)(2,1)S(1)}, bf16[1,256,512]{2,1,0:T(8,128)(2,1)S(1)}, u32[]{:S(2)}, u32[]{:S(2)}) collective-permute-start(bf16[1,256,512]{2,1,0:T(8,128)(2,1)S(1)} %get-tuple-element.24), channel_id=1, source_target_pairs={{16,0},{32,16},{48,32},{64,48},{80,64},{96,80},{112,96},{0,112},{1... | collective-permute-start | bytes 786440 | tf_op jit(solution)/shard_map/ppermute | solution.py:21
  72.2 3.9 %copy-start.21 = (bf16[1,1024,512]{2,1,0:T(8,128)(2,1)S(1)}, bf16[1,1024,512]{2,1,0:T(8,128)(2,1)}, u32[]{:S(2)}) copy-start(bf16[1,1024,512]{2,1,0:T(8,128)(2,1)} %param.13) | copy-start | bytes 3145732
  84.4 10.3 %copy-start.18 = (s32[8,4]{0,1:T(4,128)S(1)}, s32[8,4]{0,1:T(4,128)}, u32[]{:S(2)}) copy-start(s32[8,4]{0,1:T(4,128)} %param.11) | copy-start | bytes 388
  102.4 4.1 %copy-start.32 = (bf16[1,1024,512]{2,1,0:T(8,128)(2,1)S(1)}, bf16[1,1024,512]{2,1,0:T(8,128)(2,1)}, u32[]{:S(2)}) copy-start(bf16[1,1024,512]{2,1,0:T(8,128)(2,1)} %copy-done.31) | copy-start | bytes 3145732
  102.6 7.4 %collective-permute-start.6 = (bf16[1,256,512]{2,1,0:T(8,128)(2,1)S(1)}, bf16[1,256,512]{2,1,0:T(8,128)(2,1)S(1)}, u32[]{:S(2)}, u32[]{:S(2)}) collective-permute-start(bf16[1,256,512]{2,1,0:T(8,128)(2,1)S(1)} %get-tuple-element.21), channel_id=1, source_target_pairs={{112,0},{0,16},{16,32},{32,48},{48,64},{64,80},{80,96},{96,112},{1... | collective-permute-start | bytes 786440 | tf_op jit(solution)/shard_map/ppermute | solution.py:29
  103.6 4.6 %copy-start.28 = (bf16[8,512,128]{1,2,0:T(8,128)(2,1)S(1)}, bf16[8,512,128]{1,2,0:T(8,128)(2,1)}, u32[]{:S(2)}) copy-start(bf16[8,512,128]{1,2,0:T(8,128)(2,1)} %copy-done.27) | copy-start | bytes 3145732
  103.6 10.1 %collective-permute-start.7 = (bf16[1,256,512]{2,1,0:T(8,128)(2,1)S(1)}, bf16[1,256,512]{2,1,0:T(8,128)(2,1)S(1)}, u32[]{:S(2)}, u32[]{:S(2)}) collective-permute-start(bf16[1,256,512]{2,1,0:T(8,128)(2,1)S(1)} %get-tuple-element.22), channel_id=1, source_target_pairs={{16,0},{32,16},{48,32},{64,48},{80,64},{96,80},{112,96},{0,112},{1... | collective-permute-start | bytes 786440 | tf_op jit(solution)/shard_map/ppermute | solution.py:29
  108.2 5.5 %copy-start.9 = (bf16[3,512,512]{2,1,0:T(8,128)(2,1)S(1)}, bf16[3,512,512]{2,1,0:T(8,128)(2,1)}, u32[]{:S(2)}) copy-start(bf16[3,512,512]{2,1,0:T(8,128)(2,1)} %param.14) | copy-start | bytes 4718596
  108.2 5.5 %copy-start.22 = (bf16[1,1024,512]{2,1,0:T(8,128)(2,1)S(1)}, bf16[1,1024,512]{2,1,0:T(8,128)(2,1)}, u32[]{:S(2)}) copy-start(bf16[1,1024,512]{2,1,0:T(8,128)(2,1)} %param.13) | copy-start | bytes 3145732
  108.2 5.6 %copy-start.34 = (f32[1024,512]{1,0:T(8,128)S(1)}, f32[1024,512]{1,0:T(8,128)}, u32[]{:S(2)}) copy-start(f32[1024,512]{1,0:T(8,128)} %get-tuple-element.32) | copy-start | bytes 6291460
  142.0 4.1 %copy-start.6 = (bf16[1,1024,512]{2,1,0:T(8,128)(2,1)S(1)}, bf16[1,1024,512]{2,1,0:T(8,128)(2,1)}, u32[]{:S(2)}) copy-start(bf16[1,1024,512]{2,1,0:T(8,128)(2,1)} %copy-done.4) | copy-start | bytes 3145732
  142.0 4.1 %copy-start.30 = (bf16[1,1024,512]{2,1,0:T(8,128)(2,1)S(1)}, bf16[1,1024,512]{2,1,0:T(8,128)(2,1)}, u32[]{:S(2)}) copy-start(bf16[1,1024,512]{2,1,0:T(8,128)(2,1)} %copy-done.29) | copy-start | bytes 3145732
  142.2 7.4 %collective-permute-start.8 = (bf16[1,256,512]{2,1,0:T(8,128)(2,1)S(1)}, bf16[1,256,512]{2,1,0:T(8,128)(2,1)S(1)}, u32[]{:S(2)}, u32[]{:S(2)}) collective-permute-start(bf16[1,256,512]{2,1,0:T(8,128)(2,1)S(1)} %get-tuple-element.19), channel_id=1, source_target_pairs={{112,0},{0,16},{16,32},{32,48},{48,64},{64,80},{80,96},{96,112},{1... | collective-permute-start | bytes 786440 | tf_op jit(solution)/shard_map/ppermute | solution.py:29
  142.3 4.6 %copy-start.26 = (bf16[8,512,128]{1,2,0:T(8,128)(2,1)S(1)}, bf16[8,512,128]{1,2,0:T(8,128)(2,1)}, u32[]{:S(2)}) copy-start(bf16[8,512,128]{1,2,0:T(8,128)(2,1)} %copy-done.25) | copy-start | bytes 3145732
  142.3 9.3 %collective-permute-start.9 = (bf16[1,256,512]{2,1,0:T(8,128)(2,1)S(1)}, bf16[1,256,512]{2,1,0:T(8,128)(2,1)S(1)}, u32[]{:S(2)}, u32[]{:S(2)}) collective-permute-start(bf16[1,256,512]{2,1,0:T(8,128)(2,1)S(1)} %get-tuple-element.20), channel_id=1, source_target_pairs={{16,0},{32,16},{48,32},{64,48},{80,64},{96,80},{112,96},{0,112},{1... | collective-permute-start | bytes 786440 | tf_op jit(solution)/shard_map/ppermute | solution.py:29
  146.9 4.7 %copy-start.33 = (f32[1024,512]{1,0:T(8,128)S(1)}, f32[1024,512]{1,0:T(8,128)}, u32[]{:S(2)}) copy-start(f32[1024,512]{1,0:T(8,128)} %get-tuple-element.30) | copy-start | bytes 6291460
  146.9 4.7 %copy-start.35 = (f32[1,1024,512]{2,1,0:T(8,128)S(1)}, f32[1,1024,512]{2,1,0:T(8,128)}, u32[]{:S(2)}) copy-start(f32[1,1024,512]{2,1,0:T(8,128)} %get-tuple-element.34) | copy-start | bytes 6291460
  186.3 12.4 %copy-start.10 = (f32[1,1024,512]{2,1,0:T(8,128)S(1)}, f32[1,1024,512]{2,1,0:T(8,128)}, u32[]{:S(2)}) copy-start(f32[1,1024,512]{2,1,0:T(8,128)} %get-tuple-element.36) | copy-start | bytes 6291460
  186.3 12.4 %copy-start.15 = (bf16[1,1024,512]{2,1,0:T(8,128)(2,1)S(1)}, bf16[1,1024,512]{2,1,0:T(8,128)(2,1)}, u32[]{:S(2)}) copy-start(bf16[1,1024,512]{2,1,0:T(8,128)(2,1)} %copy-done.14) | copy-start | bytes 3145732
  186.5 10.1 %collective-permute-start.10 = (bf16[1,256,512]{2,1,0:T(8,128)(2,1)S(1)}, bf16[1,256,512]{2,1,0:T(8,128)(2,1)S(1)}, u32[]{:S(2)}, u32[]{:S(2)}) collective-permute-start(bf16[1,256,512]{2,1,0:T(8,128)(2,1)S(1)} %get-tuple-element.17), channel_id=1, source_target_pairs={{112,0},{0,16},{16,32},{32,48},{48,64},{64,80},{80,96},{96,112},{1... | collective-permute-start | bytes 786440 | tf_op jit(solution)/shard_map/ppermute | solution.py:29
  186.6 12.1 %collective-permute-start.11 = (bf16[1,256,512]{2,1,0:T(8,128)(2,1)S(1)}, bf16[1,256,512]{2,1,0:T(8,128)(2,1)S(1)}, u32[]{:S(2)}, u32[]{:S(2)}) collective-permute-start(bf16[1,256,512]{2,1,0:T(8,128)(2,1)S(1)} %get-tuple-element.18), channel_id=1, source_target_pairs={{16,0},{32,16},{48,32},{64,48},{80,64},{96,80},{112,96},{0,112},{1... | collective-permute-start | bytes 786440 | tf_op jit(solution)/shard_map/ppermute | solution.py:29
  (17 other events, 44.7 us)
Sparse Core Ops, SparseCore 0:
  161.4 165.6 all-reduce.8
where the time goes:
time: 353 us; the launch traced here: 346 us
  waiting for transfers between devices  158 us (45%)
  matrix products  80.3 us (23%)
  local copies, waits for them, and re-layouts  55.4 us (16%)
  starting transfers between devices  25 us (7%)
  between operations  14.9 us (4%)
  other arithmetic  11.9 us (3%)
    psum x1, waiting for transfers between devices, per_device(): self_stack, nbr_stack = lax.psum((self_stack, nbr_stack), ('dom', 'dp'))  127 us
    another operation x3, local copies, waits for them, and re-layouts  31 us
    dot_general x3, matrix products, per_device(): jnp.einsum('tse,ctsbf->cebf', chooser, contrib, precision=lax.Precision.H...  17.8 us
    ppermute x6, waiting for transfers between devices, from_behind(): return lax.ppermute(block, axis, route)  15.7 us
    dot_general x3, matrix products, per_device(): jnp.einsum('tsba,ctaf->ctsbf', weights_m, grad_agg.reshape(samples, tiles...  14.1 us
    ppermute x3, waiting for transfers between devices, with_halo(): lax.ppermute(lax.slice_in_dim(block, 0, width, axis=dim), axis, backward)  13 us
    ppermute x6, starting transfers between devices, from_behind(): return lax.ppermute(block, axis, route)  11.9 us
    dot_general x3, matrix products, per_device(): jnp.einsum('tsab,ctsbf->ctaf', weights_m, gathered, preferred_element_typ...  10.4 us
  transfers between devices with their start and end apart: 13, of which 13 were waited for; matrix products, arithmetic and copies ran while one was open for 12% of the time, Pallas kernels for 0%

commit v1 on v0

v1 whole, which is shorter than its diff:
```python
import functools
import math

import jax
import jax.numpy as jnp
from jax import lax
from jax.experimental import pallas as pl
from jax.experimental.pallas import tpu as pltpu
from jax.sharding import Mesh
from jax.sharding import PartitionSpec as P

LAYERS = 3
TB = 128
TILES = 8
SLOTS = 4
HALO = 2
F = 512
ROWS = TILES * TB
RIM = HALO * TB
EXT = TILES + 2 * HALO
BF = jnp.bfloat16
F32 = jnp.float32
EDGE = (0, 1, 6, 7)
MID = (2, 3, 4, 5)
MB = 1 << 20

SM = pl.BlockSpec(memory_space=pltpu.SMEM)
VM = pl.BlockSpec(memory_space=pltpu.VMEM)


def pinned(shape, dtype):
    return pltpu.VMEM(shape, dtype)


def call(body, name, out_shape, in_specs, scratch=(), macs=0):
    return pl.pallas_call(
        body,
        name=name,
        out_shape=out_shape,
        in_specs=in_specs,
        out_specs=jax.tree.map(lambda _: VM, out_shape, is_leaf=lambda x: hasattr(x, "shape")),
        scratch_shapes=list(scratch),
        compiler_params=pltpu.CompilerParams(vmem_limit_bytes=12 * MB),
        cost_estimate=pl.CostEstimate(flops=2 * macs, bytes_accessed=4 * MB, transcendentals=0),
    )


def rows(tile):
    return slice(tile * TB, (tile + 1) * TB)


def dot(a, b):
    return jnp.dot(a, b, preferred_element_type=F32)


def dot_nt(a, b):
    return lax.dot_general(a, b, (((1,), (1,)), ((), ())), preferred_element_type=F32)


def dot_tn(a, b):
    return lax.dot_general(a, b, (((0,), (0,)), ((), ())), preferred_element_type=F32)


def fill_ext(ext, lo, hidden, hi):
    ext[0:RIM, :] = lo[...]
    ext[RIM : RIM + ROWS, :] = hidden[...]
    ext[RIM + ROWS :, :] = hi[...]


def gather(source, ext, tile):
    return jnp.concatenate(
        [ext[pl.ds(pl.multiple_of(source[tile, s] * TB, TB), TB), :] for s in range(SLOTS)], axis=0
    )


def act(pre):
    sig = 0.5 * jnp.tanh(0.5 * pre) + 0.5
    return pre * sig, sig * (1.0 + pre * (1.0 - sig))


def scatter(source, adj_v, grad_agg, back, tile):
    part = dot(adj_v[tile], grad_agg)
    for s in range(SLOTS):
        at = pl.ds(pl.multiple_of(source[tile, s] * TB, TB), TB)
        back[at, :] += part[s * TB : (s + 1) * TB, :]


def prepare(count, blocks, state, w_self, w_nbr, adj, adj_v, own, *kept):
    for layer in range(LAYERS):
        kept[layer][...] = w_self[layer]
        kept[LAYERS + layer][...] = w_nbr[layer]
    for t in range(TILES):
        for s in range(SLOTS):
            live = (s < count[t]).astype(F32)
            block = blocks[t, s].astype(F32) * live
            adj[t, :, s * TB : (s + 1) * TB] = block.astype(BF)
            adj_v[t, s * TB : (s + 1) * TB, :] = block.astype(BF)
    own[...] = dot(state[...], w_self[0])


def forward_pair(source, adj, ext, own, hidden, w_nbr, pair):
    agg = jnp.concatenate([dot(adj[t], gather(source, ext, t)) for t in pair], axis=0).astype(BF)
    at = slice(pair[0] * TB, (pair[-1] + 1) * TB)
    pre = own[at, :] + dot(agg, w_nbr[...])
    gain, slope = act(pre)
    new = (hidden[at, :].astype(F32) + gain).astype(BF)
    return agg, new, slope


def forward_edge(source, adj, lo, hi, hidden, own, w_nbr, new_lo, new_hi, agg_e, slope_e, ext):
    fill_ext(ext, lo, hidden, hi)
    for i, (pair, out) in enumerate((((0, 1), new_lo), ((6, 7), new_hi))):
        agg, new, slope = forward_pair(source, adj, ext, own, hidden, w_nbr, pair)
        out[...] = new
        agg_e[i * RIM : (i + 1) * RIM, :] = agg
        slope_e[i * RIM : (i + 1) * RIM, :] = slope


def forward_mid(
    source, adj, lo, hi, hidden, own, w_nbr, new_lo, new_hi, agg_e, slope_e, w_self,
    new, agg_o, slope_o, own_o, ext,
):
    fill_ext(ext, lo, hidden, hi)
    for pair in ((2, 3), (4, 5)):
        at = slice(pair[0] * TB, (pair[-1] + 1) * TB)
        agg_o[at, :], new[at, :], slope_o[at, :] = forward_pair(
            source, adj, ext, own, hidden, w_nbr, pair
        )
    for i, edge in enumerate((new_lo, new_hi)):
        at = slice(i * (ROWS - RIM), i * (ROWS - RIM) + RIM)
        new[at, :] = edge[...]
        agg_o[at, :] = agg_e[i * RIM : (i + 1) * RIM, :]
        slope_o[at, :] = slope_e[i * RIM : (i + 1) * RIM, :]
    own_o[...] = dot(new[...], w_self[...])


def turn(
    source, adj, adj_v, lo, hi, hidden, own, w_nbr, cot,
    final, agg_o, gp_o, back, rim_lo, rim_hi, ext,
):
    fill_ext(ext, lo, hidden, hi)
    back[...] = jnp.zeros_like(back)
    for first in range(0, TILES, 2):
        pair = (first, first + 1)
        at = slice(pair[0] * TB, (pair[-1] + 1) * TB)
        agg, new, slope = forward_pair(source, adj, ext, own, hidden, w_nbr, pair)
        agg_o[at, :] = agg
        final[at, :] = new
        gp = (cot[at, :].astype(F32) * slope).astype(BF)
        gp_o[at, :] = gp
        grad_agg = dot_nt(gp, w_nbr[...]).astype(BF)
        for i, t in enumerate(pair):
            scatter(source, adj_v, grad_agg[i * TB : (i + 1) * TB], back, t)
    rim_lo[...] = back[0:RIM, :].astype(BF)
    rim_hi[...] = back[RIM + ROWS :, :].astype(BF)


def backward_mid(source, adj_v, gp, grad, back, w_self, slope, w_nbr, grad_o, gp_m, part):
    grad_o[...] = (
        grad[...].astype(F32) + dot_nt(gp[...], w_self[...]) + back[RIM : RIM + ROWS, :]
    )
    part[...] = jnp.zeros_like(part)
    for pair in ((2, 3), (4, 5)):
        at = slice(pair[0] * TB, (pair[-1] + 1) * TB)
        new = (grad_o[at, :] * slope[at, :]).astype(BF)
        gp_m[at.start - RIM : at.stop - RIM, :] = new
        grad_agg = dot_nt(new, w_nbr[...]).astype(BF)
        for i, t in enumerate(pair):
            scatter(source, adj_v, grad_agg[i * TB : (i + 1) * TB], part, t)


def backward_edge(
    source, adj_v, from_prev, from_next, grad, slope, w_nbr, gp_m, part,
    grad_o, gp_o, back, rim_lo, rim_hi,
):
    back[...] = part[...]
    for pair, come in (((0, 1), from_prev), ((6, 7), from_next)):
        at = slice(pair[0] * TB, (pair[-1] + 1) * TB)
        total = grad[at, :] + come[...].astype(F32)
        grad_o[at, :] = total
        new = (total * slope[at, :]).astype(BF)
        gp_o[at, :] = new
        grad_agg = dot_nt(new, w_nbr[...]).astype(BF)
        for i, t in enumerate(pair):
            scatter(source, adj_v, grad_agg[i * TB : (i + 1) * TB], back, t)
    rim_lo[...] = back[0:RIM, :].astype(BF)
    rim_hi[...] = back[RIM + ROWS :, :].astype(BF)
    grad_o[RIM : ROWS - RIM, :] = grad[RIM : ROWS - RIM, :]
    gp_o[RIM : ROWS - RIM, :] = gp_m[...]


def backward_first(gp, grad, back, w_self, grad_o):
    grad_o[...] = grad[...] + dot_nt(gp[...], w_self[...]) + back[RIM : RIM + ROWS, :]


def backward_last(grad, from_prev, from_next, out):
    out[0:RIM, :] = (grad[0:RIM, :] + from_prev[...].astype(F32)).astype(BF)
    out[RIM : ROWS - RIM, :] = grad[RIM : ROWS - RIM, :].astype(BF)
    out[ROWS - RIM :, :] = (grad[ROWS - RIM :, :] + from_next[...].astype(F32)).astype(BF)


def weight_grad(core, hidden, agg, gp, keep, send):
    for i, left in enumerate((hidden, agg)):
        full = dot_tn(left[...], gp[...]).astype(BF)
        low, high = full[:, : F // 2], full[:, F // 2 :]
        first = jnp.broadcast_to(core[0] == 0, low.shape)
        keep[i * F : (i + 1) * F, :] = jnp.where(first, low, high)
        send[i * F : (i + 1) * F, :] = jnp.where(first, high, low)


def add_halves(mine, other, out):
    out[...] = (mine[...].astype(F32) + other[...].astype(F32)).astype(BF)


def sum_parts(parts, out):
    total = parts[0].astype(F32)
    for i in range(1, parts.shape[0]):
        total += parts[i].astype(F32)
    out[...] = total.astype(BF)


def unpack(factor, core, mine, other, self_o, nbr_o):
    for i, out in enumerate((self_o, nbr_o)):
        a = mine[i * F : (i + 1) * F, :].astype(F32) * factor
        b = other[i * F : (i + 1) * F, :].astype(F32) * factor
        first = jnp.broadcast_to(core[0] == 0, a.shape)
        out[:, : F // 2] = jnp.where(first, a, b)
        out[:, F // 2 :] = jnp.where(first, b, a)


def per_device(state, blocks, source, count, cotangent, w_self, w_nbr):
    state = state.reshape(ROWS, F)
    cotangent = cotangent.reshape(ROWS, F)
    n_dom = lax.axis_size("dom")
    up = [(i, (i + 1) % n_dom) for i in range(n_dom)]
    down = [(i, (i - 1) % n_dom) for i in range(n_dom)]
    core = lax.axis_index("core").astype(jnp.int32).reshape(1)
    peers = lax.axis_size("dom") * lax.axis_size("dq")

    def swap(to_prev, to_next):
        return lax.ppermute(to_next, "dom", up), lax.ppermute(to_prev, "dom", down)

    wide = jax.ShapeDtypeStruct((RIM, F), BF)
    ext_scratch = pltpu.VMEM((EXT * TB, F), BF)
    unit = ROWS * F * F

    lo, hi = swap(state[:RIM], state[ROWS - RIM :])
    adj, adj_v, own, *kept = call(
        prepare, "prepare",
        (
            pinned((TILES, TB, SLOTS * TB), BF), pinned((TILES, SLOTS * TB, TB), BF),
            pinned((ROWS, F), F32), *[pinned((F, F), BF)] * (2 * LAYERS),
        ),
        [SM] + [VM] * 4, macs=unit,
    )(count, blocks, state, w_self, w_nbr)
    w_self, w_nbr = kept[:LAYERS], kept[LAYERS:]

    hidden = state
    hiddens, aggs, slopes = [], [], []
    for layer in range(LAYERS - 1):
        new_lo, new_hi, agg_e, slope_e = call(
            forward_edge, f"forward_edge{layer}",
            (wide, wide, pinned((2 * RIM, F), BF), pinned((2 * RIM, F), F32)),
            [SM] + [VM] * 6, [ext_scratch], macs=unit,
        )(source, adj, lo, hi, hidden, own, w_nbr[layer])
        next_lo, next_hi = swap(new_lo, new_hi)
        new, agg, slope, own = call(
            forward_mid, f"forward_mid{layer}",
            (pinned((ROWS, F), BF), pinned((ROWS, F), BF), pinned((ROWS, F), F32), pinned((ROWS, F), F32)),
            [SM] + [VM] * 11, [ext_scratch], macs=2 * unit,
        )(
            source, adj, lo, hi, hidden, own, w_nbr[layer], new_lo, new_hi, agg_e, slope_e,
            w_self[layer + 1],
        )
        hiddens.append(hidden)
        aggs.append(agg)
        slopes.append(slope)
        hidden, lo, hi = new, next_lo, next_hi

    hiddens.append(hidden)
    top = LAYERS - 1
    final, agg, gp, back, rim_lo, rim_hi = call(
        turn, "turn",
        (
            jax.ShapeDtypeStruct((ROWS, F), BF), pinned((ROWS, F), BF), pinned((ROWS, F), BF),
            pinned((EXT * TB, F), F32), wide, wide,
        ),
        [SM] + [VM] * 8, [ext_scratch], macs=4 * unit,
    )(source, adj, adj_v, lo, hi, hidden, own, w_nbr[top], cotangent)
    aggs.append(agg)
    grad = cotangent

    def weights(layer, gp):
        half = (ROWS, F // 2)
        out = jax.ShapeDtypeStruct(half, BF)
        keep, send = call(
            weight_grad, f"weight_grad{layer}", (out, out), [SM, VM, VM, VM], macs=2 * unit
        )(core, hiddens[layer], aggs[layer], gp)
        got = lax.ppermute(send, "core", [(0, 1), (1, 0)])
        return call(add_halves, f"add_halves{layer}", out, [VM, VM])(keep, got)

    def reduce(layer, chip):
        half = (ROWS, F // 2)
        depth = ROWS // peers
        parts = lax.all_to_all(
            chip.reshape(peers, depth, F // 2), ("dom", "dq"), 0, 0, tiled=True
        )
        mine = call(
            sum_parts, f"sum_parts{layer}", jax.ShapeDtypeStruct((depth, F // 2), BF), [VM]
        )(parts)
        whole = lax.all_to_all(
            jnp.broadcast_to(mine[None], parts.shape), ("dom", "dq"), 0, 0, tiled=True
        ).reshape(half)
        other = lax.ppermute(whole, "core", [(0, 1), (1, 0)])
        total_rows = lax.axis_size("dq") * lax.axis_size("core") * n_dom * ROWS
        grads = jax.ShapeDtypeStruct((F, F), F32)
        return call(
            functools.partial(unpack, 1.0 / math.sqrt(total_rows)), f"unpack{layer}",
            (grads, grads), [SM, VM, VM],
        )(core, whole, other)

    results = []
    for layer in range(top, 0, -1):
        from_prev, from_next = swap(rim_lo, rim_hi)
        chip = weights(layer, gp)
        grad, gp_m, part = call(
            backward_mid, f"backward_mid{layer}",
            (pinned((ROWS, F), F32), pinned((ROWS - 2 * RIM, F), BF), pinned((EXT * TB, F), F32)),
            [SM] + [VM] * 7, macs=3 * unit,
        )(source, adj_v, gp, grad, back, w_self[layer], slopes[layer - 1], w_nbr[layer - 1])
        grad, gp, back, rim_lo, rim_hi = call(
            backward_edge, f"backward_edge{layer - 1}",
            (pinned((ROWS, F), F32), pinned((ROWS, F), BF), pinned((EXT * TB, F), F32), wide, wide),
            [SM] + [VM] * 8, macs=unit,
        )(source, adj_v, from_prev, from_next, grad, slopes[layer - 1], w_nbr[layer - 1], gp_m, part)
        results.append(reduce(layer, chip))

    from_prev, from_next = swap(rim_lo, rim_hi)
    chip = weights(0, gp)
    grad = call(
        backward_first, "backward_first", pinned((ROWS, F), F32), [VM] * 4, macs=unit
    )(gp, grad, back, w_self[0])
    results.append(reduce(0, chip))
    state_grad = call(
        backward_last, "backward_last", jax.ShapeDtypeStruct((ROWS, F), BF), [VM] * 3
    )(grad, from_prev, from_next)
    results = results[::-1]
    return (
        final[None],
        state_grad[None],
        jnp.stack([r[0] for r in results]),
        jnp.stack([r[1] for r in results]),
    )


def solution(mesh):
    dom, dp = mesh.devices.shape
    fine = Mesh(mesh.devices.reshape(dom, dp // 2, 2), ("dom", "dq", "core"))
    nodes = P(("dq", "core"), "dom", None)
    in_specs = (nodes, P("dom", None, None, None), P("dom", None), P("dom"), nodes, P(), P())
    out_specs = (nodes, nodes, P(), P())
    return jax.shard_map(
        per_device, mesh=fine, in_specs=in_specs, out_specs=out_specs, check_vma=False
    )
```

time: 353 us -> 244 us (0.69); the launches traced: 346 us -> 242 us
  waiting for transfers between devices: 158 us -> 63 us
  matrix products: 80.3 us -> 0 us
  starting transfers between devices: 25 us -> 84.5 us
  Pallas kernels: 0 us -> 43.9 us
  between operations: 14.9 us -> 1.11 us
  local copies, waits for them, and re-layouts: 55.4 us -> 46 us
  other arithmetic: 11.9 us -> 3.41 us
    psum x1 -> x0, waiting for transfers between devices: 127 us -> none  [per_device(): self_stack, nbr_stack = lax.psum((self_stack, nbr_stack), ('dom', 'dp'))]
    dot_general x27 -> x0, matrix products: 80.3 us -> none  [the longest x3 17.8 us: per_device(): jnp.einsum('tse,ctsbf->cebf', chooser, contrib, precision=lax.Precision.H...]
    all_to_all x0 -> x6, starting transfers between devices: none -> 45.2 us  [the longest x3 23.9 us: reduce(): lax.all_to_all(chip.reshape(peers, depth, F // 2), ('dom', 'dq'), 0, 0, t...]
    pallas_call x0 -> x24, Pallas kernels: none -> 43.9 us  [the longest x1 6.41 us: per_device(): call(turn, 'turn', (jax.ShapeDtypeStruct((ROWS, F), BF), pinned((ROWS, F)...]
    all_to_all x0 -> x6, waiting for transfers between devices: none -> 41.3 us  [the longest x3 23.6 us: reduce(): lax.all_to_all(jnp.broadcast_to(mine[None], parts.shape), ('dom', 'dq'),...]
    unnamed x74 -> x131, local copies, waits for them, and re-layouts: 8.99 us -> 41.5 us
    another operation x3 -> x0, local copies, waits for them, and re-layouts: 31 us -> none
    ppermute x12 -> x18, starting transfers between devices: 25 us -> 39.4 us  [the longest x6 21.2 us: swap(): lax.ppermute(to_prev, 'dom', down)]
  transfers between devices with their start and end apart: 13 -> 24, of which waited for: 13 -> 14; matrix products, arithmetic and copies ran while one was open for 12% -> 1% of each run, Pallas kernels for 0% -> 12%
where the time goes in v1:
time: 244 us; the launch traced here: 242 us
  starting transfers between devices  84.5 us (35%)
  waiting for transfers between devices  63 us (26%)
  local copies, waits for them, and re-layouts  46 us (19%)
  Pallas kernels  43.9 us (18%)
  other arithmetic  3.41 us (1%)
    unnamed x131, local copies, waits for them, and re-layouts  41.5 us
    all_to_all x3, starting transfers between devices, reduce(): lax.all_to_all(chip.reshape(peers, depth, F // 2), ('dom', 'dq'), 0, 0, t...  23.9 us
    all_to_all x3, waiting for transfers between devices, reduce(): lax.all_to_all(jnp.broadcast_to(mine[None], parts.shape), ('dom', 'dq'),...  23.6 us
    all_to_all x3, starting transfers between devices, reduce(): lax.all_to_all(jnp.broadcast_to(mine[None], parts.shape), ('dom', 'dq'),...  21.3 us
    ppermute x6, starting transfers between devices, swap(): lax.ppermute(to_prev, 'dom', down)  21.2 us
    all_to_all x3, waiting for transfers between devices, reduce(): lax.all_to_all(chip.reshape(peers, depth, F // 2), ('dom', 'dq'), 0, 0, t...  17.7 us
    ppermute x6, waiting for transfers between devices, swap(): lax.ppermute(to_prev, 'dom', down)  11.7 us
    ppermute x6, waiting for transfers between devices, swap(): lax.ppermute(to_next, 'dom', up)  9.92 us
  transfers between devices with their start and end apart: 24, of which 14 were waited for; matrix products, arithmetic and copies ran while one was open for 1% of the time, Pallas kernels for 12%

profile of v1, /device:TPU:1, one launch (start us, length us, event | category | flops | bytes accessed | tf_op | source)
XLA Modules:
  0.0 242.0 jit_solution(17564974894905274065)
XLA Ops:
  2.6 5.5 %collective-permute-start.1 = (bf16[256,512]{1,0:T(8,128)(2,1)}, bf16[256,512]{1,0:T(8,128)(2,1)S(1)}, u32[]{:S(2)}, u32[]{:S(2)}) collective-permute-start(bf16[256,512]{1,0:T(8,128)(2,1)} %get-tuple-element.122), channel_id=1, source_target_pairs={{0,112},{16,0},{32,16},{48,32},{64,48},{80,64},{96,80},{112,96},{1... | collective-permute-start | bytes 786440 | tf_op jit(solution)/shard_map/ppermute | solution.py:241
  16.4 3.6 %collective-permute-done.lo = bf16[256,512]{1,0:T(8,128)(2,1)} collective-permute-done((bf16[256,512]{1,0:T(8,128)(2,1)}, bf16[256,512]{1,0:T(8,128)(2,1)}, u32[]{:S(2)}, u32[]{:S(2)}) %collective-permute-start) | collective-permute-done | bytes 262176 | tf_op jit(solution)/shard_map/ppermute | solution.py:241
  26.8 2.8 %forward_mid0.1 = (bf16[1024,512]{1,0:T(8,128)(2,1)S(1)}, bf16[1024,512]{1,0:T(8,128)(2,1)S(1)}, f32[1024,512]{1,0:T(8,128)S(1)}, f32[1024,512]{1,0:T(8,128)S(1)}) custom-call(s32[8,4]{1,0:T(8,128)S(1)} %copy.15.source, bf16[8,128,512]{2,1,0:T(8,128)(2,1)S(1)} %get-tuple-element.63.adj, bf16[256,512]{1,0:T(8,128)(2,1)} %collective-permute-done.lo, ...), custom_call_target="tpu_custom_call" | custom-call | flops 1073741824 | bytes 4194304 | tf_op jit(solution)/shard_map/forward_mid0/pallas_call | solution.py:267
  30.7 3.5 %collective-permute-done.3.hi = bf16[256,512]{1,0:T(8,128)(2,1)S(1)} collective-permute-done((bf16[256,512]{1,0:T(8,128)(2,1)S(1)}, bf16[256,512]{1,0:T(8,128)(2,1)S(1)}, u32[]{:S(2)}, u32[]{:S(2)}) %collective-permute-start.3) | collective-permute-done | bytes 262176 | tf_op jit(solution)/shard_map/ppermute | solution.py:241
  34.2 2.6 %forward_edge1.1 = (bf16[256,512]{1,0:T(8,128)(2,1)}, bf16[256,512]{1,0:T(8,128)(2,1)}, bf16[512,512]{1,0:T(8,128)(2,1)S(1)}, f32[512,512]{1,0:T(8,128)S(1)}) custom-call(s32[8,4]{1,0:T(8,128)S(1)} %copy.15.source, bf16[8,128,512]{2,1,0:T(8,128)(2,1)S(1)} %get-tuple-element.63.adj, bf16[256,512]{1,0:T(8,128)(2,1)S(1)} %collective-permute-done.2.lo, ...), custom_call_target="tpu_custom_call" | custom-call | flops 536870912 | bytes 4194304 | tf_op jit(solution)/shard_map/forward_edge1/pallas_call | solution.py:261
  39.3 3.6 %collective-permute-start.5 = (bf16[256,512]{1,0:T(8,128)(2,1)}, bf16[256,512]{1,0:T(8,128)(2,1)}, u32[]{:S(2)}, u32[]{:S(2)}) collective-permute-start(bf16[256,512]{1,0:T(8,128)(2,1)} %get-tuple-element.76.new_lo), channel_id=1, source_target_pairs={{0,112},{16,0},{32,16},{48,32},{64,48},{80,64},{96,80},{112,96},{1... | collective-permute-start | bytes 786440 | tf_op jit(solution)/shard_map/ppermute | solution.py:241
  51.0 3.0 %forward_mid1.1 = (bf16[1024,512]{1,0:T(8,128)(2,1)S(1)}, bf16[1024,512]{1,0:T(8,128)(2,1)S(1)}, f32[1024,512]{1,0:T(8,128)S(1)}, f32[1024,512]{1,0:T(8,128)S(1)}) custom-call(s32[8,4]{1,0:T(8,128)S(1)} %copy.15.source, bf16[8,128,512]{2,1,0:T(8,128)(2,1)S(1)} %get-tuple-element.63.adj, bf16[256,512]{1,0:T(8,128)(2,1)S(1)} %collective-permute-done.2.lo, ...), custom_call_target="tpu_custom_call" | custom-call | flops 1073741824 | bytes 4194304 | tf_op jit(solution)/shard_map/forward_mid1/pallas_call | solution.py:267
  54.0 6.4 %turn.1 = (bf16[1024,512]{1,0:T(8,128)(2,1)}, bf16[1024,512]{1,0:T(8,128)(2,1)S(1)}, bf16[1024,512]{1,0:T(8,128)(2,1)S(1)}, f32[1536,512]{1,0:T(8,128)S(1)}, bf1...) custom-call(s32[8,4]{1,0:T(8,128)S(1)} %copy.15.source, bf16[8,128,512]{2,1,0:T(8,128)(2,1)S(1)} %get-tuple-element.63.adj, ...), custom_call_target="tpu_custom_call" | custom-call | flops 2147483648 | bytes 4194304 | tf_op jit(solution)/shard_map/turn/pallas_call | solution.py:282
  61.7 2.8 %collective-permute-start.16 = (bf16[1024,256]{1,0:T(8,128)(2,1)S(1)}, bf16[1024,256]{1,0:T(8,128)(2,1)S(1)}, u32[]{:S(2)}, u32[]{:S(2)}) collective-permute-start(bf16[1024,256]{1,0:T(8,128)(2,1)S(1)} %get-tuple-element.117), channel_id=1, source_target_pairs={{0,1},{1,0},{2,3},{3,2},{4,5},{5,4},{6,7},{7,6},{8,9},{9,8},{10,11... | collective-permute-start | bytes 1572872 | tf_op jit(solution)/shard_map/ppermute | solution.py:299
  64.6 3.6 %collective-permute-start.7 = (bf16[256,512]{1,0:T(8,128)(2,1)S(1)}, bf16[256,512]{1,0:T(8,128)(2,1)S(1)}, u32[]{:S(2)}, u32[]{:S(2)}) collective-permute-start(bf16[256,512]{1,0:T(8,128)(2,1)S(1)} %get-tuple-element.85), channel_id=1, source_target_pairs={{0,112},{16,0},{32,16},{48,32},{64,48},{80,64},{96,80},{112,96},{1... | collective-permute-start | bytes 786440 | tf_op jit(solution)/shard_map/ppermute | solution.py:241
  68.1 2.7 %backward_mid2.1 = (f32[1024,512]{1,0:T(8,128)S(1)}, bf16[512,512]{1,0:T(8,128)(2,1)S(1)}, f32[1536,512]{1,0:T(8,128)S(1)}) custom-call(s32[8,4]{1,0:T(8,128)S(1)} %copy.15.source, bf16[8,512,128]{2,1,0:T(8,128)(2,1)S(1)} %get-tuple-element.64.adj_v, bf16[1024,512]{1,0:T(8,128)(2,1)S(1)} %get-tuple-element.86.gp, bf16[1024,512]{1,0:T(8,128)(2,1)S(1)} %bitcast.29, ...), custom_call_target="tpu_custom_call" | custom-call | flops 1610612736 | bytes 4194304 | tf_op jit(solution)/shard_map/backward_mid2/pallas_call | solution.py:326
  70.8 3.7 %collective-permute-done.6.from_prev = bf16[256,512]{1,0:T(8,128)(2,1)S(1)} collective-permute-done((bf16[256,512]{1,0:T(8,128)(2,1)S(1)}, bf16[256,512]{1,0:T(8,128)(2,1)S(1)}, u32[]{:S(2)}, u32[]{:S(2)}) %collective-permute-start.6) | collective-permute-done | bytes 262176 | tf_op jit(solution)/shard_map/ppermute | solution.py:241
  84.4 12.1 %all-to-all-start.4 = ((bf16[64,16,256]{2,1,0:T(8,128)(2,1)}), bf16[64,16,256]{2,1,0:T(8,128)(2,1)}, u32[]{:S(2)}, u32[]{:S(2)}) async-start(bf16[64,16,256]{2,1,0:T(8,128)(2,1)} %bitcast.26), calls=%async_computation.4 | async-start | bytes 1048576 | tf_op jit(solution)/shard_map/all_to_all | solution.py:305
  99.6 8.2 %all-to-all-done.4.parts = bf16[64,16,256]{2,1,0:T(8,128)(2,1)} async-done(((bf16[64,16,256]{2,1,0:T(8,128)(2,1)}), bf16[64,16,256]{2,1,0:T(8,128)(2,1)}, u32[]{:S(2)}, u32[]{:S(2)}) %all-to-all-start.4) | async-done | bytes 524320 | tf_op jit(solution)/shard_map/all_to_all | solution.py:305
  107.8 5.9 %all-to-all-start.2 = ((bf16[64,16,256]{2,1,0:T(8,128)(2,1)}), bf16[64,16,256]{2,1,0:T(8,128)(2,1)}, u32[]{:S(2)}, u32[]{:S(2)}) async-start(bf16[64,16,256]{2,1,0:T(8,128)(2,1)} %bitcast.25), calls=%async_computation.2 | async-start | bytes 1048576 | tf_op jit(solution)/shard_map/all_to_all | solution.py:305
  114.7 2.6 %collective-permute-start.9 = (bf16[256,512]{1,0:T(8,128)(2,1)}, bf16[256,512]{1,0:T(8,128)(2,1)S(1)}, u32[]{:S(2)}, u32[]{:S(2)}) collective-permute-start(bf16[256,512]{1,0:T(8,128)(2,1)} %copy-done.63), channel_id=1, source_target_pairs={{0,112},{16,0},{32,16},{48,32},{64,48},{80,64},{96,80},{112,96},{1... | collective-permute-start | bytes 786440 | tf_op jit(solution)/shard_map/ppermute | solution.py:241
  123.6 2.6 %backward_mid1.1 = (f32[1024,512]{1,0:T(8,128)S(1)}, bf16[512,512]{1,0:T(8,128)(2,1)S(1)}, f32[1536,512]{1,0:T(8,128)S(1)}) custom-call(s32[8,4]{1,0:T(8,128)S(1)} %copy.15.source, bf16[8,512,128]{2,1,0:T(8,128)(2,1)S(1)} %get-tuple-element.64.adj_v, bf16[1024,512]{1,0:T(8,128)(2,1)S(1)} %copy-done.37, f32[1024,512]{1,0:T(8,128)S(1)} %copy-done.22, ...), custom_call_target="tpu_custom_call" | custom-call | flops 1610612736 | bytes 4194304 | tf_op jit(solution)/shard_map/backward_mid1/pallas_call | solution.py:326
  126.7 3.1 %collective-permute-done.9.from_next = bf16[256,512]{1,0:T(8,128)(2,1)S(1)} collective-permute-done((bf16[256,512]{1,0:T(8,128)(2,1)}, bf16[256,512]{1,0:T(8,128)(2,1)S(1)}, u32[]{:S(2)}, u32[]{:S(2)}) %collective-permute-start.9) | collective-permute-done | bytes 262176 | tf_op jit(solution)/shard_map/ppermute | solution.py:241
  136.9 3.2 %collective-permute-start.12 = (bf16[1024,256]{1,0:T(8,128)(2,1)S(1)}, bf16[1024,256]{1,0:T(8,128)(2,1)S(1)}, u32[]{:S(2)}, u32[]{:S(2)}) collective-permute-start(bf16[1024,256]{1,0:T(8,128)(2,1)S(1)} %get-tuple-element.109), channel_id=1, source_target_pairs={{0,1},{1,0},{2,3},{3,2},{4,5},{5,4},{6,7},{7,6},{8,9},{9,8},{10,11... | collective-permute-start | bytes 1572872 | tf_op jit(solution)/shard_map/ppermute | solution.py:299
  142.1 9.8 %all-to-all-start.5 = ((bf16[64,16,256]{2,1,0:T(8,128)(2,1)}), bf16[64,16,256]{2,1,0:T(8,128)(2,1)}, u32[]{:S(2)}, u32[]{:S(2)}) async-start(bf16[64,16,256]{2,1,0:T(8,128)(2,1)} %broadcast_in_dim.28), calls=%async_computation.5 | async-start | bytes 1048576 | tf_op jit(solution)/shard_map/all_to_all | solution.py:311
  155.7 8.1 %all-to-all-done.5 = bf16[64,16,256]{2,1,0:T(8,128)(2,1)} async-done(((bf16[64,16,256]{2,1,0:T(8,128)(2,1)}), bf16[64,16,256]{2,1,0:T(8,128)(2,1)}, u32[]{:S(2)}, u32[]{:S(2)}) %all-to-all-start.5) | async-done | bytes 524320 | tf_op jit(solution)/shard_map/all_to_all | solution.py:311
  163.8 5.9 %all-to-all-start = ((bf16[64,16,256]{2,1,0:T(8,128)(2,1)}), bf16[64,16,256]{2,1,0:T(8,128)(2,1)}, u32[]{:S(2)}, u32[]{:S(2)}) async-start(bf16[64,16,256]{2,1,0:T(8,128)(2,1)} %bitcast.27), calls=%async_computation | async-start | bytes 1048576 | tf_op jit(solution)/shard_map/all_to_all | solution.py:305
  170.8 9.5 %all-to-all-done.parts = bf16[64,16,256]{2,1,0:T(8,128)(2,1)} async-done(((bf16[64,16,256]{2,1,0:T(8,128)(2,1)}), bf16[64,16,256]{2,1,0:T(8,128)(2,1)}, u32[]{:S(2)}, u32[]{:S(2)}) %all-to-all-start) | async-done | bytes 524320 | tf_op jit(solution)/shard_map/all_to_all | solution.py:305
  181.1 5.9 %all-to-all-start.3 = ((bf16[64,16,256]{2,1,0:T(8,128)(2,1)}), bf16[64,16,256]{2,1,0:T(8,128)(2,1)}, u32[]{:S(2)}, u32[]{:S(2)}) async-start(bf16[64,16,256]{2,1,0:T(8,128)(2,1)} %broadcast_in_dim.13), calls=%async_computation.3 | async-start | bytes 1048576 | tf_op jit(solution)/shard_map/all_to_all | solution.py:311
  188.2 9.2 %all-to-all-done.3 = bf16[64,16,256]{2,1,0:T(8,128)(2,1)} async-done(((bf16[64,16,256]{2,1,0:T(8,128)(2,1)}), bf16[64,16,256]{2,1,0:T(8,128)(2,1)}, u32[]{:S(2)}, u32[]{:S(2)}) %all-to-all-start.3) | async-done | bytes 524320 | tf_op jit(solution)/shard_map/all_to_all | solution.py:311
  198.3 5.5 %all-to-all-start.1 = ((bf16[64,16,256]{2,1,0:T(8,128)(2,1)}), bf16[64,16,256]{2,1,0:T(8,128)(2,1)}, u32[]{:S(2)}, u32[]{:S(2)}) async-start(bf16[64,16,256]{2,1,0:T(8,128)(2,1)} %broadcast_in_dim.12), calls=%async_computation.1 | async-start | bytes 1048576 | tf_op jit(solution)/shard_map/all_to_all | solution.py:311
  203.8 4.0 %collective-permute-start.17 = (bf16[1024,256]{1,0:T(8,128)(2,1)}, bf16[1024,256]{1,0:T(8,128)(2,1)}, u32[]{:S(2)}, u32[]{:S(2)}) collective-permute-start(bf16[1024,256]{1,0:T(8,128)(2,1)} %bitcast.14.mine), channel_id=1, source_target_pairs={{0,1},{1,0},{2,3},{3,2},{4,5},{5,4},{6,7},{7,6},{8,9},{9,8},{10,11... | collective-permute-start | bytes 1572872 | tf_op jit(solution)/shard_map/ppermute | solution.py:314
  208.0 6.3 %all-to-all-done.1 = bf16[64,16,256]{2,1,0:T(8,128)(2,1)} async-done(((bf16[64,16,256]{2,1,0:T(8,128)(2,1)}), bf16[64,16,256]{2,1,0:T(8,128)(2,1)}, u32[]{:S(2)}, u32[]{:S(2)}) %all-to-all-start.1) | async-done | bytes 524320 | tf_op jit(solution)/shard_map/all_to_all | solution.py:311
  214.3 5.0 %collective-permute-start.13 = (bf16[1024,256]{1,0:T(8,128)(2,1)}, bf16[1024,256]{1,0:T(8,128)(2,1)S(1)}, u32[]{:S(2)}, u32[]{:S(2)}) collective-permute-start(bf16[1024,256]{1,0:T(8,128)(2,1)} %bitcast.8.mine), channel_id=1, source_target_pairs={{0,1},{1,0},{2,3},{3,2},{4,5},{5,4},{6,7},{7,6},{8,9},{9,8},{10,11... | collective-permute-start | bytes 1572872 | tf_op jit(solution)/shard_map/ppermute | solution.py:314
  219.3 3.6 %collective-permute-start.11 = (bf16[256,512]{1,0:T(8,128)(2,1)S(1)}, bf16[256,512]{1,0:T(8,128)(2,1)S(1)}, u32[]{:S(2)}, u32[]{:S(2)}) collective-permute-start(bf16[256,512]{1,0:T(8,128)(2,1)S(1)} %copy-done.61), channel_id=1, source_target_pairs={{0,112},{16,0},{32,16},{48,32},{64,48},{80,64},{96,80},{112,96},{1... | collective-permute-start | bytes 786440 | tf_op jit(solution)/shard_map/ppermute | solution.py:241
  229.5 3.6 %collective-permute-done.11.from_next = bf16[256,512]{1,0:T(8,128)(2,1)S(1)} collective-permute-done((bf16[256,512]{1,0:T(8,128)(2,1)S(1)}, bf16[256,512]{1,0:T(8,128)(2,1)S(1)}, u32[]{:S(2)}, u32[]{:S(2)}) %collective-permute-start.11) | collective-permute-done | bytes 262176 | tf_op jit(solution)/shard_map/ppermute | solution.py:241
  238.6 3.4 %pad_maximum_fusion = (f32[3,512,512]{2,1,0:T(8,128)}, f32[3,512,512]{2,1,0:T(8,128)}) fusion(f32[1,512,512]{2,1,0:T(8,128)S(1)} %bitcast.30, f32[1,512,512]{2,1,0:T(8,128)S(1)} %bitcast.32, f32[1,512,512]{2,1,0:T(8,128)S(1)} %bitcast.34, f32[1,512,512]{2,1,0:T(8,128)S(1)} %bitcast.31, f32[1,512,512]{2,1,0:T(8,128)S(1)} %bitcast.33, f32[1,512,512]{2,1,0:T(8,128)S(1)} %bitcast.35), kind=kLoop, calls=%fused_computation | loop fusion | flops 3145728 | bytes 12582912 | tf_op jit(solution)/shard_map/stack | solution.py:351
  (176 shorter events, 79.5 us)
Async XLA Ops:
  0.6 19.4 %copy-start.1 = (bf16[1,1024,512]{2,1,0:T(8,128)(2,1)S(1)}, bf16[1,1024,512]{2,1,0:T(8,128)(2,1)}, u32[]{:S(2)}) copy-start(bf16[1,1024,512]{2,1,0:T(8,128)(2,1)} %param.7) | copy-start | bytes 3145732
  2.6 13.8 %collective-permute-start.1 = (bf16[256,512]{1,0:T(8,128)(2,1)}, bf16[256,512]{1,0:T(8,128)(2,1)S(1)}, u32[]{:S(2)}, u32[]{:S(2)}) collective-permute-start(bf16[256,512]{1,0:T(8,128)(2,1)} %get-tuple-element.122), channel_id=1, source_target_pairs={{0,112},{16,0},{32,16},{48,32},{64,48},{80,64},{96,80},{112,96},{1... | collective-permute-start | bytes 786440 | tf_op jit(solution)/shard_map/ppermute | solution.py:241
  8.1 11.9 %collective-permute-start = (bf16[256,512]{1,0:T(8,128)(2,1)}, bf16[256,512]{1,0:T(8,128)(2,1)}, u32[]{:S(2)}, u32[]{:S(2)}) collective-permute-start(bf16[256,512]{1,0:T(8,128)(2,1)} %get-tuple-element.123), channel_id=1, source_target_pairs={{0,16},{16,32},{32,48},{48,64},{64,80},{80,96},{96,112},{112,0},{1... | collective-permute-start | bytes 786440 | tf_op jit(solution)/shard_map/ppermute | solution.py:241
  16.3 13.3 %copy-start.2 = (bf16[512,512]{1,0:T(8,128)(2,1)}, bf16[512,512]{1,0:T(8,128)(2,1)S(1)}, u32[]{:S(2)}) copy-start(bf16[512,512]{1,0:T(8,128)(2,1)S(1)} %get-tuple-element.66.w_nbr) | copy-start | bytes 1572868
  16.3 13.3 %copy-start.23 = (bf16[512,512]{1,0:T(8,128)(2,1)}, bf16[512,512]{1,0:T(8,128)(2,1)S(1)}, u32[]{:S(2)}) copy-start(bf16[512,512]{1,0:T(8,128)(2,1)S(1)} %get-tuple-element.71.w_self) | copy-start | bytes 1572868
  16.3 17.9 %copy-start.4 = (bf16[512,512]{1,0:T(8,128)(2,1)}, bf16[512,512]{1,0:T(8,128)(2,1)S(1)}, u32[]{:S(2)}) copy-start(bf16[512,512]{1,0:T(8,128)(2,1)S(1)} %get-tuple-element.74.w_nbr) | copy-start | bytes 1572868
  22.2 8.4 %collective-permute-start.2 = (bf16[256,512]{1,0:T(8,128)(2,1)S(1)}, bf16[256,512]{1,0:T(8,128)(2,1)S(1)}, u32[]{:S(2)}, u32[]{:S(2)}) collective-permute-start(bf16[256,512]{1,0:T(8,128)(2,1)S(1)} %get-tuple-element.67.new_hi), channel_id=1, source_target_pairs={{0,16},{16,32},{32,48},{48,64},{64,80},{80,96},{96,112},{112,0},{1... | collective-permute-start | bytes 786440 | tf_op jit(solution)/shard_map/ppermute | solution.py:241
  23.5 10.7 %collective-permute-start.3 = (bf16[256,512]{1,0:T(8,128)(2,1)S(1)}, bf16[256,512]{1,0:T(8,128)(2,1)S(1)}, u32[]{:S(2)}, u32[]{:S(2)}) collective-permute-start(bf16[256,512]{1,0:T(8,128)(2,1)S(1)} %get-tuple-element.68.new_lo), channel_id=1, source_target_pairs={{0,112},{16,0},{32,16},{48,32},{64,48},{80,64},{96,80},{112,96},{1... | collective-permute-start | bytes 786440 | tf_op jit(solution)/shard_map/ppermute | solution.py:241
  39.3 14.7 %collective-permute-start.4 = (bf16[256,512]{1,0:T(8,128)(2,1)}, bf16[256,512]{1,0:T(8,128)(2,1)}, u32[]{:S(2)}, u32[]{:S(2)}) collective-permute-start(bf16[256,512]{1,0:T(8,128)(2,1)} %get-tuple-element.75.new_hi), channel_id=1, source_target_pairs={{0,16},{16,32},{32,48},{48,64},{64,80},{80,96},{96,112},{112,0},{1... | collective-permute-start | bytes 786440 | tf_op jit(solution)/shard_map/ppermute | solution.py:241
  39.3 14.7 %collective-permute-start.5 = (bf16[256,512]{1,0:T(8,128)(2,1)}, bf16[256,512]{1,0:T(8,128)(2,1)}, u32[]{:S(2)}, u32[]{:S(2)}) collective-permute-start(bf16[256,512]{1,0:T(8,128)(2,1)} %get-tuple-element.76.new_lo), channel_id=1, source_target_pairs={{0,112},{16,0},{32,16},{48,32},{64,48},{80,64},{96,80},{112,96},{1... | collective-permute-start | bytes 786440 | tf_op jit(solution)/shard_map/ppermute | solution.py:241
  61.7 21.7 %collective-permute-start.16 = (bf16[1024,256]{1,0:T(8,128)(2,1)S(1)}, bf16[1024,256]{1,0:T(8,128)(2,1)S(1)}, u32[]{:S(2)}, u32[]{:S(2)}) collective-permute-start(bf16[1024,256]{1,0:T(8,128)(2,1)S(1)} %get-tuple-element.117), channel_id=1, source_target_pairs={{0,1},{1,0},{2,3},{3,2},{4,5},{5,4},{6,7},{7,6},{8,9},{9,8},{10,11... | collective-permute-start | bytes 1572872 | tf_op jit(solution)/shard_map/ppermute | solution.py:299
  64.5 10.0 %collective-permute-start.6 = (bf16[256,512]{1,0:T(8,128)(2,1)S(1)}, bf16[256,512]{1,0:T(8,128)(2,1)S(1)}, u32[]{:S(2)}, u32[]{:S(2)}) collective-permute-start(bf16[256,512]{1,0:T(8,128)(2,1)S(1)} %get-tuple-element.84), channel_id=1, source_target_pairs={{0,16},{16,32},{32,48},{48,64},{64,80},{80,96},{96,112},{112,0},{1... | collective-permute-start | bytes 786440 | tf_op jit(solution)/shard_map/ppermute | solution.py:241
  64.6 11.5 %collective-permute-start.7 = (bf16[256,512]{1,0:T(8,128)(2,1)S(1)}, bf16[256,512]{1,0:T(8,128)(2,1)S(1)}, u32[]{:S(2)}, u32[]{:S(2)}) collective-permute-start(bf16[256,512]{1,0:T(8,128)(2,1)S(1)} %get-tuple-element.85), channel_id=1, source_target_pairs={{0,112},{16,0},{32,16},{48,32},{64,48},{80,64},{96,80},{112,96},{1... | collective-permute-start | bytes 786440 | tf_op jit(solution)/shard_map/ppermute | solution.py:241
  82.7 34.6 %copy-start.3 = (bf16[512,512]{1,0:T(8,128)(2,1)S(1)}, bf16[512,512]{1,0:T(8,128)(2,1)}, u32[]{:S(2)}) copy-start(bf16[512,512]{1,0:T(8,128)(2,1)} %copy-done.2) | copy-start | bytes 1572868
  82.7 34.6 %copy-start.24 = (bf16[512,512]{1,0:T(8,128)(2,1)S(1)}, bf16[512,512]{1,0:T(8,128)(2,1)}, u32[]{:S(2)}) copy-start(bf16[512,512]{1,0:T(8,128)(2,1)} %copy-done.23) | copy-start | bytes 1572868
  82.7 13.8 %collective-permute-start.14 = (bf16[1024,256]{1,0:T(8,128)(2,1)}, bf16[1024,256]{1,0:T(8,128)(2,1)}, u32[]{:S(2)}, u32[]{:S(2)}) collective-permute-start(bf16[1024,256]{1,0:T(8,128)(2,1)} %get-tuple-element.113), channel_id=1, source_target_pairs={{0,1},{1,0},{2,3},{3,2},{4,5},{5,4},{6,7},{7,6},{8,9},{9,8},{10,11... | collective-permute-start | bytes 1572872 | tf_op jit(solution)/shard_map/ppermute | solution.py:299
  84.4 23.4 %all-to-all-start.4 = ((bf16[64,16,256]{2,1,0:T(8,128)(2,1)}), bf16[64,16,256]{2,1,0:T(8,128)(2,1)}, u32[]{:S(2)}, u32[]{:S(2)}) async-start(bf16[64,16,256]{2,1,0:T(8,128)(2,1)} %bitcast.26), calls=%async_computation.4 | async-start | bytes 1048576 | tf_op jit(solution)/shard_map/all_to_all | solution.py:305
  107.8 33.4 %all-to-all-start.2 = ((bf16[64,16,256]{2,1,0:T(8,128)(2,1)}), bf16[64,16,256]{2,1,0:T(8,128)(2,1)}, u32[]{:S(2)}, u32[]{:S(2)}) async-start(bf16[64,16,256]{2,1,0:T(8,128)(2,1)} %bitcast.25), calls=%async_computation.2 | async-start | bytes 1048576 | tf_op jit(solution)/shard_map/all_to_all | solution.py:305
  113.7 13.1 %collective-permute-start.8 = (bf16[256,512]{1,0:T(8,128)(2,1)}, bf16[256,512]{1,0:T(8,128)(2,1)S(1)}, u32[]{:S(2)}, u32[]{:S(2)}) collective-permute-start(bf16[256,512]{1,0:T(8,128)(2,1)} %copy-done.64), channel_id=1, source_target_pairs={{0,16},{16,32},{32,48},{48,64},{64,80},{80,96},{96,112},{112,0},{1... | collective-permute-start | bytes 786440 | tf_op jit(solution)/shard_map/ppermute | solution.py:241
  114.7 15.1 %collective-permute-start.9 = (bf16[256,512]{1,0:T(8,128)(2,1)}, bf16[256,512]{1,0:T(8,128)(2,1)S(1)}, u32[]{:S(2)}, u32[]{:S(2)}) collective-permute-start(bf16[256,512]{1,0:T(8,128)(2,1)} %copy-done.63), channel_id=1, source_target_pairs={{0,112},{16,0},{32,16},{48,32},{64,48},{80,64},{96,80},{112,96},{1... | collective-permute-start | bytes 786440 | tf_op jit(solution)/shard_map/ppermute | solution.py:241
  136.9 15.0 %collective-permute-start.12 = (bf16[1024,256]{1,0:T(8,128)(2,1)S(1)}, bf16[1024,256]{1,0:T(8,128)(2,1)S(1)}, u32[]{:S(2)}, u32[]{:S(2)}) collective-permute-start(bf16[1024,256]{1,0:T(8,128)(2,1)S(1)} %get-tuple-element.109), channel_id=1, source_target_pairs={{0,1},{1,0},{2,3},{3,2},{4,5},{5,4},{6,7},{7,6},{8,9},{9,8},{10,11... | collective-permute-start | bytes 1572872 | tf_op jit(solution)/shard_map/ppermute | solution.py:299
  142.1 21.7 %all-to-all-start.5 = ((bf16[64,16,256]{2,1,0:T(8,128)(2,1)}), bf16[64,16,256]{2,1,0:T(8,128)(2,1)}, u32[]{:S(2)}, u32[]{:S(2)}) async-start(bf16[64,16,256]{2,1,0:T(8,128)(2,1)} %broadcast_in_dim.28), calls=%async_computation.5 | async-start | bytes 1048576 | tf_op jit(solution)/shard_map/all_to_all | solution.py:311
  154.7 64.5 %copy-start.61 = (bf16[256,512]{1,0:T(8,128)(2,1)S(1)}, bf16[256,512]{1,0:T(8,128)(2,1)}, u32[]{:S(2)}) copy-start(bf16[256,512]{1,0:T(8,128)(2,1)} %copy-done.60) | copy-start | bytes 786436
  154.7 68.1 %copy-start.16 = (f32[1536,512]{1,0:T(8,128)S(1)}, f32[1536,512]{1,0:T(8,128)}, u32[]{:S(2)}) copy-start(f32[1536,512]{1,0:T(8,128)} %copy-done.15) | copy-start | bytes 9437188
  163.8 16.5 %all-to-all-start = ((bf16[64,16,256]{2,1,0:T(8,128)(2,1)}), bf16[64,16,256]{2,1,0:T(8,128)(2,1)}, u32[]{:S(2)}, u32[]{:S(2)}) async-start(bf16[64,16,256]{2,1,0:T(8,128)(2,1)} %bitcast.27), calls=%async_computation | async-start | bytes 1048576 | tf_op jit(solution)/shard_map/all_to_all | solution.py:305
  181.1 16.3 %all-to-all-start.3 = ((bf16[64,16,256]{2,1,0:T(8,128)(2,1)}), bf16[64,16,256]{2,1,0:T(8,128)(2,1)}, u32[]{:S(2)}, u32[]{:S(2)}) async-start(bf16[64,16,256]{2,1,0:T(8,128)(2,1)} %broadcast_in_dim.13), calls=%async_computation.3 | async-start | bytes 1048576 | tf_op jit(solution)/shard_map/all_to_all | solution.py:311
  198.3 16.0 %all-to-all-start.1 = ((bf16[64,16,256]{2,1,0:T(8,128)(2,1)}), bf16[64,16,256]{2,1,0:T(8,128)(2,1)}, u32[]{:S(2)}, u32[]{:S(2)}) async-start(bf16[64,16,256]{2,1,0:T(8,128)(2,1)} %broadcast_in_dim.12), calls=%async_computation.1 | async-start | bytes 1048576 | tf_op jit(solution)/shard_map/all_to_all | solution.py:311
  203.8 30.4 %collective-permute-start.17 = (bf16[1024,256]{1,0:T(8,128)(2,1)}, bf16[1024,256]{1,0:T(8,128)(2,1)}, u32[]{:S(2)}, u32[]{:S(2)}) collective-permute-start(bf16[1024,256]{1,0:T(8,128)(2,1)} %bitcast.14.mine), channel_id=1, source_target_pairs={{0,1},{1,0},{2,3},{3,2},{4,5},{5,4},{6,7},{7,6},{8,9},{9,8},{10,11... | collective-permute-start | bytes 1572872 | tf_op jit(solution)/shard_map/ppermute | solution.py:314
  207.9 27.9 %collective-permute-start.15 = (bf16[1024,256]{1,0:T(8,128)(2,1)}, bf16[1024,256]{1,0:T(8,128)(2,1)}, u32[]{:S(2)}, u32[]{:S(2)}) collective-permute-start(bf16[1024,256]{1,0:T(8,128)(2,1)} %bitcast.11.mine), channel_id=1, source_target_pairs={{0,1},{1,0},{2,3},{3,2},{4,5},{5,4},{6,7},{7,6},{8,9},{9,8},{10,11... | collective-permute-start | bytes 1572872 | tf_op jit(solution)/shard_map/ppermute | solution.py:314
  214.3 22.9 %collective-permute-start.13 = (bf16[1024,256]{1,0:T(8,128)(2,1)}, bf16[1024,256]{1,0:T(8,128)(2,1)S(1)}, u32[]{:S(2)}, u32[]{:S(2)}) collective-permute-start(bf16[1024,256]{1,0:T(8,128)(2,1)} %bitcast.8.mine), channel_id=1, source_target_pairs={{0,1},{1,0},{2,3},{3,2},{4,5},{5,4},{6,7},{7,6},{8,9},{9,8},{10,11... | collective-permute-start | bytes 1572872 | tf_op jit(solution)/shard_map/ppermute | solution.py:314
  219.3 10.3 %collective-permute-start.10 = (bf16[256,512]{1,0:T(8,128)(2,1)}, bf16[256,512]{1,0:T(8,128)(2,1)S(1)}, u32[]{:S(2)}, u32[]{:S(2)}) collective-permute-start(bf16[256,512]{1,0:T(8,128)(2,1)} %copy-done.62), channel_id=1, source_target_pairs={{0,16},{16,32},{32,48},{48,64},{64,80},{80,96},{96,112},{112,0},{1... | collective-permute-start | bytes 786440 | tf_op jit(solution)/shard_map/ppermute | solution.py:241
  219.3 13.9 %collective-permute-start.11 = (bf16[256,512]{1,0:T(8,128)(2,1)S(1)}, bf16[256,512]{1,0:T(8,128)(2,1)S(1)}, u32[]{:S(2)}, u32[]{:S(2)}) collective-permute-start(bf16[256,512]{1,0:T(8,128)(2,1)S(1)} %copy-done.61), channel_id=1, source_target_pairs={{0,112},{16,0},{32,16},{48,32},{64,48},{80,64},{96,80},{112,96},{1... | collective-permute-start | bytes 786440 | tf_op jit(solution)/shard_map/ppermute | solution.py:241
  (57 other events, 159.2 us)

commit v2 on v1

--- a/solution.py
+++ b/solution.py
@@ -26,13 +26,14 @@
 
 SM = pl.BlockSpec(memory_space=pltpu.SMEM)
 VM = pl.BlockSpec(memory_space=pltpu.VMEM)
+HB = pl.BlockSpec(memory_space=pltpu.HBM)
 
 
 def pinned(shape, dtype):
     return pltpu.VMEM(shape, dtype)
 
 
-def call(body, name, out_shape, in_specs, scratch=(), macs=0):
+def call(body, name, out_shape, in_specs, scratch=()):
     return pl.pallas_call(
         body,
         name=name,
@@ -41,7 +42,7 @@
         out_specs=jax.tree.map(lambda _: VM, out_shape, is_leaf=lambda x: hasattr(x, "shape")),
         scratch_shapes=list(scratch),
         compiler_params=pltpu.CompilerParams(vmem_limit_bytes=12 * MB),
-        cost_estimate=pl.CostEstimate(flops=2 * macs, bytes_accessed=4 * MB, transcendentals=0),
+        cost_estimate=pl.CostEstimate(flops=1, bytes_accessed=1, transcendentals=0),
     )
 
 
@@ -69,7 +70,7 @@
 
 def gather(source, ext, tile):
     return jnp.concatenate(
-        [ext[pl.ds(pl.multiple_of(source[tile, s] * TB, TB), TB), :] for s in range(SLOTS)], axis=0
+        [ext[pl.ds(pl.multiple_of(source[s, tile] * TB, TB), TB), :] for s in range(SLOTS)], axis=0
     )
 
 
@@ -81,21 +82,43 @@
 def scatter(source, adj_v, grad_agg, back, tile):
     part = dot(adj_v[tile], grad_agg)
     for s in range(SLOTS):
-        at = pl.ds(pl.multiple_of(source[tile, s] * TB, TB), TB)
+        at = pl.ds(pl.multiple_of(source[s, tile] * TB, TB), TB)
         back[at, :] += part[s * TB : (s + 1) * TB, :]
 
 
-def prepare(count, blocks, state, w_self, w_nbr, adj, adj_v, own, *kept):
+def edge_tiles(state, lo, hi, sems):
+    copies = [
+        pltpu.make_async_copy(state.at[pl.ds(0, RIM), :], lo, sems.at[0]),
+        pltpu.make_async_copy(state.at[pl.ds(ROWS - RIM, RIM), :], hi, sems.at[1]),
+    ]
+    for copy in copies:
+        copy.start()
+    for copy in copies:
+        copy.wait()
+
+
+def prepare(count, blocks, state, w_self, w_nbr, adj, adj_v, own, hidden, *rest):
+    kept, (raw, sems) = rest[: 2 * LAYERS], rest[2 * LAYERS :]
+    loads = [(state, hidden), (w_self.at[0], kept[0]), (blocks, raw)]
     for layer in range(LAYERS):
-        kept[layer][...] = w_self[layer]
-        kept[LAYERS + layer][...] = w_nbr[layer]
+        if layer:
+            loads.append((w_self.at[layer], kept[layer]))
+        loads.append((w_nbr.at[layer], kept[LAYERS + layer]))
+    copies = [pltpu.make_async_copy(a, b, sems.at[i]) for i, (a, b) in enumerate(loads)]
+    for copy in copies:
+        copy.start()
+    copies[0].wait()
+    copies[1].wait()
+    own[...] = dot(hidden[...], kept[0][...])
+    copies[2].wait()
     for t in range(TILES):
         for s in range(SLOTS):
             live = (s < count[t]).astype(F32)
-            block = blocks[t, s].astype(F32) * live
-            adj[t, :, s * TB : (s + 1) * TB] = block.astype(BF)
-            adj_v[t, s * TB : (s + 1) * TB, :] = block.astype(BF)
-    own[...] = dot(state[...], w_self[0])
+            block = (raw[t, s].astype(F32) * live).astype(BF)
+            adj[t, :, s * TB : (s + 1) * TB] = block
+            adj_v[t, s * TB : (s + 1) * TB, :] = block
+    for copy in copies[3:]:
+        copy.wait()
 
 
 def forward_pair(source, adj, ext, own, hidden, w_nbr, pair):
@@ -199,42 +222,62 @@
     out[ROWS - RIM :, :] = (grad[ROWS - RIM :, :] + from_next[...].astype(F32)).astype(BF)
 
 
-def weight_grad(core, hidden, agg, gp, keep, send):
+def weight_grad(hidden, agg, gp, keep, send):
+    core = lax.axis_index("core")
     for i, left in enumerate((hidden, agg)):
         full = dot_tn(left[...], gp[...]).astype(BF)
         low, high = full[:, : F // 2], full[:, F // 2 :]
-        first = jnp.broadcast_to(core[0] == 0, low.shape)
+        first = jnp.broadcast_to(core == 0, low.shape)
         keep[i * F : (i + 1) * F, :] = jnp.where(first, low, high)
         send[i * F : (i + 1) * F, :] = jnp.where(first, high, low)
 
 
 def add_halves(mine, other, out):
     out[...] = (mine[...].astype(F32) + other[...].astype(F32)).astype(BF)
+
+
+def all_parts(*refs):
+    out = refs[-1]
+    depth = out.shape[1] // LAYERS
+    for layer in range(LAYERS):
+        if layer:
+            chip = refs[layer + 1][...]
+        else:
+            chip = (refs[0][...].astype(F32) + refs[1][...].astype(F32)).astype(BF)
+        for i in range(out.shape[0]):
+            out[i, layer * depth : (layer + 1) * depth, :] = chip[i * depth : (i + 1) * depth, :]
 
 
 def sum_parts(parts, out):
     total = parts[0].astype(F32)
     for i in range(1, parts.shape[0]):
         total += parts[i].astype(F32)
-    out[...] = total.astype(BF)
-
-
-def unpack(factor, core, mine, other, self_o, nbr_o):
-    for i, out in enumerate((self_o, nbr_o)):
-        a = mine[i * F : (i + 1) * F, :].astype(F32) * factor
-        b = other[i * F : (i + 1) * F, :].astype(F32) * factor
-        first = jnp.broadcast_to(core[0] == 0, a.shape)
-        out[:, : F // 2] = jnp.where(first, a, b)
-        out[:, F // 2 :] = jnp.where(first, b, a)
+    total = total.astype(BF)
+    for i in range(out.shape[0]):
+        out[i] = total
+
+
+def unpack(factor, mine, other, *outs):
+    core = lax.axis_index("core")
+    depth = mine.shape[1] // LAYERS
+    for layer in range(LAYERS):
+        at = slice(layer * depth, (layer + 1) * depth)
+        for i, out in enumerate(outs):
+            group = slice(i * F // depth, (i + 1) * F // depth)
+            a = mine[group, at, :].reshape(F, F // 2).astype(F32) * factor
+            b = other[group, at, :].reshape(F, F // 2).astype(F32) * factor
+            first = jnp.broadcast_to(core == 0, a.shape)
+            out[layer, :, : F // 2] = jnp.where(first, a, b)
+            out[layer, :, F // 2 :] = jnp.where(first, b, a)
 
 
 def per_device(state, blocks, source, count, cotangent, w_self, w_nbr):
     state = state.reshape(ROWS, F)
+    source = source.T
     cotangent = cotangent.reshape(ROWS, F)
     n_dom = lax.axis_size("dom")
     up = [(i, (i + 1) % n_dom) for i in range(n_dom)]
     down = [(i, (i - 1) % n_dom) for i in range(n_dom)]
-    core = lax.axis_index("core").astype(jnp.int32).reshape(1)
     peers = lax.axis_size("dom") * lax.axis_size("dq")
 
     def swap(to_prev, to_next):
@@ -242,32 +285,33 @@
 
     wide = jax.ShapeDtypeStruct((RIM, F), BF)
     ext_scratch = pltpu.VMEM((EXT * TB, F), BF)
-    unit = ROWS * F * F
-
-    lo, hi = swap(state[:RIM], state[ROWS - RIM :])
-    adj, adj_v, own, *kept = call(
+
+    lo, hi = swap(
+        *call(edge_tiles, "edge_tiles", (wide, wide), [HB], [pltpu.SemaphoreType.DMA((2,))])(state)
+    )
+    adj, adj_v, own, hidden, *kept = call(
         prepare, "prepare",
         (
             pinned((TILES, TB, SLOTS * TB), BF), pinned((TILES, SLOTS * TB, TB), BF),
-            pinned((ROWS, F), F32), *[pinned((F, F), BF)] * (2 * LAYERS),
+            pinned((ROWS, F), F32), pinned((ROWS, F), BF), *[pinned((F, F), BF)] * (2 * LAYERS),
         ),
-        [SM] + [VM] * 4, macs=unit,
+        [SM] + [HB] * 4,
+        [pltpu.VMEM((TILES, SLOTS, TB, TB), BF), pltpu.SemaphoreType.DMA((2 * LAYERS + 2,))],
     )(count, blocks, state, w_self, w_nbr)
     w_self, w_nbr = kept[:LAYERS], kept[LAYERS:]
 
-    hidden = state
     hiddens, aggs, slopes = [], [], []
     for layer in range(LAYERS - 1):
         new_lo, new_hi, agg_e, slope_e = call(
             forward_edge, f"forward_edge{layer}",
             (wide, wide, pinned((2 * RIM, F), BF), pinned((2 * RIM, F), F32)),
-            [SM] + [VM] * 6, [ext_scratch], macs=unit,
+            [SM] + [VM] * 6, [ext_scratch],
         )(source, adj, lo, hi, hidden, own, w_nbr[layer])
         next_lo, next_hi = swap(new_lo, new_hi)
         new, agg, slope, own = call(
             forward_mid, f"forward_mid{layer}",
             (pinned((ROWS, F), BF), pinned((ROWS, F), BF), pinned((ROWS, F), F32), pinned((ROWS, F), F32)),
-            [SM] + [VM] * 11, [ext_scratch], macs=2 * unit,
+            [SM] + [VM] * 11, [ext_scratch],
         )(
             source, adj, lo, hi, hidden, own, w_nbr[layer], new_lo, new_hi, agg_e, slope_e,
             w_self[layer + 1],
@@ -285,72 +329,57 @@
             jax.ShapeDtypeStruct((ROWS, F), BF), pinned((ROWS, F), BF), pinned((ROWS, F), BF),
             pinned((EXT * TB, F), F32), wide, wide,
         ),
-        [SM] + [VM] * 8, [ext_scratch], macs=4 * unit,
+        [SM] + [VM] * 8, [ext_scratch],
     )(source, adj, adj_v, lo, hi, hidden, own, w_nbr[top], cotangent)
     aggs.append(agg)
     grad = cotangent
 
+    half = jax.ShapeDtypeStruct((ROWS, F // 2), BF)
+    pieces = jax.ShapeDtypeStruct((peers, LAYERS * ROWS // peers, F // 2), BF)
+    flip = [(0, 1), (1, 0)]
+
     def weights(layer, gp):
-        half = (ROWS, F // 2)
-        out = jax.ShapeDtypeStruct(half, BF)
-        keep, send = call(
-            weight_grad, f"weight_grad{layer}", (out, out), [SM, VM, VM, VM], macs=2 * unit
-        )(core, hiddens[layer], aggs[layer], gp)
-        got = lax.ppermute(send, "core", [(0, 1), (1, 0)])
-        return call(add_halves, f"add_halves{layer}", out, [VM, VM])(keep, got)
-
-    def reduce(layer, chip):
-        half = (ROWS, F // 2)
-        depth = ROWS // peers
-        parts = lax.all_to_all(
-            chip.reshape(peers, depth, F // 2), ("dom", "dq"), 0, 0, tiled=True
+        keep, send = call(weight_grad, f"weight_grad{layer}", (half, half), [VM] * 3)(
+            hiddens[layer], aggs[layer], gp
         )
-        mine = call(
-            sum_parts, f"sum_parts{layer}", jax.ShapeDtypeStruct((depth, F // 2), BF), [VM]
-        )(parts)
-        whole = lax.all_to_all(
-            jnp.broadcast_to(mine[None], parts.shape), ("dom", "dq"), 0, 0, tiled=True
-        ).reshape(half)
-        other = lax.ppermute(whole, "core", [(0, 1), (1, 0)])
-        total_rows = lax.axis_size("dq") * lax.axis_size("core") * n_dom * ROWS
-        grads = jax.ShapeDtypeStruct((F, F), F32)
-        return call(
-            functools.partial(unpack, 1.0 / math.sqrt(total_rows)), f"unpack{layer}",
-            (grads, grads), [SM, VM, VM],
-        )(core, whole, other)
-
-    results = []
-    for layer in range(top, 0, -1):
+        return keep, lax.ppermute(send, "core", flip)
+
+    def spread(array):
+        return lax.all_to_all(array, ("dom", "dq"), 0, 0, tiled=True)
+
+    chips = []
+    for layer in range(top, -1, -1):
         from_prev, from_next = swap(rim_lo, rim_hi)
-        chip = weights(layer, gp)
-        grad, gp_m, part = call(
-            backward_mid, f"backward_mid{layer}",
-            (pinned((ROWS, F), F32), pinned((ROWS - 2 * RIM, F), BF), pinned((EXT * TB, F), F32)),
-            [SM] + [VM] * 7, macs=3 * unit,
-        )(source, adj_v, gp, grad, back, w_self[layer], slopes[layer - 1], w_nbr[layer - 1])
-        grad, gp, back, rim_lo, rim_hi = call(
-            backward_edge, f"backward_edge{layer - 1}",
-            (pinned((ROWS, F), F32), pinned((ROWS, F), BF), pinned((EXT * TB, F), F32), wide, wide),
-            [SM] + [VM] * 8, macs=unit,
-        )(source, adj_v, from_prev, from_next, grad, slopes[layer - 1], w_nbr[layer - 1], gp_m, part)
-        results.append(reduce(layer, chip))
-
-    from_prev, from_next = swap(rim_lo, rim_hi)
-    chip = weights(0, gp)
+        keep, got = weights(layer, gp)
+        if layer:
+            chips.append(call(add_halves, f"add_halves{layer}", half, [VM] * 2)(keep, got))
+            grad, gp_m, part = call(
+                backward_mid, f"backward_mid{layer}",
+                (pinned((ROWS, F), F32), pinned((ROWS - 2 * RIM, F), BF), pinned((EXT * TB, F), F32)),
+                [SM] + [VM] * 7,
+            )(source, adj_v, gp, grad, back, w_self[layer], slopes[layer - 1], w_nbr[layer - 1])
+            grad, gp, back, rim_lo, rim_hi = call(
+                backward_edge, f"backward_edge{layer - 1}",
+                (pinned((ROWS, F), F32), pinned((ROWS, F), BF), pinned((EXT * TB, F), F32), wide, wide),
+                [SM] + [VM] * 8,
+            )(source, adj_v, from_prev, from_next, grad, slopes[layer - 1], w_nbr[layer - 1], gp_m, part)
     grad = call(
-        backward_first, "backward_first", pinned((ROWS, F), F32), [VM] * 4, macs=unit
+        backward_first, "backward_first", jax.ShapeDtypeStruct((ROWS, F), F32), [VM] * 4
     )(gp, grad, back, w_self[0])
-    results.append(reduce(0, chip))
+    parts = spread(call(all_parts, "all_parts", pieces, [VM] * 4)(keep, got, *chips[::-1]))
     state_grad = call(
         backward_last, "backward_last", jax.ShapeDtypeStruct((ROWS, F), BF), [VM] * 3
     )(grad, from_prev, from_next)
-    results = results[::-1]
-    return (
-        final[None],
-        state_grad[None],
-        jnp.stack([r[0] for r in results]),
-        jnp.stack([r[1] for r in results]),
-    )
+    out = call(sum_parts, "sum_parts", pieces, [VM])(parts)
+    out, state_grad = lax.optimization_barrier((out, state_grad))
+    whole = spread(out)
+    other = lax.ppermute(whole, "core", flip)
+    total_rows = lax.axis_size("dq") * lax.axis_size("core") * n_dom * ROWS
+    grads = jax.ShapeDtypeStruct((LAYERS, F, F), F32)
+    self_grad, nbr_grad = call(
+        functools.partial(unpack, 1.0 / math.sqrt(total_rows)), "unpack", (grads, grads), [VM] * 2
+    )(whole, other)
+    return final[None], state_grad[None], self_grad, nbr_grad
 
 
 def solution(mesh):

time: 244 us -> 170 us (0.70)
  starting transfers between devices: 84.5 us -> 42.5 us
  local copies, waits for them, and re-layouts: 46 us -> 12.6 us
  blocking collectives: 0 us -> 29 us
  waiting for transfers between devices: 63 us -> 47.4 us
  Pallas kernels: 43.9 us -> 37.3 us
  other arithmetic: 3.41 us -> 0 us
    all_to_all x6 -> x1, waiting for transfers between devices: 41.3 us -> 0.01 us  [spread(): return lax.all_to_all(array, ('dom', 'dq'), 0, 0, tiled=True)]
    all_to_all x6 -> x1, starting transfers between devices: 45.2 us -> 9.94 us  [spread(): return lax.all_to_all(array, ('dom', 'dq'), 0, 0, tiled=True)]
    all_to_all x0 -> x1, blocking collectives: none -> 29 us  [spread(): return lax.all_to_all(array, ('dom', 'dq'), 0, 0, tiled=True)]
    unnamed x131 -> x26, local copies, waits for them, and re-layouts: 41.5 us -> 12.6 us
    ppermute x6, waiting for transfers between devices: 9.92 us -> 25.2 us  [swap(): lax.ppermute(to_next, 'dom', up)]
    ppermute x6 -> x4, starting transfers between devices: 15.8 us -> 8.75 us  [the longest x3 5.33 us: weights(): return (keep, lax.ppermute(send, 'core', flip))]
    ppermute x6, waiting for transfers between devices: 11.7 us -> 17.9 us  [swap(): lax.ppermute(to_prev, 'dom', down)]
    pallas_call x13 -> x10, Pallas kernels: 14.5 us -> 9.94 us  [the longest x3 3.86 us: weights(): call(weight_grad, f'weight_grad{layer}', (half, half), [VM] * 3)]
  transfers between devices with their start and end apart: 24 -> 17, of which waited for: 14 -> 11; matrix products, arithmetic and copies ran while one was open for 1% -> 0% of each run, Pallas kernels for 12% -> 12%
where the time goes in v2:
time: 170 us
  waiting for transfers between devices  47.4 us (28%)
  starting transfers between devices  42.5 us (25%)
  Pallas kernels  37.3 us (22%)
  blocking collectives  29 us (17%)
  local copies, waits for them, and re-layouts  12.6 us (7%)
    all_to_all x1, blocking collectives, spread(): return lax.all_to_all(array, ('dom', 'dq'), 0, 0, tiled=True)  29 us
    ppermute x6, waiting for transfers between devices, swap(): lax.ppermute(to_next, 'dom', up)  25.2 us
    ppermute x6, waiting for transfers between devices, swap(): lax.ppermute(to_prev, 'dom', down)  17.9 us
    ppermute x6, starting transfers between devices, swap(): lax.ppermute(to_prev, 'dom', down)  17.1 us
    unnamed x26, local copies, waits for them, and re-layouts  12.6 us
    all_to_all x1, starting transfers between devices, spread(): return lax.all_to_all(array, ('dom', 'dq'), 0, 0, tiled=True)  9.94 us
    ppermute x6, starting transfers between devices, swap(): lax.ppermute(to_next, 'dom', up)  6.71 us
    pallas_call x1, Pallas kernels, per_device(): call(turn, 'turn', (jax.ShapeDtypeStruct((ROWS, F), BF), pinned((ROWS, F)...  6.35 us
  transfers between devices with their start and end apart: 17, of which 11 were waited for; matrix products, arithmetic and copies ran while one was open for 0% of the time, Pallas kernels for 12%

profile of v2, /device:TPU:1, one launch (start us, length us, event | category | flops | bytes accessed | tf_op | source)
XLA Modules:
  0.0 169.6 jit_solution(17494006739036893291)
XLA Ops:
  1.9 2.1 %collective-permute-start = (bf16[256,512]{1,0:T(8,128)(2,1)S(1)}, bf16[256,512]{1,0:T(8,128)(2,1)S(1)}, u32[]{:S(2)}, u32[]{:S(2)}) collective-permute-start(bf16[256,512]{1,0:T(8,128)(2,1)S(1)} %get-tuple-element.66), channel_id=1, source_target_pairs={{0,16},{16,32},{32,48},{48,64},{64,80},{80,96},{96,112},{112,0},{1... | collective-permute-start | bytes 786440 | tf_op jit(solution)/shard_map/ppermute | solution.py:284
  4.0 3.6 %collective-permute-start.1 = (bf16[256,512]{1,0:T(8,128)(2,1)S(1)}, bf16[256,512]{1,0:T(8,128)(2,1)S(1)}, u32[]{:S(2)}, u32[]{:S(2)}) collective-permute-start(bf16[256,512]{1,0:T(8,128)(2,1)S(1)} %get-tuple-element.67), channel_id=1, source_target_pairs={{0,112},{16,0},{32,16},{48,32},{64,48},{80,64},{96,80},{112,96},{1... | collective-permute-start | bytes 786440 | tf_op jit(solution)/shard_map/ppermute | solution.py:284
  13.5 1.9 %prepare.1 = (bf16[8,128,512]{2,1,0:T(8,128)(2,1)S(1)}, bf16[8,512,128]{2,1,0:T(8,128)(2,1)S(1)}, f32[1024,512]{1,0:T(8,128)S(1)}, bf16[1024,512]{1,0:T(8,128)(2...) custom-call(s32[8]{0:T(128)S(1)} %copy-done.11, ...), custom_call_target="tpu_custom_call" | custom-call | flops 1 | bytes 1 | tf_op jit(solution)/shard_map/prepare/pallas_call | solution.py:292
  15.5 1.5 collective-permute-done.1.hi
  17.0 1.8 %forward_edge0.1 = (bf16[256,512]{1,0:T(8,128)(2,1)S(1)}, bf16[256,512]{1,0:T(8,128)(2,1)S(1)}, bf16[512,512]{1,0:T(8,128)(2,1)S(1)}, f32[512,512]{1,0:T(8,128)S(1)}) custom-call(s32[4,8]{1,0:T(4,128)S(1)} %bitcast.9, bf16[8,128,512]{2,1,0:T(8,128)(2,1)S(1)} %get-tuple-element.64.adj, bf16[256,512]{1,0:T(8,128)(2,1)S(1)} %collective-permute-done.lo, ...), custom_call_target="tpu_custom_call" | custom-call | flops 1 | bytes 1 | tf_op jit(solution)/shard_map/forward_edge0/pallas_call | solution.py:305
  20.1 2.4 %collective-permute-start.3 = (bf16[256,512]{1,0:T(8,128)(2,1)S(1)}, bf16[256,512]{1,0:T(8,128)(2,1)S(1)}, u32[]{:S(2)}, u32[]{:S(2)}) collective-permute-start(bf16[256,512]{1,0:T(8,128)(2,1)S(1)} %get-tuple-element.72.new_lo), channel_id=1, source_target_pairs={{0,112},{16,0},{32,16},{48,32},{64,48},{80,64},{96,80},{112,96},{1... | collective-permute-start | bytes 786440 | tf_op jit(solution)/shard_map/ppermute | solution.py:284
  22.4 2.4 %forward_mid0.1 = (bf16[1024,512]{1,0:T(8,128)(2,1)S(1)}, bf16[1024,512]{1,0:T(8,128)(2,1)S(1)}, f32[1024,512]{1,0:T(8,128)S(1)}, f32[1024,512]{1,0:T(8,128)S(1)}) custom-call(s32[4,8]{1,0:T(4,128)S(1)} %bitcast.10, bf16[8,128,512]{2,1,0:T(8,128)(2,1)S(1)} %get-tuple-element.64.adj, bf16[256,512]{1,0:T(8,128)(2,1)S(1)} %collective-permute-done.lo, ...), custom_call_target="tpu_custom_call" | custom-call | flops 1 | bytes 1 | tf_op jit(solution)/shard_map/forward_mid0/pallas_call | solution.py:311
  24.8 2.4 %collective-permute-done.2.lo = bf16[256,512]{1,0:T(8,128)(2,1)S(1)} collective-permute-done((bf16[256,512]{1,0:T(8,128)(2,1)S(1)}, bf16[256,512]{1,0:T(8,128)(2,1)S(1)}, u32[]{:S(2)}, u32[]{:S(2)}) %collective-permute-start.2) | collective-permute-done | bytes 262176 | tf_op jit(solution)/shard_map/ppermute | solution.py:284
  27.2 4.9 %collective-permute-done.3.hi = bf16[256,512]{1,0:T(8,128)(2,1)S(1)} collective-permute-done((bf16[256,512]{1,0:T(8,128)(2,1)S(1)}, bf16[256,512]{1,0:T(8,128)(2,1)S(1)}, u32[]{:S(2)}, u32[]{:S(2)}) %collective-permute-start.3) | collective-permute-done | bytes 262176 | tf_op jit(solution)/shard_map/ppermute | solution.py:284
  32.1 1.8 %forward_edge1.1 = (bf16[256,512]{1,0:T(8,128)(2,1)S(1)}, bf16[256,512]{1,0:T(8,128)(2,1)S(1)}, bf16[512,512]{1,0:T(8,128)(2,1)S(1)}, f32[512,512]{1,0:T(8,128)S(1)}) custom-call(s32[4,8]{1,0:T(4,128)S(1)} %bitcast.11, bf16[8,128,512]{2,1,0:T(8,128)(2,1)S(1)} %get-tuple-element.64.adj, bf16[256,512]{1,0:T(8,128)(2,1)S(1)} %collective-permute-done.2.lo, ...), custom_call_target="tpu_custom_call" | custom-call | flops 1 | bytes 1 | tf_op jit(solution)/shard_map/forward_edge1/pallas_call | solution.py:305
  35.2 2.4 %collective-permute-start.5 = (bf16[256,512]{1,0:T(8,128)(2,1)S(1)}, bf16[256,512]{1,0:T(8,128)(2,1)S(1)}, u32[]{:S(2)}, u32[]{:S(2)}) collective-permute-start(bf16[256,512]{1,0:T(8,128)(2,1)S(1)} %get-tuple-element.80.new_lo), channel_id=1, source_target_pairs={{0,112},{16,0},{32,16},{48,32},{64,48},{80,64},{96,80},{112,96},{1... | collective-permute-start | bytes 786440 | tf_op jit(solution)/shard_map/ppermute | solution.py:284
  37.6 2.4 %forward_mid1.1 = (bf16[1024,512]{1,0:T(8,128)(2,1)S(1)}, bf16[1024,512]{1,0:T(8,128)(2,1)S(1)}, f32[1024,512]{1,0:T(8,128)S(1)}, f32[1024,512]{1,0:T(8,128)S(1)}) custom-call(s32[4,8]{1,0:T(4,128)S(1)} %bitcast.12, bf16[8,128,512]{2,1,0:T(8,128)(2,1)S(1)} %get-tuple-element.64.adj, bf16[256,512]{1,0:T(8,128)(2,1)S(1)} %collective-permute-done.2.lo, ...), custom_call_target="tpu_custom_call" | custom-call | flops 1 | bytes 1 | tf_op jit(solution)/shard_map/forward_mid1/pallas_call | solution.py:311
  41.3 4.7 %collective-permute-done.5.hi = bf16[256,512]{1,0:T(8,128)(2,1)S(1)} collective-permute-done((bf16[256,512]{1,0:T(8,128)(2,1)S(1)}, bf16[256,512]{1,0:T(8,128)(2,1)S(1)}, u32[]{:S(2)}, u32[]{:S(2)}) %collective-permute-start.5) | collective-permute-done | bytes 262176 | tf_op jit(solution)/shard_map/ppermute | solution.py:284
  46.0 6.4 %turn.1 = (bf16[1024,512]{1,0:T(8,128)(2,1)}, bf16[1024,512]{1,0:T(8,128)(2,1)S(1)}, bf16[1024,512]{1,0:T(8,128)(2,1)S(1)}, f32[1536,512]{1,0:T(8,128)S(1)}, bf1...) custom-call(s32[4,8]{1,0:T(4,128)S(1)} %bitcast.13, bf16[8,128,512]{2,1,0:T(8,128)(2,1)S(1)} %get-tuple-element.64.adj, ...), custom_call_target="tpu_custom_call" | custom-call | flops 1 | bytes 1 | tf_op jit(solution)/shard_map/turn/pallas_call | solution.py:326
  53.2 2.7 %collective-permute-start.7 = (bf16[256,512]{1,0:T(8,128)(2,1)S(1)}, bf16[256,512]{1,0:T(8,128)(2,1)S(1)}, u32[]{:S(2)}, u32[]{:S(2)}) collective-permute-start(bf16[256,512]{1,0:T(8,128)(2,1)S(1)} %get-tuple-element.90), channel_id=1, source_target_pairs={{0,112},{16,0},{32,16},{48,32},{64,48},{80,64},{96,80},{112,96},{1... | collective-permute-start | bytes 786440 | tf_op jit(solution)/shard_map/ppermute | solution.py:284
  55.9 2.6 %backward_mid2.1 = (f32[1024,512]{1,0:T(8,128)S(1)}, bf16[512,512]{1,0:T(8,128)(2,1)S(1)}, f32[1536,512]{1,0:T(8,128)S(1)}) custom-call(s32[4,8]{1,0:T(4,128)S(1)} %bitcast.14, bf16[8,512,128]{2,1,0:T(8,128)(2,1)S(1)} %get-tuple-element.65.adj_v, bf16[1024,512]{1,0:T(8,128)(2,1)S(1)} %get-tuple-element.91.gp, bf16[1024,512]{1,0:T(8,128)(2,1)S(1)} %bitcast.6, ...), custom_call_target="tpu_custom_call" | custom-call | flops 1 | bytes 1 | tf_op jit(solution)/shard_map/backward_mid2/pallas_call | solution.py:356
  59.7 3.7 %collective-permute-done.7.from_next = bf16[256,512]{1,0:T(8,128)(2,1)S(1)} collective-permute-done((bf16[256,512]{1,0:T(8,128)(2,1)S(1)}, bf16[256,512]{1,0:T(8,128)(2,1)S(1)}, u32[]{:S(2)}, u32[]{:S(2)}) %collective-permute-start.7) | collective-permute-done | bytes 262176 | tf_op jit(solution)/shard_map/ppermute | solution.py:284
  63.4 2.2 %backward_edge1.1 = (f32[1024,512]{1,0:T(8,128)S(1)}, bf16[1024,512]{1,0:T(8,128)(2,1)S(1)}, f32[1536,512]{1,0:T(8,128)S(1)}, bf16[256,512]{1,0:T(8,128)(2,1)S(1)}, bf16[256,512]{1,0:T(8,128)(2,1)S(1)}) custom-call(s32[4,8]{1,0:T(4,128)S(1)} %bitcast.15, bf16[8,512,128]{2,1,0:T(8,128)(2,1)S(1)} %get-tuple-element.65.adj_v, ...), custom_call_target="tpu_custom_call" | custom-call | flops 1 | bytes 1 | tf_op jit(solution)/shard_map/backward_edge1/pallas_call | solution.py:361
  65.7 3.6 %collective-permute-start.9 = (bf16[256,512]{1,0:T(8,128)(2,1)S(1)}, bf16[256,512]{1,0:T(8,128)(2,1)S(1)}, u32[]{:S(2)}, u32[]{:S(2)}) collective-permute-start(bf16[256,512]{1,0:T(8,128)(2,1)S(1)} %get-tuple-element.98), channel_id=1, source_target_pairs={{0,112},{16,0},{32,16},{48,32},{64,48},{80,64},{96,80},{112,96},{1... | collective-permute-start | bytes 786440 | tf_op jit(solution)/shard_map/ppermute | solution.py:284
  70.5 4.6 %collective-permute-start.12 = (bf16[1024,256]{1,0:T(8,128)(2,1)S(1)}, bf16[1024,256]{1,0:T(8,128)(2,1)S(1)}, u32[]{:S(2)}, u32[]{:S(2)}) collective-permute-start(bf16[1024,256]{1,0:T(8,128)(2,1)S(1)} %get-tuple-element.114), channel_id=1, source_target_pairs={{0,1},{1,0},{2,3},{3,2},{4,5},{5,4},{6,7},{7,6},{8,9},{9,8},{10,11... | collective-permute-start | bytes 1572872 | tf_op jit(solution)/shard_map/ppermute | solution.py:345
  76.6 2.6 %backward_mid1.1 = (f32[1024,512]{1,0:T(8,128)S(1)}, bf16[512,512]{1,0:T(8,128)(2,1)S(1)}, f32[1536,512]{1,0:T(8,128)S(1)}) custom-call(s32[4,8]{1,0:T(4,128)S(1)} %bitcast.16, bf16[8,512,128]{2,1,0:T(8,128)(2,1)S(1)} %get-tuple-element.65.adj_v, bf16[1024,512]{1,0:T(8,128)(2,1)S(1)} %get-tuple-element.99.gp, f32[1024,512]{1,0:T(8,128)S(1)} %get-tuple-element.100.grad, ...), custom_call_target="tpu_custom_call" | custom-call | flops 1 | bytes 1 | tf_op jit(solution)/shard_map/backward_mid1/pallas_call | solution.py:356
  79.2 2.2 %backward_edge0.1 = (f32[1024,512]{1,0:T(8,128)S(1)}, bf16[1024,512]{1,0:T(8,128)(2,1)S(1)}, f32[1536,512]{1,0:T(8,128)S(1)}, bf16[256,512]{1,0:T(8,128)(2,1)S(1)}, bf16[256,512]{1,0:T(8,128)(2,1)S(1)}) custom-call(s32[4,8]{1,0:T(4,128)S(1)} %bitcast.17, bf16[8,512,128]{2,1,0:T(8,128)(2,1)S(1)} %get-tuple-element.65.adj_v, ...), custom_call_target="tpu_custom_call" | custom-call | flops 1 | bytes 1 | tf_op jit(solution)/shard_map/backward_edge0/pallas_call | solution.py:361
  88.2 9.9 %all-to-all-start = ((bf16[64,48,256]{2,1,0:T(8,128)(2,1)}), bf16[64,48,256]{2,1,0:T(8,128)(2,1)S(1)}, u32[]{:S(2)}, u32[]{:S(2)}) async-start(bf16[64,48,256]{2,1,0:T(8,128)(2,1)} %all_parts.1), calls=%async_computation | async-start | bytes 3145728 | tf_op jit(solution)/shard_map/all_to_all | solution.py:348
  99.2 2.6 %collective-permute-start.14 = (bf16[256,512]{1,0:T(8,128)(2,1)S(1)}, bf16[256,512]{1,0:T(8,128)(2,1)S(1)}, u32[]{:S(2)}, u32[]{:S(2)}) collective-permute-start(bf16[256,512]{1,0:T(8,128)(2,1)S(1)} %get-tuple-element.119), channel_id=1, source_target_pairs={{0,112},{16,0},{32,16},{48,32},{64,48},{80,64},{96,80},{112,96},{1... | collective-permute-start | bytes 786440 | tf_op jit(solution)/shard_map/ppermute | solution.py:284
  101.8 1.9 %copy-done.4 = f32[1536,512]{1,0:T(8,128)S(1)} copy-done((f32[1536,512]{1,0:T(8,128)S(1)}, f32[1536,512]{1,0:T(8,128)}, u32[]{:S(2)}) %copy-start.4) | copy-done | bytes 3145752
  103.6 1.6 copy-done.6
  106.0 20.3 %collective-permute-done.13.from_prev = bf16[256,512]{1,0:T(8,128)(2,1)S(1)} collective-permute-done((bf16[256,512]{1,0:T(8,128)(2,1)}, bf16[256,512]{1,0:T(8,128)(2,1)S(1)}, u32[]{:S(2)}, u32[]{:S(2)}) %collective-permute-start.13) | collective-permute-done | bytes 262176 | tf_op jit(solution)/shard_map/ppermute | solution.py:284
  126.2 3.1 %collective-permute-done.14.from_next = bf16[256,512]{1,0:T(8,128)(2,1)S(1)} collective-permute-done((bf16[256,512]{1,0:T(8,128)(2,1)S(1)}, bf16[256,512]{1,0:T(8,128)(2,1)S(1)}, u32[]{:S(2)}, u32[]{:S(2)}) %collective-permute-start.14) | collective-permute-done | bytes 262176 | tf_op jit(solution)/shard_map/ppermute | solution.py:284
  130.8 29.0 %all_to_all.10.mine = bf16[64,48,256]{2,1,0:T(8,128)(2,1)S(1)} all-to-all(bf16[64,48,256]{2,1,0:T(8,128)(2,1)S(1)} %sum_parts.1), channel_id=1, replica_groups=mesh['dom'=8,'dq'=8,'core'=2] {'dom','dq'}, dimensions={0} | all-to-all | bytes 3145728 | tf_op jit(solution)/shard_map/all_to_all | solution.py:348
  159.8 3.4 %collective-permute-start.15 = (bf16[64,48,256]{2,1,0:T(8,128)(2,1)S(1)}, bf16[64,48,256]{2,1,0:T(8,128)(2,1)S(1)}, u32[]{:S(2)}, u32[]{:S(2)}) collective-permute-start(bf16[64,48,256]{2,1,0:T(8,128)(2,1)S(1)} %all_to_all.10.mine), channel_id=1, source_target_pairs={{0,1},{1,0},{2,3},{3,2},{4,5},{5,4},{6,7},{7,6},{8,9},{9,8},{10,11... | collective-permute-start | bytes 4718600 | tf_op jit(solution)/shard_map/ppermute | solution.py:376
  163.2 3.0 %collective-permute-done.15.other = bf16[64,48,256]{2,1,0:T(8,128)(2,1)S(1)} collective-permute-done((bf16[64,48,256]{2,1,0:T(8,128)(2,1)S(1)}, bf16[64,48,256]{2,1,0:T(8,128)(2,1)S(1)}, u32[]{:S(2)}, u32[]{:S(2)}) %collective-permute-start.15) | collective-permute-done | bytes 1572896 | tf_op jit(solution)/shard_map/ppermute | solution.py:376
  166.2 3.4 %unpack.1 = (f32[3,512,512]{2,1,0:T(8,128)}, f32[3,512,512]{2,1,0:T(8,128)}) custom-call(bf16[64,48,256]{2,1,0:T(8,128)(2,1)S(1)} %all_to_all.10.mine, bf16[64,48,256]{2,1,0:T(8,128)(2,1)S(1)} %collective-permute-done.15.other), custom_call_target="tpu_custom_call" | custom-call | flops 1 | bytes 1 | tf_op jit(solution)/shard_map/unpack/pallas_call | solution.py:379
  (50 shorter events, 25.8 us)
Async XLA Ops:
  0.6 1.2 copy-start.1
  1.9 13.5 %collective-permute-start = (bf16[256,512]{1,0:T(8,128)(2,1)S(1)}, bf16[256,512]{1,0:T(8,128)(2,1)S(1)}, u32[]{:S(2)}, u32[]{:S(2)}) collective-permute-start(bf16[256,512]{1,0:T(8,128)(2,1)S(1)} %get-tuple-element.66), channel_id=1, source_target_pairs={{0,16},{16,32},{32,48},{48,64},{64,80},{80,96},{96,112},{112,0},{1... | collective-permute-start | bytes 786440 | tf_op jit(solution)/shard_map/ppermute | solution.py:284
  4.0 12.9 %collective-permute-start.1 = (bf16[256,512]{1,0:T(8,128)(2,1)S(1)}, bf16[256,512]{1,0:T(8,128)(2,1)S(1)}, u32[]{:S(2)}, u32[]{:S(2)}) collective-permute-start(bf16[256,512]{1,0:T(8,128)(2,1)S(1)} %get-tuple-element.67), channel_id=1, source_target_pairs={{0,112},{16,0},{32,16},{48,32},{64,48},{80,64},{96,80},{112,96},{1... | collective-permute-start | bytes 786440 | tf_op jit(solution)/shard_map/ppermute | solution.py:284
  7.6 1.2 copy-start.2
  8.8 1.4 copy-start.7
  10.2 1.4 copy-start.8
  11.6 1.2 copy-start.9
  12.9 0.7 copy-start.11
  13.5 3.5 %copy-start.10 = (s32[8,4]{0,1:T(4,128)S(1)}, s32[8,4]{0,1:T(4,128)}, u32[]{:S(2)}) copy-start(s32[8,4]{0,1:T(4,128)} %param.9) | copy-start | bytes 388
  18.8 8.4 %collective-permute-start.2 = (bf16[256,512]{1,0:T(8,128)(2,1)S(1)}, bf16[256,512]{1,0:T(8,128)(2,1)S(1)}, u32[]{:S(2)}, u32[]{:S(2)}) collective-permute-start(bf16[256,512]{1,0:T(8,128)(2,1)S(1)} %get-tuple-element.71.new_hi), channel_id=1, source_target_pairs={{0,16},{16,32},{32,48},{48,64},{64,80},{80,96},{96,112},{112,0},{1... | collective-permute-start | bytes 786440 | tf_op jit(solution)/shard_map/ppermute | solution.py:284
  20.1 12.0 %collective-permute-start.3 = (bf16[256,512]{1,0:T(8,128)(2,1)S(1)}, bf16[256,512]{1,0:T(8,128)(2,1)S(1)}, u32[]{:S(2)}, u32[]{:S(2)}) collective-permute-start(bf16[256,512]{1,0:T(8,128)(2,1)S(1)} %get-tuple-element.72.new_lo), channel_id=1, source_target_pairs={{0,112},{16,0},{32,16},{48,32},{64,48},{80,64},{96,80},{112,96},{1... | collective-permute-start | bytes 786440 | tf_op jit(solution)/shard_map/ppermute | solution.py:284
  33.9 7.4 %collective-permute-start.4 = (bf16[256,512]{1,0:T(8,128)(2,1)S(1)}, bf16[256,512]{1,0:T(8,128)(2,1)S(1)}, u32[]{:S(2)}, u32[]{:S(2)}) collective-permute-start(bf16[256,512]{1,0:T(8,128)(2,1)S(1)} %get-tuple-element.79.new_hi), channel_id=1, source_target_pairs={{0,16},{16,32},{32,48},{48,64},{64,80},{80,96},{96,112},{112,0},{1... | collective-permute-start | bytes 786440 | tf_op jit(solution)/shard_map/ppermute | solution.py:284
  35.2 10.8 %collective-permute-start.5 = (bf16[256,512]{1,0:T(8,128)(2,1)S(1)}, bf16[256,512]{1,0:T(8,128)(2,1)S(1)}, u32[]{:S(2)}, u32[]{:S(2)}) collective-permute-start(bf16[256,512]{1,0:T(8,128)(2,1)S(1)} %get-tuple-element.80.new_lo), channel_id=1, source_target_pairs={{0,112},{16,0},{32,16},{48,32},{64,48},{80,64},{96,80},{112,96},{1... | collective-permute-start | bytes 786440 | tf_op jit(solution)/shard_map/ppermute | solution.py:284
  37.6 8.4 %copy-start = (bf16[1,1024,512]{2,1,0:T(8,128)(2,1)S(1)}, bf16[1,1024,512]{2,1,0:T(8,128)(2,1)}, u32[]{:S(2)}) copy-start(bf16[1,1024,512]{2,1,0:T(8,128)(2,1)} %param.11) | copy-start | bytes 3145732
  52.3 7.3 %collective-permute-start.6 = (bf16[256,512]{1,0:T(8,128)(2,1)S(1)}, bf16[256,512]{1,0:T(8,128)(2,1)S(1)}, u32[]{:S(2)}, u32[]{:S(2)}) collective-permute-start(bf16[256,512]{1,0:T(8,128)(2,1)S(1)} %get-tuple-element.89), channel_id=1, source_target_pairs={{0,16},{16,32},{32,48},{48,64},{64,80},{80,96},{96,112},{112,0},{1... | collective-permute-start | bytes 786440 | tf_op jit(solution)/shard_map/ppermute | solution.py:284
  53.2 10.2 %collective-permute-start.7 = (bf16[256,512]{1,0:T(8,128)(2,1)S(1)}, bf16[256,512]{1,0:T(8,128)(2,1)S(1)}, u32[]{:S(2)}, u32[]{:S(2)}) collective-permute-start(bf16[256,512]{1,0:T(8,128)(2,1)S(1)} %get-tuple-element.90), channel_id=1, source_target_pairs={{0,112},{16,0},{32,16},{48,32},{64,48},{80,64},{96,80},{112,96},{1... | collective-permute-start | bytes 786440 | tf_op jit(solution)/shard_map/ppermute | solution.py:284
  65.6 13.6 %collective-permute-start.8 = (bf16[256,512]{1,0:T(8,128)(2,1)S(1)}, bf16[256,512]{1,0:T(8,128)(2,1)S(1)}, u32[]{:S(2)}, u32[]{:S(2)}) collective-permute-start(bf16[256,512]{1,0:T(8,128)(2,1)S(1)} %get-tuple-element.97), channel_id=1, source_target_pairs={{0,16},{16,32},{32,48},{48,64},{64,80},{80,96},{96,112},{112,0},{1... | collective-permute-start | bytes 786440 | tf_op jit(solution)/shard_map/ppermute | solution.py:284
  65.7 13.5 %collective-permute-start.9 = (bf16[256,512]{1,0:T(8,128)(2,1)S(1)}, bf16[256,512]{1,0:T(8,128)(2,1)S(1)}, u32[]{:S(2)}, u32[]{:S(2)}) collective-permute-start(bf16[256,512]{1,0:T(8,128)(2,1)S(1)} %get-tuple-element.98), channel_id=1, source_target_pairs={{0,112},{16,0},{32,16},{48,32},{64,48},{80,64},{96,80},{112,96},{1... | collective-permute-start | bytes 786440 | tf_op jit(solution)/shard_map/ppermute | solution.py:284
  70.5 14.8 %collective-permute-start.12 = (bf16[1024,256]{1,0:T(8,128)(2,1)S(1)}, bf16[1024,256]{1,0:T(8,128)(2,1)S(1)}, u32[]{:S(2)}, u32[]{:S(2)}) collective-permute-start(bf16[1024,256]{1,0:T(8,128)(2,1)S(1)} %get-tuple-element.114), channel_id=1, source_target_pairs={{0,1},{1,0},{2,3},{3,2},{4,5},{5,4},{6,7},{7,6},{8,9},{9,8},{10,11... | collective-permute-start | bytes 1572872 | tf_op jit(solution)/shard_map/ppermute | solution.py:345
  76.5 9.0 %collective-permute-start.11 = (bf16[1024,256]{1,0:T(8,128)(2,1)S(1)}, bf16[1024,256]{1,0:T(8,128)(2,1)S(1)}, u32[]{:S(2)}, u32[]{:S(2)}) collective-permute-start(bf16[1024,256]{1,0:T(8,128)(2,1)S(1)} %get-tuple-element.111), channel_id=1, source_target_pairs={{0,1},{1,0},{2,3},{3,2},{4,5},{5,4},{6,7},{7,6},{8,9},{9,8},{10,11... | collective-permute-start | bytes 1572872 | tf_op jit(solution)/shard_map/ppermute | solution.py:345
  81.4 1.3 copy-start.5
  82.7 0.7 copy-start.12
  82.7 2.7 %copy-start.3 = (f32[1536,512]{1,0:T(8,128)}, f32[1536,512]{1,0:T(8,128)S(1)}, u32[]{:S(2)}) copy-start(f32[1536,512]{1,0:T(8,128)S(1)} %get-tuple-element.116.back) | copy-start | bytes 9437188
  84.7 2.1 %collective-permute-start.10 = (bf16[1024,256]{1,0:T(8,128)(2,1)S(1)}, bf16[1024,256]{1,0:T(8,128)(2,1)S(1)}, u32[]{:S(2)}, u32[]{:S(2)}) collective-permute-start(bf16[1024,256]{1,0:T(8,128)(2,1)S(1)} %get-tuple-element.108), channel_id=1, source_target_pairs={{0,1},{1,0},{2,3},{3,2},{4,5},{5,4},{6,7},{7,6},{8,9},{9,8},{10,11... | collective-permute-start | bytes 1572872 | tf_op jit(solution)/shard_map/ppermute | solution.py:345
  88.2 42.3 %all-to-all-start = ((bf16[64,48,256]{2,1,0:T(8,128)(2,1)}), bf16[64,48,256]{2,1,0:T(8,128)(2,1)S(1)}, u32[]{:S(2)}, u32[]{:S(2)}) async-start(bf16[64,48,256]{2,1,0:T(8,128)(2,1)} %all_parts.1), calls=%async_computation | async-start | bytes 3145728 | tf_op jit(solution)/shard_map/all_to_all | solution.py:348
  98.1 28.1 %collective-permute-start.13 = (bf16[256,512]{1,0:T(8,128)(2,1)}, bf16[256,512]{1,0:T(8,128)(2,1)S(1)}, u32[]{:S(2)}, u32[]{:S(2)}) collective-permute-start(bf16[256,512]{1,0:T(8,128)(2,1)} %copy-done.12), channel_id=1, source_target_pairs={{0,16},{16,32},{32,48},{48,64},{64,80},{80,96},{96,112},{112,0},{1... | collective-permute-start | bytes 786440 | tf_op jit(solution)/shard_map/ppermute | solution.py:284
  99.2 30.2 %collective-permute-start.14 = (bf16[256,512]{1,0:T(8,128)(2,1)S(1)}, bf16[256,512]{1,0:T(8,128)(2,1)S(1)}, u32[]{:S(2)}, u32[]{:S(2)}) collective-permute-start(bf16[256,512]{1,0:T(8,128)(2,1)S(1)} %get-tuple-element.119), channel_id=1, source_target_pairs={{0,112},{16,0},{32,16},{48,32},{64,48},{80,64},{96,80},{112,96},{1... | collective-permute-start | bytes 786440 | tf_op jit(solution)/shard_map/ppermute | solution.py:284
  101.7 1.9 %copy-start.4 = (f32[1536,512]{1,0:T(8,128)S(1)}, f32[1536,512]{1,0:T(8,128)}, u32[]{:S(2)}) copy-start(f32[1536,512]{1,0:T(8,128)} %copy-done.3) | copy-start | bytes 9437188
  103.6 1.6 copy-start.6
  159.8 6.5 %collective-permute-start.15 = (bf16[64,48,256]{2,1,0:T(8,128)(2,1)S(1)}, bf16[64,48,256]{2,1,0:T(8,128)(2,1)S(1)}, u32[]{:S(2)}, u32[]{:S(2)}) collective-permute-start(bf16[64,48,256]{2,1,0:T(8,128)(2,1)S(1)} %all_to_all.10.mine), channel_id=1, source_target_pairs={{0,1},{1,0},{2,3},{3,2},{4,5},{5,4},{6,7},{7,6},{8,9},{9,8},{10,11... | collective-permute-start | bytes 4718600 | tf_op jit(solution)/shard_map/ppermute | solution.py:376

commit v3 on v2

--- a/solution.py
+++ b/solution.py
@@ -222,7 +222,7 @@
     out[ROWS - RIM :, :] = (grad[ROWS - RIM :, :] + from_next[...].astype(F32)).astype(BF)
 
 
-def weight_grad(hidden, agg, gp, keep, send):
+def weight_grad(hidden, agg, gp, _, keep, send):
     core = lax.axis_index("core")
     for i, left in enumerate((hidden, agg)):
         full = dot_tn(left[...], gp[...]).astype(BF)
@@ -232,27 +232,45 @@
         send[i * F : (i + 1) * F, :] = jnp.where(first, high, low)
 
 
-def add_halves(mine, other, out):
-    out[...] = (mine[...].astype(F32) + other[...].astype(F32)).astype(BF)
+def add_halves(mine, other, _, keep, send):
+    y_bit = lax.rem(lax.div(lax.axis_index("dq"), jnp.int32(2)), jnp.int32(2))
+    chip = (mine[...].astype(F32) + other[...].astype(F32)).astype(BF)
+    low, high = chip[:, : F // 4], chip[:, F // 4 :]
+    first = jnp.broadcast_to(y_bit == 0, low.shape)
+    keep[...] = jnp.where(first, low, high)
+    send[...] = jnp.where(first, high, low)
 
 
 def all_parts(*refs):
     out = refs[-1]
-    depth = out.shape[1] // LAYERS
-    for layer in range(LAYERS):
-        if layer:
-            chip = refs[layer + 1][...]
-        else:
-            chip = (refs[0][...].astype(F32) + refs[1][...].astype(F32)).astype(BF)
-        for i in range(out.shape[0]):
-            out[i, layer * depth : (layer + 1) * depth, :] = chip[i * depth : (i + 1) * depth, :]
+    depth = out.shape[1] // 2
+    sums = [(refs[2 * i][...].astype(F32) + refs[2 * i + 1][...].astype(F32)).astype(BF) for i in range(LAYERS)]
+    for i in range(out.shape[0]):
+        at = slice(i * depth, (i + 1) * depth)
+        out[i, :depth, :] = sums[0][at, :]
+        out[i, depth:, : F // 4] = sums[1][at, :]
+        out[i, depth:, F // 4 :] = sums[2][at, :]
 
 
 def sum_parts(parts, out):
-    total = parts[0].astype(F32)
-    for i in range(1, parts.shape[0]):
-        total += parts[i].astype(F32)
-    total = total.astype(BF)
+    depth = parts.shape[1] // 2
+    first = parts[0, :depth, :].astype(F32)
+    halves = [None, None]
+    for i in range(parts.shape[0]):
+        if i:
+            first += parts[i, :depth, :].astype(F32)
+        half = parts[i, depth:, :].astype(F32)
+        y_bit = i // 2 % 2
+        halves[y_bit] = half if halves[y_bit] is None else halves[y_bit] + half
+    low, high = halves
+    total = jnp.concatenate(
+        [
+            first,
+            jnp.concatenate([low[:, : F // 4], high[:, : F // 4]], axis=1),
+            jnp.concatenate([low[:, F // 4 :], high[:, F // 4 :]], axis=1),
+        ],
+        axis=0,
+    ).astype(BF)
     for i in range(out.shape[0]):
         out[i] = total
 
@@ -335,43 +353,56 @@
     grad = cotangent
 
     half = jax.ShapeDtypeStruct((ROWS, F // 2), BF)
-    pieces = jax.ShapeDtypeStruct((peers, LAYERS * ROWS // peers, F // 2), BF)
+    quarter = jax.ShapeDtypeStruct((ROWS, F // 4), BF)
+    sent = jax.ShapeDtypeStruct((peers, 2 * ROWS // peers, F // 2), BF)
+    summed = jax.ShapeDtypeStruct((peers, LAYERS * ROWS // peers, F // 2), BF)
     flip = [(0, 1), (1, 0)]
-
-    def weights(layer, gp):
-        keep, send = call(weight_grad, f"weight_grad{layer}", (half, half), [VM] * 3)(
-            hiddens[layer], aggs[layer], gp
+    y_flip = [(i, i ^ 2) for i in range(lax.axis_size("dq"))]
+
+    def weights(layer, gp, after):
+        keep, send = call(weight_grad, f"weight_grad{layer}", (half, half), [VM] * 3 + [HB])(
+            hiddens[layer], aggs[layer], gp, after
         )
         return keep, lax.ppermute(send, "core", flip)
 
     def spread(array):
         return lax.all_to_all(array, ("dom", "dq"), 0, 0, tiled=True)
 
-    chips = []
+    def pair(layer, keep, got, after):
+        mine, yours = call(add_halves, f"add_halves{layer}", (quarter, quarter), [VM, VM, HB])(
+            keep, got, after
+        )
+        return [mine, lax.ppermute(yours, "dq", y_flip)]
+
+    halves, waiting = [], None
     for layer in range(top, -1, -1):
         from_prev, from_next = swap(rim_lo, rim_hi)
-        keep, got = weights(layer, gp)
         if layer:
-            chips.append(call(add_halves, f"add_halves{layer}", half, [VM] * 2)(keep, got))
             grad, gp_m, part = call(
                 backward_mid, f"backward_mid{layer}",
                 (pinned((ROWS, F), F32), pinned((ROWS - 2 * RIM, F), BF), pinned((EXT * TB, F), F32)),
                 [SM] + [VM] * 7,
             )(source, adj_v, gp, grad, back, w_self[layer], slopes[layer - 1], w_nbr[layer - 1])
+            keep, got = weights(layer, gp, gp_m)
+            if waiting:
+                halves = pair(*waiting, gp_m)
             grad, gp, back, rim_lo, rim_hi = call(
                 backward_edge, f"backward_edge{layer - 1}",
                 (pinned((ROWS, F), F32), pinned((ROWS, F), BF), pinned((EXT * TB, F), F32), wide, wide),
                 [SM] + [VM] * 8,
             )(source, adj_v, from_prev, from_next, grad, slopes[layer - 1], w_nbr[layer - 1], gp_m, part)
+            waiting = layer, keep, got
     grad = call(
         backward_first, "backward_first", jax.ShapeDtypeStruct((ROWS, F), F32), [VM] * 4
     )(gp, grad, back, w_self[0])
-    parts = spread(call(all_parts, "all_parts", pieces, [VM] * 4)(keep, got, *chips[::-1]))
+    keep, got = weights(0, gp, grad)
     state_grad = call(
         backward_last, "backward_last", jax.ShapeDtypeStruct((ROWS, F), BF), [VM] * 3
     )(grad, from_prev, from_next)
-    out = call(sum_parts, "sum_parts", pieces, [VM])(parts)
+    halves = pair(*waiting, rim_lo) + halves
+    out = call(all_parts, "all_parts", sent, [VM] * 6)(keep, got, *halves)
     out, state_grad = lax.optimization_barrier((out, state_grad))
+    out = call(sum_parts, "sum_parts", summed, [VM])(spread(out))
     whole = spread(out)
     other = lax.ppermute(whole, "core", flip)
     total_rows = lax.axis_size("dq") * lax.axis_size("core") * n_dom * ROWS

time: 170 us -> 164 us (0.965)
  blocking collectives: 29 us -> 50.7 us
  waiting for transfers between devices: 47.4 us -> 27.9 us
  local copies, waits for them, and re-layouts: 12.6 us -> 7.15 us
  starting transfers between devices: 42.5 us -> 40.5 us
    all_to_all x1 -> x2, blocking collectives: 29 us -> 50.7 us  [spread(): return lax.all_to_all(array, ('dom', 'dq'), 0, 0, tiled=True)]
    ppermute x6, waiting for transfers between devices: 25.2 us -> 8.22 us  [swap(): lax.ppermute(to_next, 'dom', up)]
    all_to_all x1 -> x0, starting transfers between devices: 9.94 us -> none  [spread(): return lax.all_to_all(array, ('dom', 'dq'), 0, 0, tiled=True)]
    unnamed x26 -> x16, local copies, waits for them, and re-layouts: 12.6 us -> 7.15 us
    ppermute x3, starting transfers between devices: 5.33 us -> 10.3 us  [weights(): return (keep, lax.ppermute(send, 'core', flip))]
    ppermute x6, waiting for transfers between devices: 17.9 us -> 14.5 us  [swap(): lax.ppermute(to_prev, 'dom', down)]
    ppermute x0 -> x2, waiting for transfers between devices: none -> 2.18 us  [pair(): return [mine, lax.ppermute(yours, 'dq', y_flip)]]
  transfers between devices with their start and end apart: 17 -> 18, of which waited for: 11 -> 9; matrix products, arithmetic and copies ran while one was open for 0% -> 0% of each run, Pallas kernels for 12% -> 14%
where the time goes in v3:
time: 164 us; the launch traced here: 163 us
  blocking collectives  50.7 us (31%)
  starting transfers between devices  40.5 us (25%)
  Pallas kernels  36.3 us (22%)
  waiting for transfers between devices  27.9 us (17%)
  local copies, waits for them, and re-layouts  7.15 us (4%)
    all_to_all x2, blocking collectives, spread(): return lax.all_to_all(array, ('dom', 'dq'), 0, 0, tiled=True)  50.7 us
    ppermute x6, starting transfers between devices, swap(): lax.ppermute(to_prev, 'dom', down)  18.1 us
    ppermute x6, waiting for transfers between devices, swap(): lax.ppermute(to_prev, 'dom', down)  14.5 us
    ppermute x3, starting transfers between devices, weights(): return (keep, lax.ppermute(send, 'core', flip))  10.3 us
    ppermute x6, waiting for transfers between devices, swap(): lax.ppermute(to_next, 'dom', up)  8.22 us
    unnamed x16, local copies, waits for them, and re-layouts  7.15 us
    pallas_call x1, Pallas kernels, per_device(): call(turn, 'turn', (jax.ShapeDtypeStruct((ROWS, F), BF), pinned((ROWS, F)...  6.35 us
    ppermute x6, starting transfers between devices, swap(): lax.ppermute(to_next, 'dom', up)  5.63 us
  transfers between devices with their start and end apart: 18, of which 9 were waited for; matrix products, arithmetic and copies ran while one was open for 0% of the time, Pallas kernels for 14%

profile of v3, /device:TPU:1, one launch (start us, length us, event | category | flops | bytes accessed | tf_op | source)
XLA Modules:
  0.0 163.4 jit_solution(7428750601928867295)
XLA Ops:
  1.9 2.1 %collective-permute-start = (bf16[256,512]{1,0:T(8,128)(2,1)S(1)}, bf16[256,512]{1,0:T(8,128)(2,1)S(1)}, u32[]{:S(2)}, u32[]{:S(2)}) collective-permute-start(bf16[256,512]{1,0:T(8,128)(2,1)S(1)} %get-tuple-element.70), channel_id=1, source_target_pairs={{0,16},{16,32},{32,48},{48,64},{64,80},{80,96},{96,112},{112,0},{1... | collective-permute-start | bytes 786440 | tf_op jit(solution)/shard_map/ppermute | solution.py:302
  4.0 3.6 %collective-permute-start.1 = (bf16[256,512]{1,0:T(8,128)(2,1)S(1)}, bf16[256,512]{1,0:T(8,128)(2,1)S(1)}, u32[]{:S(2)}, u32[]{:S(2)}) collective-permute-start(bf16[256,512]{1,0:T(8,128)(2,1)S(1)} %get-tuple-element.71), channel_id=1, source_target_pairs={{0,112},{16,0},{32,16},{48,32},{64,48},{80,64},{96,80},{112,96},{1... | collective-permute-start | bytes 786440 | tf_op jit(solution)/shard_map/ppermute | solution.py:302
  13.5 1.9 %prepare.1 = (bf16[8,128,512]{2,1,0:T(8,128)(2,1)S(1)}, bf16[8,512,128]{2,1,0:T(8,128)(2,1)S(1)}, f32[1024,512]{1,0:T(8,128)S(1)}, bf16[1024,512]{1,0:T(8,128)(2...) custom-call(s32[8]{0:T(128)S(1)} %copy-done.7, ...), custom_call_target="tpu_custom_call" | custom-call | flops 1 | bytes 1 | tf_op jit(solution)/shard_map/prepare/pallas_call | solution.py:310
  15.5 1.5 collective-permute-done.1.hi
  17.0 1.8 %forward_edge0.1 = (bf16[256,512]{1,0:T(8,128)(2,1)S(1)}, bf16[256,512]{1,0:T(8,128)(2,1)S(1)}, bf16[512,512]{1,0:T(8,128)(2,1)S(1)}, f32[512,512]{1,0:T(8,128)S(1)}) custom-call(s32[4,8]{1,0:T(4,128)S(1)} %bitcast.9, bf16[8,128,512]{2,1,0:T(8,128)(2,1)S(1)} %get-tuple-element.68.adj, bf16[256,512]{1,0:T(8,128)(2,1)S(1)} %collective-permute-done.lo, ...), custom_call_target="tpu_custom_call" | custom-call | flops 1 | bytes 1 | tf_op jit(solution)/shard_map/forward_edge0/pallas_call | solution.py:323
  20.1 2.4 %collective-permute-start.3 = (bf16[256,512]{1,0:T(8,128)(2,1)S(1)}, bf16[256,512]{1,0:T(8,128)(2,1)S(1)}, u32[]{:S(2)}, u32[]{:S(2)}) collective-permute-start(bf16[256,512]{1,0:T(8,128)(2,1)S(1)} %get-tuple-element.76.new_lo), channel_id=1, source_target_pairs={{0,112},{16,0},{32,16},{48,32},{64,48},{80,64},{96,80},{112,96},{1... | collective-permute-start | bytes 786440 | tf_op jit(solution)/shard_map/ppermute | solution.py:302
  22.4 2.4 %forward_mid0.1 = (bf16[1024,512]{1,0:T(8,128)(2,1)S(1)}, bf16[1024,512]{1,0:T(8,128)(2,1)S(1)}, f32[1024,512]{1,0:T(8,128)S(1)}, f32[1024,512]{1,0:T(8,128)S(1)}) custom-call(s32[4,8]{1,0:T(4,128)S(1)} %bitcast.10, bf16[8,128,512]{2,1,0:T(8,128)(2,1)S(1)} %get-tuple-element.68.adj, bf16[256,512]{1,0:T(8,128)(2,1)S(1)} %collective-permute-done.lo, ...), custom_call_target="tpu_custom_call" | custom-call | flops 1 | bytes 1 | tf_op jit(solution)/shard_map/forward_mid0/pallas_call | solution.py:329
  24.8 2.4 %collective-permute-done.2.lo = bf16[256,512]{1,0:T(8,128)(2,1)S(1)} collective-permute-done((bf16[256,512]{1,0:T(8,128)(2,1)S(1)}, bf16[256,512]{1,0:T(8,128)(2,1)S(1)}, u32[]{:S(2)}, u32[]{:S(2)}) %collective-permute-start.2) | collective-permute-done | bytes 262176 | tf_op jit(solution)/shard_map/ppermute | solution.py:302
  27.2 4.9 %collective-permute-done.3.hi = bf16[256,512]{1,0:T(8,128)(2,1)S(1)} collective-permute-done((bf16[256,512]{1,0:T(8,128)(2,1)S(1)}, bf16[256,512]{1,0:T(8,128)(2,1)S(1)}, u32[]{:S(2)}, u32[]{:S(2)}) %collective-permute-start.3) | collective-permute-done | bytes 262176 | tf_op jit(solution)/shard_map/ppermute | solution.py:302
  32.1 1.8 %forward_edge1.1 = (bf16[256,512]{1,0:T(8,128)(2,1)S(1)}, bf16[256,512]{1,0:T(8,128)(2,1)S(1)}, bf16[512,512]{1,0:T(8,128)(2,1)S(1)}, f32[512,512]{1,0:T(8,128)S(1)}) custom-call(s32[4,8]{1,0:T(4,128)S(1)} %bitcast.11, bf16[8,128,512]{2,1,0:T(8,128)(2,1)S(1)} %get-tuple-element.68.adj, bf16[256,512]{1,0:T(8,128)(2,1)S(1)} %collective-permute-done.2.lo, ...), custom_call_target="tpu_custom_call" | custom-call | flops 1 | bytes 1 | tf_op jit(solution)/shard_map/forward_edge1/pallas_call | solution.py:323
  35.2 2.4 %collective-permute-start.5 = (bf16[256,512]{1,0:T(8,128)(2,1)S(1)}, bf16[256,512]{1,0:T(8,128)(2,1)S(1)}, u32[]{:S(2)}, u32[]{:S(2)}) collective-permute-start(bf16[256,512]{1,0:T(8,128)(2,1)S(1)} %get-tuple-element.84.new_lo), channel_id=1, source_target_pairs={{0,112},{16,0},{32,16},{48,32},{64,48},{80,64},{96,80},{112,96},{1... | collective-permute-start | bytes 786440 | tf_op jit(solution)/shard_map/ppermute | solution.py:302
  37.6 2.4 %forward_mid1.1 = (bf16[1024,512]{1,0:T(8,128)(2,1)S(1)}, bf16[1024,512]{1,0:T(8,128)(2,1)S(1)}, f32[1024,512]{1,0:T(8,128)S(1)}, f32[1024,512]{1,0:T(8,128)S(1)}) custom-call(s32[4,8]{1,0:T(4,128)S(1)} %bitcast.12, bf16[8,128,512]{2,1,0:T(8,128)(2,1)S(1)} %get-tuple-element.68.adj, bf16[256,512]{1,0:T(8,128)(2,1)S(1)} %collective-permute-done.2.lo, ...), custom_call_target="tpu_custom_call" | custom-call | flops 1 | bytes 1 | tf_op jit(solution)/shard_map/forward_mid1/pallas_call | solution.py:329
  41.3 4.7 %collective-permute-done.5.hi = bf16[256,512]{1,0:T(8,128)(2,1)S(1)} collective-permute-done((bf16[256,512]{1,0:T(8,128)(2,1)S(1)}, bf16[256,512]{1,0:T(8,128)(2,1)S(1)}, u32[]{:S(2)}, u32[]{:S(2)}) %collective-permute-start.5) | collective-permute-done | bytes 262176 | tf_op jit(solution)/shard_map/ppermute | solution.py:302
  46.0 6.4 %turn.1 = (bf16[1024,512]{1,0:T(8,128)(2,1)}, bf16[1024,512]{1,0:T(8,128)(2,1)S(1)}, bf16[1024,512]{1,0:T(8,128)(2,1)S(1)}, f32[1536,512]{1,0:T(8,128)S(1)}, bf1...) custom-call(s32[4,8]{1,0:T(4,128)S(1)} %bitcast.13, bf16[8,128,512]{2,1,0:T(8,128)(2,1)S(1)} %get-tuple-element.68.adj, ...), custom_call_target="tpu_custom_call" | custom-call | flops 1 | bytes 1 | tf_op jit(solution)/shard_map/turn/pallas_call | solution.py:344
  53.2 2.7 %collective-permute-start.7 = (bf16[256,512]{1,0:T(8,128)(2,1)S(1)}, bf16[256,512]{1,0:T(8,128)(2,1)S(1)}, u32[]{:S(2)}, u32[]{:S(2)}) collective-permute-start(bf16[256,512]{1,0:T(8,128)(2,1)S(1)} %get-tuple-element.94), channel_id=1, source_target_pairs={{0,112},{16,0},{32,16},{48,32},{64,48},{80,64},{96,80},{112,96},{1... | collective-permute-start | bytes 786440 | tf_op jit(solution)/shard_map/ppermute | solution.py:302
  55.9 2.6 %backward_mid2.1 = (f32[1024,512]{1,0:T(8,128)S(1)}, bf16[512,512]{1,0:T(8,128)(2,1)S(1)}, f32[1536,512]{1,0:T(8,128)S(1)}) custom-call(s32[4,8]{1,0:T(4,128)S(1)} %bitcast.14, bf16[8,512,128]{2,1,0:T(8,128)(2,1)S(1)} %get-tuple-element.69.adj_v, bf16[1024,512]{1,0:T(8,128)(2,1)S(1)} %get-tuple-element.95.gp, bf16[1024,512]{1,0:T(8,128)(2,1)S(1)} %bitcast.6, ...), custom_call_target="tpu_custom_call" | custom-call | flops 1 | bytes 1 | tf_op jit(solution)/shard_map/backward_mid2/pallas_call | solution.py:381
  59.9 4.0 %collective-permute-start.13 = (bf16[1024,256]{1,0:T(8,128)(2,1)S(1)}, bf16[1024,256]{1,0:T(8,128)(2,1)S(1)}, u32[]{:S(2)}, u32[]{:S(2)}) collective-permute-start(bf16[1024,256]{1,0:T(8,128)(2,1)S(1)} %get-tuple-element.124), channel_id=1, source_target_pairs={{0,1},{1,0},{2,3},{3,2},{4,5},{5,4},{6,7},{7,6},{8,9},{9,8},{10,11... | collective-permute-start | bytes 1572872 | tf_op jit(solution)/shard_map/ppermute | solution.py:366
  63.9 2.2 %backward_edge1.1 = (f32[1024,512]{1,0:T(8,128)S(1)}, bf16[1024,512]{1,0:T(8,128)(2,1)S(1)}, f32[1536,512]{1,0:T(8,128)S(1)}, bf16[256,512]{1,0:T(8,128)(2,1)S(1)}, bf16[256,512]{1,0:T(8,128)(2,1)S(1)}) custom-call(s32[4,8]{1,0:T(4,128)S(1)} %bitcast.15, bf16[8,512,128]{2,1,0:T(8,128)(2,1)S(1)} %get-tuple-element.69.adj_v, ...), custom_call_target="tpu_custom_call" | custom-call | flops 1 | bytes 1 | tf_op jit(solution)/shard_map/backward_edge1/pallas_call | solution.py:389
  66.2 3.6 %collective-permute-start.9 = (bf16[256,512]{1,0:T(8,128)(2,1)S(1)}, bf16[256,512]{1,0:T(8,128)(2,1)S(1)}, u32[]{:S(2)}, u32[]{:S(2)}) collective-permute-start(bf16[256,512]{1,0:T(8,128)(2,1)S(1)} %get-tuple-element.102), channel_id=1, source_target_pairs={{0,112},{16,0},{32,16},{48,32},{64,48},{80,64},{96,80},{112,96},{1... | collective-permute-start | bytes 786440 | tf_op jit(solution)/shard_map/ppermute | solution.py:302
  69.8 2.6 %backward_mid1.1 = (f32[1024,512]{1,0:T(8,128)S(1)}, bf16[512,512]{1,0:T(8,128)(2,1)S(1)}, f32[1536,512]{1,0:T(8,128)S(1)}) custom-call(s32[4,8]{1,0:T(4,128)S(1)} %bitcast.16, bf16[8,512,128]{2,1,0:T(8,128)(2,1)S(1)} %get-tuple-element.69.adj_v, bf16[1024,512]{1,0:T(8,128)(2,1)S(1)} %get-tuple-element.103.gp, f32[1024,512]{1,0:T(8,128)S(1)} %get-tuple-element.104.grad, ...), custom_call_target="tpu_custom_call" | custom-call | flops 1 | bytes 1 | tf_op jit(solution)/shard_map/backward_mid1/pallas_call | solution.py:381
  73.7 4.1 %collective-permute-start.11 = (bf16[1024,256]{1,0:T(8,128)(2,1)S(1)}, bf16[1024,256]{1,0:T(8,128)(2,1)S(1)}, u32[]{:S(2)}, u32[]{:S(2)}) collective-permute-start(bf16[1024,256]{1,0:T(8,128)(2,1)S(1)} %get-tuple-element.118), channel_id=1, source_target_pairs={{0,1},{1,0},{2,3},{3,2},{4,5},{5,4},{6,7},{7,6},{8,9},{9,8},{10,11... | collective-permute-start | bytes 1572872 | tf_op jit(solution)/shard_map/ppermute | solution.py:366
  77.8 2.2 %backward_edge0.1 = (f32[1024,512]{1,0:T(8,128)S(1)}, bf16[1024,512]{1,0:T(8,128)(2,1)S(1)}, f32[1536,512]{1,0:T(8,128)S(1)}, bf16[256,512]{1,0:T(8,128)(2,1)S(1)}, bf16[256,512]{1,0:T(8,128)(2,1)S(1)}) custom-call(s32[4,8]{1,0:T(4,128)S(1)} %bitcast.17, bf16[8,512,128]{2,1,0:T(8,128)(2,1)S(1)} %get-tuple-element.69.adj_v, ...), custom_call_target="tpu_custom_call" | custom-call | flops 1 | bytes 1 | tf_op jit(solution)/shard_map/backward_edge0/pallas_call | solution.py:389
  82.0 2.1 %collective-permute-start.10 = (bf16[1024,256]{1,0:T(8,128)(2,1)S(1)}, bf16[1024,256]{1,0:T(8,128)(2,1)S(1)}, u32[]{:S(2)}, u32[]{:S(2)}) collective-permute-start(bf16[1024,256]{1,0:T(8,128)(2,1)S(1)} %get-tuple-element.115), channel_id=1, source_target_pairs={{0,1},{1,0},{2,3},{3,2},{4,5},{5,4},{6,7},{7,6},{8,9},{9,8},{10,11... | collective-permute-start | bytes 1572872 | tf_op jit(solution)/shard_map/ppermute | solution.py:366
  84.1 3.6 %collective-permute-start.16 = (bf16[256,512]{1,0:T(8,128)(2,1)S(1)}, bf16[256,512]{1,0:T(8,128)(2,1)S(1)}, u32[]{:S(2)}, u32[]{:S(2)}) collective-permute-start(bf16[256,512]{1,0:T(8,128)(2,1)S(1)} %get-tuple-element.119._), channel_id=1, source_target_pairs={{0,112},{16,0},{32,16},{48,32},{64,48},{80,64},{96,80},{112,96},{1... | collective-permute-start | bytes 786440 | tf_op jit(solution)/shard_map/ppermute | solution.py:302
  89.7 4.4 %collective-permute-done.15.from_prev = bf16[256,512]{1,0:T(8,128)(2,1)S(1)} collective-permute-done((bf16[256,512]{1,0:T(8,128)(2,1)S(1)}, bf16[256,512]{1,0:T(8,128)(2,1)S(1)}, u32[]{:S(2)}, u32[]{:S(2)}) %collective-permute-start.15) | collective-permute-done | bytes 262176 | tf_op jit(solution)/shard_map/ppermute | solution.py:302
  94.1 3.4 %collective-permute-done.16.from_next = bf16[256,512]{1,0:T(8,128)(2,1)S(1)} collective-permute-done((bf16[256,512]{1,0:T(8,128)(2,1)S(1)}, bf16[256,512]{1,0:T(8,128)(2,1)S(1)}, u32[]{:S(2)}, u32[]{:S(2)}) %collective-permute-start.16) | collective-permute-done | bytes 262176 | tf_op jit(solution)/shard_map/ppermute | solution.py:302
  98.6 2.2 %collective-permute-done.12.refs_3_ = bf16[1024,128]{1,0:T(8,128)(2,1)S(1)} collective-permute-done((bf16[1024,128]{1,0:T(8,128)(2,1)S(1)}, bf16[1024,128]{1,0:T(8,128)(2,1)S(1)}, u32[]{:S(2)}, u32[]{:S(2)}) %collective-permute-start.12) | collective-permute-done | bytes 262176 | tf_op jit(solution)/shard_map/ppermute | solution.py:375
  101.1 24.7 %all_to_all.10.parts = bf16[64,32,256]{2,1,0:T(8,128)(2,1)S(1)} all-to-all(bf16[64,32,256]{2,1,0:T(8,128)(2,1)S(1)} %all_parts.1), channel_id=1, replica_groups=mesh['dom'=8,'dq'=8,'core'=2] {'dom','dq'}, dimensions={0} | all-to-all | bytes 2097152 | tf_op jit(solution)/shard_map/all_to_all | solution.py:369
  126.0 26.1 %all_to_all.11.mine = bf16[64,48,256]{2,1,0:T(8,128)(2,1)S(1)} all-to-all(bf16[64,48,256]{2,1,0:T(8,128)(2,1)S(1)} %sum_parts.1), channel_id=1, replica_groups=mesh['dom'=8,'dq'=8,'core'=2] {'dom','dq'}, dimensions={0} | all-to-all | bytes 3145728 | tf_op jit(solution)/shard_map/all_to_all | solution.py:369
  152.1 4.9 %collective-permute-start.17 = (bf16[64,48,256]{2,1,0:T(8,128)(2,1)S(1)}, bf16[64,48,256]{2,1,0:T(8,128)(2,1)S(1)}, u32[]{:S(2)}, u32[]{:S(2)}) collective-permute-start(bf16[64,48,256]{2,1,0:T(8,128)(2,1)S(1)} %all_to_all.11.mine), channel_id=1, source_target_pairs={{0,1},{1,0},{2,3},{3,2},{4,5},{5,4},{6,7},{7,6},{8,9},{9,8},{10,11... | collective-permute-start | bytes 4718600 | tf_op jit(solution)/shard_map/ppermute | solution.py:407
  156.9 3.0 %collective-permute-done.17.other = bf16[64,48,256]{2,1,0:T(8,128)(2,1)S(1)} collective-permute-done((bf16[64,48,256]{2,1,0:T(8,128)(2,1)S(1)}, bf16[64,48,256]{2,1,0:T(8,128)(2,1)S(1)}, u32[]{:S(2)}, u32[]{:S(2)}) %collective-permute-start.17) | collective-permute-done | bytes 1572896 | tf_op jit(solution)/shard_map/ppermute | solution.py:407
  160.0 3.4 %unpack.1 = (f32[3,512,512]{2,1,0:T(8,128)}, f32[3,512,512]{2,1,0:T(8,128)}) custom-call(bf16[64,48,256]{2,1,0:T(8,128)(2,1)S(1)} %all_to_all.11.mine, bf16[64,48,256]{2,1,0:T(8,128)(2,1)S(1)} %collective-permute-done.17.other), custom_call_target="tpu_custom_call" | custom-call | flops 1 | bytes 1 | tf_op jit(solution)/shard_map/unpack/pallas_call | solution.py:410
  (43 shorter events, 20.3 us)
Async XLA Ops:
  0.6 1.2 copy-start.1
  1.9 13.5 %collective-permute-start = (bf16[256,512]{1,0:T(8,128)(2,1)S(1)}, bf16[256,512]{1,0:T(8,128)(2,1)S(1)}, u32[]{:S(2)}, u32[]{:S(2)}) collective-permute-start(bf16[256,512]{1,0:T(8,128)(2,1)S(1)} %get-tuple-element.70), channel_id=1, source_target_pairs={{0,16},{16,32},{32,48},{48,64},{64,80},{80,96},{96,112},{112,0},{1... | collective-permute-start | bytes 786440 | tf_op jit(solution)/shard_map/ppermute | solution.py:302
  4.0 12.9 %collective-permute-start.1 = (bf16[256,512]{1,0:T(8,128)(2,1)S(1)}, bf16[256,512]{1,0:T(8,128)(2,1)S(1)}, u32[]{:S(2)}, u32[]{:S(2)}) collective-permute-start(bf16[256,512]{1,0:T(8,128)(2,1)S(1)} %get-tuple-element.71), channel_id=1, source_target_pairs={{0,112},{16,0},{32,16},{48,32},{64,48},{80,64},{96,80},{112,96},{1... | collective-permute-start | bytes 786440 | tf_op jit(solution)/shard_map/ppermute | solution.py:302
  7.6 1.2 copy-start.2
  8.8 1.4 copy-start.3
  10.2 1.4 copy-start.4
  11.6 1.2 copy-start.5
  12.9 0.7 copy-start.7
  13.5 3.5 %copy-start.6 = (s32[8,4]{0,1:T(4,128)S(1)}, s32[8,4]{0,1:T(4,128)}, u32[]{:S(2)}) copy-start(s32[8,4]{0,1:T(4,128)} %param.9) | copy-start | bytes 388
  18.8 8.4 %collective-permute-start.2 = (bf16[256,512]{1,0:T(8,128)(2,1)S(1)}, bf16[256,512]{1,0:T(8,128)(2,1)S(1)}, u32[]{:S(2)}, u32[]{:S(2)}) collective-permute-start(bf16[256,512]{1,0:T(8,128)(2,1)S(1)} %get-tuple-element.75.new_hi), channel_id=1, source_target_pairs={{0,16},{16,32},{32,48},{48,64},{64,80},{80,96},{96,112},{112,0},{1... | collective-permute-start | bytes 786440 | tf_op jit(solution)/shard_map/ppermute | solution.py:302
  20.1 12.0 %collective-permute-start.3 = (bf16[256,512]{1,0:T(8,128)(2,1)S(1)}, bf16[256,512]{1,0:T(8,128)(2,1)S(1)}, u32[]{:S(2)}, u32[]{:S(2)}) collective-permute-start(bf16[256,512]{1,0:T(8,128)(2,1)S(1)} %get-tuple-element.76.new_lo), channel_id=1, source_target_pairs={{0,112},{16,0},{32,16},{48,32},{64,48},{80,64},{96,80},{112,96},{1... | collective-permute-start | bytes 786440 | tf_op jit(solution)/shard_map/ppermute | solution.py:302
  33.9 7.4 %collective-permute-start.4 = (bf16[256,512]{1,0:T(8,128)(2,1)S(1)}, bf16[256,512]{1,0:T(8,128)(2,1)S(1)}, u32[]{:S(2)}, u32[]{:S(2)}) collective-permute-start(bf16[256,512]{1,0:T(8,128)(2,1)S(1)} %get-tuple-element.83.new_hi), channel_id=1, source_target_pairs={{0,16},{16,32},{32,48},{48,64},{64,80},{80,96},{96,112},{112,0},{1... | collective-permute-start | bytes 786440 | tf_op jit(solution)/shard_map/ppermute | solution.py:302
  35.2 10.8 %collective-permute-start.5 = (bf16[256,512]{1,0:T(8,128)(2,1)S(1)}, bf16[256,512]{1,0:T(8,128)(2,1)S(1)}, u32[]{:S(2)}, u32[]{:S(2)}) collective-permute-start(bf16[256,512]{1,0:T(8,128)(2,1)S(1)} %get-tuple-element.84.new_lo), channel_id=1, source_target_pairs={{0,112},{16,0},{32,16},{48,32},{64,48},{80,64},{96,80},{112,96},{1... | collective-permute-start | bytes 786440 | tf_op jit(solution)/shard_map/ppermute | solution.py:302
  37.6 8.4 %copy-start = (bf16[1,1024,512]{2,1,0:T(8,128)(2,1)S(1)}, bf16[1,1024,512]{2,1,0:T(8,128)(2,1)}, u32[]{:S(2)}) copy-start(bf16[1,1024,512]{2,1,0:T(8,128)(2,1)} %param.11) | copy-start | bytes 3145732
  52.3 11.6 %collective-permute-start.6 = (bf16[256,512]{1,0:T(8,128)(2,1)S(1)}, bf16[256,512]{1,0:T(8,128)(2,1)S(1)}, u32[]{:S(2)}, u32[]{:S(2)}) collective-permute-start(bf16[256,512]{1,0:T(8,128)(2,1)S(1)} %get-tuple-element.93), channel_id=1, source_target_pairs={{0,16},{16,32},{32,48},{48,64},{64,80},{80,96},{96,112},{112,0},{1... | collective-permute-start | bytes 786440 | tf_op jit(solution)/shard_map/ppermute | solution.py:302
  53.2 10.7 %collective-permute-start.7 = (bf16[256,512]{1,0:T(8,128)(2,1)S(1)}, bf16[256,512]{1,0:T(8,128)(2,1)S(1)}, u32[]{:S(2)}, u32[]{:S(2)}) collective-permute-start(bf16[256,512]{1,0:T(8,128)(2,1)S(1)} %get-tuple-element.94), channel_id=1, source_target_pairs={{0,112},{16,0},{32,16},{48,32},{64,48},{80,64},{96,80},{112,96},{1... | collective-permute-start | bytes 786440 | tf_op jit(solution)/shard_map/ppermute | solution.py:302
  59.9 27.9 %collective-permute-start.13 = (bf16[1024,256]{1,0:T(8,128)(2,1)S(1)}, bf16[1024,256]{1,0:T(8,128)(2,1)S(1)}, u32[]{:S(2)}, u32[]{:S(2)}) collective-permute-start(bf16[1024,256]{1,0:T(8,128)(2,1)S(1)} %get-tuple-element.124), channel_id=1, source_target_pairs={{0,1},{1,0},{2,3},{3,2},{4,5},{5,4},{6,7},{7,6},{8,9},{9,8},{10,11... | collective-permute-start | bytes 1572872 | tf_op jit(solution)/shard_map/ppermute | solution.py:366
  66.1 11.7 %collective-permute-start.8 = (bf16[256,512]{1,0:T(8,128)(2,1)S(1)}, bf16[256,512]{1,0:T(8,128)(2,1)S(1)}, u32[]{:S(2)}, u32[]{:S(2)}) collective-permute-start(bf16[256,512]{1,0:T(8,128)(2,1)S(1)} %get-tuple-element.101), channel_id=1, source_target_pairs={{0,16},{16,32},{32,48},{48,64},{64,80},{80,96},{96,112},{112,0},{1... | collective-permute-start | bytes 786440 | tf_op jit(solution)/shard_map/ppermute | solution.py:302
  66.2 11.6 %collective-permute-start.9 = (bf16[256,512]{1,0:T(8,128)(2,1)S(1)}, bf16[256,512]{1,0:T(8,128)(2,1)S(1)}, u32[]{:S(2)}, u32[]{:S(2)}) collective-permute-start(bf16[256,512]{1,0:T(8,128)(2,1)S(1)} %get-tuple-element.102), channel_id=1, source_target_pairs={{0,112},{16,0},{32,16},{48,32},{64,48},{80,64},{96,80},{112,96},{1... | collective-permute-start | bytes 786440 | tf_op jit(solution)/shard_map/ppermute | solution.py:302
  73.7 15.6 %collective-permute-start.11 = (bf16[1024,256]{1,0:T(8,128)(2,1)S(1)}, bf16[1024,256]{1,0:T(8,128)(2,1)S(1)}, u32[]{:S(2)}, u32[]{:S(2)}) collective-permute-start(bf16[1024,256]{1,0:T(8,128)(2,1)S(1)} %get-tuple-element.118), channel_id=1, source_target_pairs={{0,1},{1,0},{2,3},{3,2},{4,5},{5,4},{6,7},{7,6},{8,9},{9,8},{10,11... | collective-permute-start | bytes 1572872 | tf_op jit(solution)/shard_map/ppermute | solution.py:366
  82.0 18.8 %collective-permute-start.10 = (bf16[1024,256]{1,0:T(8,128)(2,1)S(1)}, bf16[1024,256]{1,0:T(8,128)(2,1)S(1)}, u32[]{:S(2)}, u32[]{:S(2)}) collective-permute-start(bf16[1024,256]{1,0:T(8,128)(2,1)S(1)} %get-tuple-element.115), channel_id=1, source_target_pairs={{0,1},{1,0},{2,3},{3,2},{4,5},{5,4},{6,7},{7,6},{8,9},{9,8},{10,11... | collective-permute-start | bytes 1572872 | tf_op jit(solution)/shard_map/ppermute | solution.py:366
  84.1 10.0 %collective-permute-start.15 = (bf16[256,512]{1,0:T(8,128)(2,1)S(1)}, bf16[256,512]{1,0:T(8,128)(2,1)S(1)}, u32[]{:S(2)}, u32[]{:S(2)}) collective-permute-start(bf16[256,512]{1,0:T(8,128)(2,1)S(1)} %get-tuple-element.127), channel_id=1, source_target_pairs={{0,16},{16,32},{32,48},{48,64},{64,80},{80,96},{96,112},{112,0},{1... | collective-permute-start | bytes 786440 | tf_op jit(solution)/shard_map/ppermute | solution.py:302
  84.1 13.4 %collective-permute-start.16 = (bf16[256,512]{1,0:T(8,128)(2,1)S(1)}, bf16[256,512]{1,0:T(8,128)(2,1)S(1)}, u32[]{:S(2)}, u32[]{:S(2)}) collective-permute-start(bf16[256,512]{1,0:T(8,128)(2,1)S(1)} %get-tuple-element.119._), channel_id=1, source_target_pairs={{0,112},{16,0},{32,16},{48,32},{64,48},{80,64},{96,80},{112,96},{1... | collective-permute-start | bytes 786440 | tf_op jit(solution)/shard_map/ppermute | solution.py:302
  87.9 10.7 %collective-permute-start.14 = (bf16[1024,128]{1,0:T(8,128)(2,1)S(1)}, bf16[1024,128]{1,0:T(8,128)(2,1)S(1)}, u32[]{:S(2)}, u32[]{:S(2)}) collective-permute-start(bf16[1024,128]{1,0:T(8,128)(2,1)S(1)} %get-tuple-element.126), channel_id=1, source_target_pairs={{0,4},{2,6},{4,0},{6,2},{8,12},{10,14},{12,8},{14,10},{1,5},{3,7},... | collective-permute-start | bytes 786440 | tf_op jit(solution)/shard_map/ppermute | solution.py:375
  89.5 11.3 %collective-permute-start.12 = (bf16[1024,128]{1,0:T(8,128)(2,1)S(1)}, bf16[1024,128]{1,0:T(8,128)(2,1)S(1)}, u32[]{:S(2)}, u32[]{:S(2)}) collective-permute-start(bf16[1024,128]{1,0:T(8,128)(2,1)S(1)} %get-tuple-element.121), channel_id=1, source_target_pairs={{0,4},{2,6},{4,0},{6,2},{8,12},{10,14},{12,8},{14,10},{1,5},{3,7},... | collective-permute-start | bytes 786440 | tf_op jit(solution)/shard_map/ppermute | solution.py:375
  152.1 7.9 %collective-permute-start.17 = (bf16[64,48,256]{2,1,0:T(8,128)(2,1)S(1)}, bf16[64,48,256]{2,1,0:T(8,128)(2,1)S(1)}, u32[]{:S(2)}, u32[]{:S(2)}) collective-permute-start(bf16[64,48,256]{2,1,0:T(8,128)(2,1)S(1)} %all_to_all.11.mine), channel_id=1, source_target_pairs={{0,1},{1,0},{2,3},{3,2},{4,5},{5,4},{6,7},{7,6},{8,9},{9,8},{10,11... | collective-permute-start | bytes 4718600 | tf_op jit(solution)/shard_map/ppermute | solution.py:407

commit v4 on v3

--- a/solution.py
+++ b/solution.py
@@ -33,16 +33,17 @@
     return pltpu.VMEM(shape, dtype)
 
 
-def call(body, name, out_shape, in_specs, scratch=()):
+def call(body, name, out_shape, in_specs, scratch=(), out_spec=VM, aliases={}, flops=1):
     return pl.pallas_call(
         body,
         name=name,
         out_shape=out_shape,
         in_specs=in_specs,
-        out_specs=jax.tree.map(lambda _: VM, out_shape, is_leaf=lambda x: hasattr(x, "shape")),
+        out_specs=jax.tree.map(lambda _: out_spec, out_shape, is_leaf=lambda x: hasattr(x, "shape")),
         scratch_shapes=list(scratch),
+        input_output_aliases=aliases,
         compiler_params=pltpu.CompilerParams(vmem_limit_bytes=12 * MB),
-        cost_estimate=pl.CostEstimate(flops=1, bytes_accessed=1, transcendentals=0),
+        cost_estimate=pl.CostEstimate(flops=flops, bytes_accessed=1, transcendentals=0),
     )
 
 
@@ -216,10 +217,13 @@
     grad_o[...] = grad[...] + dot_nt(gp[...], w_self[...]) + back[RIM : RIM + ROWS, :]
 
 
-def backward_last(grad, from_prev, from_next, out):
-    out[0:RIM, :] = (grad[0:RIM, :] + from_prev[...].astype(F32)).astype(BF)
-    out[RIM : ROWS - RIM, :] = grad[RIM : ROWS - RIM, :].astype(BF)
-    out[ROWS - RIM :, :] = (grad[ROWS - RIM :, :] + from_next[...].astype(F32)).astype(BF)
+def backward_last(grad, from_prev, from_next, out, ready, sem):
+    ready[0:RIM, :] = (grad[0:RIM, :] + from_prev[...].astype(F32)).astype(BF)
+    ready[RIM : ROWS - RIM, :] = grad[RIM : ROWS - RIM, :].astype(BF)
+    ready[ROWS - RIM :, :] = (grad[ROWS - RIM :, :] + from_next[...].astype(F32)).astype(BF)
+    copy = pltpu.make_async_copy(ready, out, sem)
+    copy.start()
+    copy.wait()
 
 
 def weight_grad(hidden, agg, gp, _, keep, send):
@@ -241,15 +245,18 @@
     send[...] = jnp.where(first, high, low)
 
 
-def all_parts(*refs):
-    out = refs[-1]
+def upper_parts(mine_1, other_1, mine_2, other_2, out):
+    for i, (a, b) in enumerate(((mine_1, other_1), (mine_2, other_2))):
+        out[:, i * F // 4 : (i + 1) * F // 4] = (a[...].astype(F32) + b[...].astype(F32)).astype(BF)
+
+
+def all_parts(mine, other, upper, _, out):
     depth = out.shape[1] // 2
-    sums = [(refs[2 * i][...].astype(F32) + refs[2 * i + 1][...].astype(F32)).astype(BF) for i in range(LAYERS)]
+    base = (mine[...].astype(F32) + other[...].astype(F32)).astype(BF)
     for i in range(out.shape[0]):
         at = slice(i * depth, (i + 1) * depth)
-        out[i, :depth, :] = sums[0][at, :]
-        out[i, depth:, : F // 4] = sums[1][at, :]
-        out[i, depth:, F // 4 :] = sums[2][at, :]
+        out[i, :depth, :] = base[at, :]
+        out[i, depth:, :] = upper[at, :]
 
 
 def sum_parts(parts, out):
@@ -275,18 +282,25 @@
         out[i] = total
 
 
-def unpack(factor, mine, other, *outs):
+def unpack(factor, flip, half, *refs):
+    self_o, nbr_o, ready, sems = refs[-4:]
     core = lax.axis_index("core")
-    depth = mine.shape[1] // LAYERS
+    start = pl.multiple_of((1 - core if flip else core) * (F // 2), F // 2)
+    depth = half.shape[1] // LAYERS
+    copies = []
     for layer in range(LAYERS):
         at = slice(layer * depth, (layer + 1) * depth)
-        for i, out in enumerate(outs):
+        for i, out in enumerate((self_o, nbr_o)):
             group = slice(i * F // depth, (i + 1) * F // depth)
-            a = mine[group, at, :].reshape(F, F // 2).astype(F32) * factor
-            b = other[group, at, :].reshape(F, F // 2).astype(F32) * factor
-            first = jnp.broadcast_to(core == 0, a.shape)
-            out[layer, :, : F // 2] = jnp.where(first, a, b)
-            out[layer, :, F // 2 :] = jnp.where(first, b, a)
+            ready[layer, i] = half[group, at, :].reshape(F, F // 2).astype(F32) * factor
+            copies.append(
+                pltpu.make_async_copy(
+                    ready.at[layer, i], out.at[layer, :, pl.ds(start, F // 2)], sems.at[layer, i]
+                )
+            )
+            copies[-1].start()
+    for copy in copies:
+        copy.wait()
 
 
 def per_device(state, blocks, source, count, cotangent, w_self, w_nbr):
@@ -389,27 +403,34 @@
             grad, gp, back, rim_lo, rim_hi = call(
                 backward_edge, f"backward_edge{layer - 1}",
                 (pinned((ROWS, F), F32), pinned((ROWS, F), BF), pinned((EXT * TB, F), F32), wide, wide),
-                [SM] + [VM] * 8,
+                [SM] + [VM] * 8, flops=9 * 10**9,
             )(source, adj_v, from_prev, from_next, grad, slopes[layer - 1], w_nbr[layer - 1], gp_m, part)
             waiting = layer, keep, got
     grad = call(
         backward_first, "backward_first", jax.ShapeDtypeStruct((ROWS, F), F32), [VM] * 4
     )(gp, grad, back, w_self[0])
-    keep, got = weights(0, gp, grad)
+    halves = pair(*waiting, rim_lo) + halves
+    keep, got = weights(0, gp, halves[0])
     state_grad = call(
-        backward_last, "backward_last", jax.ShapeDtypeStruct((ROWS, F), BF), [VM] * 3
+        backward_last, "backward_last", jax.ShapeDtypeStruct((ROWS, F), BF), [VM] * 3,
+        [pltpu.VMEM((ROWS, F), BF), pltpu.SemaphoreType.DMA], HB, flops=9 * 10**9,
     )(grad, from_prev, from_next)
-    halves = pair(*waiting, rim_lo) + halves
-    out = call(all_parts, "all_parts", sent, [VM] * 6)(keep, got, *halves)
-    out, state_grad = lax.optimization_barrier((out, state_grad))
+    upper = call(upper_parts, "upper_parts", half, [VM] * 4, flops=9 * 10**9)(*halves)
+    out = call(all_parts, "all_parts", sent, [VM] * 3 + [HB])(keep, got, upper, state_grad)
     out = call(sum_parts, "sum_parts", summed, [VM])(spread(out))
     whole = spread(out)
     other = lax.ppermute(whole, "core", flip)
     total_rows = lax.axis_size("dq") * lax.axis_size("core") * n_dom * ROWS
     grads = jax.ShapeDtypeStruct((LAYERS, F, F), F32)
+    factor = 1.0 / math.sqrt(total_rows)
+    scratch = [pltpu.VMEM((LAYERS, 2, F, F // 2), F32), pltpu.SemaphoreType.DMA((LAYERS, 2))]
+    own = call(
+        functools.partial(unpack, factor, False), "unpack_own", (grads, grads), [VM], scratch, HB
+    )(whole)
     self_grad, nbr_grad = call(
-        functools.partial(unpack, 1.0 / math.sqrt(total_rows)), "unpack", (grads, grads), [VM] * 2
-    )(whole, other)
+        functools.partial(unpack, factor, True), "unpack_other", (grads, grads), [VM, HB, HB],
+        scratch, HB, {1: 0, 2: 1},
+    )(other, *own)
     return final[None], state_grad[None], self_grad, nbr_grad
 
 

time: 164 us -> 158 us (0.963)
  starting transfers between devices: 40.5 us -> 36.9 us
  blocking collectives: 50.7 us -> 48.9 us
    ppermute x3, starting transfers between devices: 10.3 us -> 6.4 us  [weights(): return (keep, lax.ppermute(send, 'core', flip))]
    ppermute x6, waiting for transfers between devices: 8.22 us -> 4.9 us  [swap(): lax.ppermute(to_next, 'dom', up)]
    ppermute x6, waiting for transfers between devices: 14.5 us -> 16.4 us  [swap(): lax.ppermute(to_prev, 'dom', down)]
    all_to_all x2, blocking collectives: 50.7 us -> 48.9 us  [spread(): return lax.all_to_all(array, ('dom', 'dq'), 0, 0, tiled=True)]
    ppermute x2, waiting for transfers between devices: 2.18 us -> 3.95 us  [pair(): return [mine, lax.ppermute(yours, 'dq', y_flip)]]
    ppermute x1, waiting for transfers between devices: 3.04 us -> 1.28 us  [per_device(): other = lax.ppermute(whole, 'core', flip)]
    unnamed x16 -> x18, local copies, waits for them, and re-layouts: 7.15 us -> 8.22 us
    pallas_call x2 -> x4, Pallas kernels: 3.66 us -> 3.76 us  [the longest x1 1.75 us: per_device(): call(functools.partial(unpack, factor, False), 'unpack_own', (grads, grad...]
  transfers between devices with their start and end apart: 18 -> 18, of which waited for: 9 -> 10; matrix products, arithmetic and copies ran while one was open for 0% -> 0% of each run, Pallas kernels for 14% -> 14%
where the time goes in v4:
time: 158 us
  blocking collectives  48.9 us (31%)
  starting transfers between devices  36.9 us (23%)
  Pallas kernels  36.4 us (23%)
  waiting for transfers between devices  26.6 us (17%)
  local copies, waits for them, and re-layouts  8.22 us (5%)
    all_to_all x2, blocking collectives, spread(): return lax.all_to_all(array, ('dom', 'dq'), 0, 0, tiled=True)  48.9 us
    ppermute x6, starting transfers between devices, swap(): lax.ppermute(to_prev, 'dom', down)  18.1 us
    ppermute x6, waiting for transfers between devices, swap(): lax.ppermute(to_prev, 'dom', down)  16.4 us
    unnamed x18, local copies, waits for them, and re-layouts  8.22 us
    ppermute x3, starting transfers between devices, weights(): return (keep, lax.ppermute(send, 'core', flip))  6.4 us
    pallas_call x1, Pallas kernels, per_device(): call(turn, 'turn', (jax.ShapeDtypeStruct((ROWS, F), BF), pinned((ROWS, F)...  6.35 us
    ppermute x6, starting transfers between devices, swap(): lax.ppermute(to_next, 'dom', up)  5.7 us
    pallas_call x2, Pallas kernels, per_device(): call(backward_mid, f'backward_mid{layer}', (pinned((ROWS, F), F32), pinne...  5.29 us
  transfers between devices with their start and end apart: 18, of which 10 were waited for; matrix products, arithmetic and copies ran while one was open for 0% of the time, Pallas kernels for 14%

profile of v4, /device:TPU:1, one launch (start us, length us, event | category | flops | bytes accessed | tf_op | source)
XLA Modules:
  0.0 158.1 jit_solution(3774854463423055253)
XLA Ops:
  1.9 2.1 %collective-permute-start = (bf16[256,512]{1,0:T(8,128)(2,1)S(1)}, bf16[256,512]{1,0:T(8,128)(2,1)S(1)}, u32[]{:S(2)}, u32[]{:S(2)}) collective-permute-start(bf16[256,512]{1,0:T(8,128)(2,1)S(1)} %get-tuple-element.70), channel_id=1, source_target_pairs={{0,16},{16,32},{32,48},{48,64},{64,80},{80,96},{96,112},{112,0},{1... | collective-permute-start | bytes 786440 | tf_op jit(solution)/shard_map/ppermute | solution.py:316
  4.0 3.6 %collective-permute-start.1 = (bf16[256,512]{1,0:T(8,128)(2,1)S(1)}, bf16[256,512]{1,0:T(8,128)(2,1)S(1)}, u32[]{:S(2)}, u32[]{:S(2)}) collective-permute-start(bf16[256,512]{1,0:T(8,128)(2,1)S(1)} %get-tuple-element.71), channel_id=1, source_target_pairs={{0,112},{16,0},{32,16},{48,32},{64,48},{80,64},{96,80},{112,96},{1... | collective-permute-start | bytes 786440 | tf_op jit(solution)/shard_map/ppermute | solution.py:316
  8.8 1.4 copy-done.3
  13.5 1.9 %prepare.1 = (bf16[8,128,512]{2,1,0:T(8,128)(2,1)S(1)}, bf16[8,512,128]{2,1,0:T(8,128)(2,1)S(1)}, f32[1024,512]{1,0:T(8,128)S(1)}, bf16[1024,512]{1,0:T(8,128)(2...) custom-call(s32[8]{0:T(128)S(1)} %copy-done.8, ...), custom_call_target="tpu_custom_call" | custom-call | flops 1 | bytes 1 | tf_op jit(solution)/shard_map/prepare/pallas_call | solution.py:324
  15.5 1.5 collective-permute-done.1.hi
  17.0 1.8 %forward_edge0.1 = (bf16[256,512]{1,0:T(8,128)(2,1)S(1)}, bf16[256,512]{1,0:T(8,128)(2,1)S(1)}, bf16[512,512]{1,0:T(8,128)(2,1)S(1)}, f32[512,512]{1,0:T(8,128)S(1)}) custom-call(s32[4,8]{1,0:T(4,128)S(1)} %bitcast.10, bf16[8,128,512]{2,1,0:T(8,128)(2,1)S(1)} %get-tuple-element.68.adj, bf16[256,512]{1,0:T(8,128)(2,1)S(1)} %collective-permute-done.lo, ...), custom_call_target="tpu_custom_call" | custom-call | flops 1 | bytes 1 | tf_op jit(solution)/shard_map/forward_edge0/pallas_call | solution.py:337
  20.1 2.4 %collective-permute-start.3 = (bf16[256,512]{1,0:T(8,128)(2,1)S(1)}, bf16[256,512]{1,0:T(8,128)(2,1)S(1)}, u32[]{:S(2)}, u32[]{:S(2)}) collective-permute-start(bf16[256,512]{1,0:T(8,128)(2,1)S(1)} %get-tuple-element.76.new_lo), channel_id=1, source_target_pairs={{0,112},{16,0},{32,16},{48,32},{64,48},{80,64},{96,80},{112,96},{1... | collective-permute-start | bytes 786440 | tf_op jit(solution)/shard_map/ppermute | solution.py:316
  22.4 2.4 %forward_mid0.1 = (bf16[1024,512]{1,0:T(8,128)(2,1)S(1)}, bf16[1024,512]{1,0:T(8,128)(2,1)S(1)}, f32[1024,512]{1,0:T(8,128)S(1)}, f32[1024,512]{1,0:T(8,128)S(1)}) custom-call(s32[4,8]{1,0:T(4,128)S(1)} %bitcast.11, bf16[8,128,512]{2,1,0:T(8,128)(2,1)S(1)} %get-tuple-element.68.adj, bf16[256,512]{1,0:T(8,128)(2,1)S(1)} %collective-permute-done.lo, ...), custom_call_target="tpu_custom_call" | custom-call | flops 1 | bytes 1 | tf_op jit(solution)/shard_map/forward_mid0/pallas_call | solution.py:343
  24.8 2.4 %collective-permute-done.2.lo = bf16[256,512]{1,0:T(8,128)(2,1)S(1)} collective-permute-done((bf16[256,512]{1,0:T(8,128)(2,1)S(1)}, bf16[256,512]{1,0:T(8,128)(2,1)S(1)}, u32[]{:S(2)}, u32[]{:S(2)}) %collective-permute-start.2) | collective-permute-done | bytes 262176 | tf_op jit(solution)/shard_map/ppermute | solution.py:316
  27.2 4.9 %collective-permute-done.3.hi = bf16[256,512]{1,0:T(8,128)(2,1)S(1)} collective-permute-done((bf16[256,512]{1,0:T(8,128)(2,1)S(1)}, bf16[256,512]{1,0:T(8,128)(2,1)S(1)}, u32[]{:S(2)}, u32[]{:S(2)}) %collective-permute-start.3) | collective-permute-done | bytes 262176 | tf_op jit(solution)/shard_map/ppermute | solution.py:316
  32.1 1.8 %forward_edge1.1 = (bf16[256,512]{1,0:T(8,128)(2,1)S(1)}, bf16[256,512]{1,0:T(8,128)(2,1)S(1)}, bf16[512,512]{1,0:T(8,128)(2,1)S(1)}, f32[512,512]{1,0:T(8,128)S(1)}) custom-call(s32[4,8]{1,0:T(4,128)S(1)} %bitcast.12, bf16[8,128,512]{2,1,0:T(8,128)(2,1)S(1)} %get-tuple-element.68.adj, bf16[256,512]{1,0:T(8,128)(2,1)S(1)} %collective-permute-done.2.lo, ...), custom_call_target="tpu_custom_call" | custom-call | flops 1 | bytes 1 | tf_op jit(solution)/shard_map/forward_edge1/pallas_call | solution.py:337
  35.2 2.4 %collective-permute-start.5 = (bf16[256,512]{1,0:T(8,128)(2,1)S(1)}, bf16[256,512]{1,0:T(8,128)(2,1)S(1)}, u32[]{:S(2)}, u32[]{:S(2)}) collective-permute-start(bf16[256,512]{1,0:T(8,128)(2,1)S(1)} %get-tuple-element.84.new_lo), channel_id=1, source_target_pairs={{0,112},{16,0},{32,16},{48,32},{64,48},{80,64},{96,80},{112,96},{1... | collective-permute-start | bytes 786440 | tf_op jit(solution)/shard_map/ppermute | solution.py:316
  37.6 2.4 %forward_mid1.1 = (bf16[1024,512]{1,0:T(8,128)(2,1)S(1)}, bf16[1024,512]{1,0:T(8,128)(2,1)S(1)}, f32[1024,512]{1,0:T(8,128)S(1)}, f32[1024,512]{1,0:T(8,128)S(1)}) custom-call(s32[4,8]{1,0:T(4,128)S(1)} %bitcast.13, bf16[8,128,512]{2,1,0:T(8,128)(2,1)S(1)} %get-tuple-element.68.adj, bf16[256,512]{1,0:T(8,128)(2,1)S(1)} %collective-permute-done.2.lo, ...), custom_call_target="tpu_custom_call" | custom-call | flops 1 | bytes 1 | tf_op jit(solution)/shard_map/forward_mid1/pallas_call | solution.py:343
  41.3 4.7 %collective-permute-done.5.hi = bf16[256,512]{1,0:T(8,128)(2,1)S(1)} collective-permute-done((bf16[256,512]{1,0:T(8,128)(2,1)S(1)}, bf16[256,512]{1,0:T(8,128)(2,1)S(1)}, u32[]{:S(2)}, u32[]{:S(2)}) %collective-permute-start.5) | collective-permute-done | bytes 262176 | tf_op jit(solution)/shard_map/ppermute | solution.py:316
  46.0 6.4 %turn.1 = (bf16[1024,512]{1,0:T(8,128)(2,1)}, bf16[1024,512]{1,0:T(8,128)(2,1)S(1)}, bf16[1024,512]{1,0:T(8,128)(2,1)S(1)}, f32[1536,512]{1,0:T(8,128)S(1)}, bf1...) custom-call(s32[4,8]{1,0:T(4,128)S(1)} %bitcast.14, bf16[8,128,512]{2,1,0:T(8,128)(2,1)S(1)} %get-tuple-element.68.adj, ...), custom_call_target="tpu_custom_call" | custom-call | flops 1 | bytes 1 | tf_op jit(solution)/shard_map/turn/pallas_call | solution.py:358
  53.2 2.7 %collective-permute-start.7 = (bf16[256,512]{1,0:T(8,128)(2,1)S(1)}, bf16[256,512]{1,0:T(8,128)(2,1)S(1)}, u32[]{:S(2)}, u32[]{:S(2)}) collective-permute-start(bf16[256,512]{1,0:T(8,128)(2,1)S(1)} %get-tuple-element.93), channel_id=1, source_target_pairs={{0,112},{16,0},{32,16},{48,32},{64,48},{80,64},{96,80},{112,96},{1... | collective-permute-start | bytes 786440 | tf_op jit(solution)/shard_map/ppermute | solution.py:316
  55.9 2.7 %backward_mid2.1 = (f32[1024,512]{1,0:T(8,128)S(1)}, bf16[512,512]{1,0:T(8,128)(2,1)S(1)}, f32[1536,512]{1,0:T(8,128)S(1)}) custom-call(s32[4,8]{1,0:T(4,128)S(1)} %bitcast.15, bf16[8,512,128]{2,1,0:T(8,128)(2,1)S(1)} %get-tuple-element.69.adj_v, bf16[1024,512]{1,0:T(8,128)(2,1)S(1)} %get-tuple-element.94.gp, bf16[1024,512]{1,0:T(8,128)(2,1)S(1)} %bitcast.6, ...), custom_call_target="tpu_custom_call" | custom-call | flops 1 | bytes 1 | tf_op jit(solution)/shard_map/backward_mid2/pallas_call | solution.py:395
  59.7 3.7 %collective-permute-done.7.from_next = bf16[256,512]{1,0:T(8,128)(2,1)S(1)} collective-permute-done((bf16[256,512]{1,0:T(8,128)(2,1)S(1)}, bf16[256,512]{1,0:T(8,128)(2,1)S(1)}, u32[]{:S(2)}, u32[]{:S(2)}) %collective-permute-start.7) | collective-permute-done | bytes 262176 | tf_op jit(solution)/shard_map/ppermute | solution.py:316
  63.4 2.2 %backward_edge1.1 = (f32[1024,512]{1,0:T(8,128)S(1)}, bf16[1024,512]{1,0:T(8,128)(2,1)S(1)}, f32[1536,512]{1,0:T(8,128)S(1)}, bf16[256,512]{1,0:T(8,128)(2,1)S(1)}, bf16[256,512]{1,0:T(8,128)(2,1)S(1)}) custom-call(s32[4,8]{1,0:T(4,128)S(1)} %bitcast.16, bf16[8,512,128]{2,1,0:T(8,128)(2,1)S(1)} %get-tuple-element.69.adj_v, ...), custom_call_target="tpu_custom_call" | custom-call | flops 8999999488 | bytes 1 | tf_op jit(solution)/shard_map/backward_edge1/pallas_call | solution.py:403
  65.7 3.6 %collective-permute-start.9 = (bf16[256,512]{1,0:T(8,128)(2,1)S(1)}, bf16[256,512]{1,0:T(8,128)(2,1)S(1)}, u32[]{:S(2)}, u32[]{:S(2)}) collective-permute-start(bf16[256,512]{1,0:T(8,128)(2,1)S(1)} %get-tuple-element.101), channel_id=1, source_target_pairs={{0,112},{16,0},{32,16},{48,32},{64,48},{80,64},{96,80},{112,96},{1... | collective-permute-start | bytes 786440 | tf_op jit(solution)/shard_map/ppermute | solution.py:316
  70.6 4.6 %collective-permute-start.15 = (bf16[1024,256]{1,0:T(8,128)(2,1)S(1)}, bf16[1024,256]{1,0:T(8,128)(2,1)S(1)}, u32[]{:S(2)}, u32[]{:S(2)}) collective-permute-start(bf16[1024,256]{1,0:T(8,128)(2,1)S(1)} %get-tuple-element.125), channel_id=1, source_target_pairs={{0,1},{1,0},{2,3},{3,2},{4,5},{5,4},{6,7},{7,6},{8,9},{9,8},{10,11... | collective-permute-start | bytes 1572872 | tf_op jit(solution)/shard_map/ppermute | solution.py:380
  75.2 2.6 %backward_mid1.1 = (f32[1024,512]{1,0:T(8,128)S(1)}, bf16[512,512]{1,0:T(8,128)(2,1)S(1)}, f32[1536,512]{1,0:T(8,128)S(1)}) custom-call(s32[4,8]{1,0:T(4,128)S(1)} %bitcast.17, bf16[8,512,128]{2,1,0:T(8,128)(2,1)S(1)} %get-tuple-element.69.adj_v, bf16[1024,512]{1,0:T(8,128)(2,1)S(1)} %get-tuple-element.102.gp, f32[1024,512]{1,0:T(8,128)S(1)} %get-tuple-element.103.grad, ...), custom_call_target="tpu_custom_call" | custom-call | flops 1 | bytes 1 | tf_op jit(solution)/shard_map/backward_mid1/pallas_call | solution.py:395
  79.2 2.2 %backward_edge0.1 = (f32[1024,512]{1,0:T(8,128)S(1)}, bf16[1024,512]{1,0:T(8,128)(2,1)S(1)}, f32[1536,512]{1,0:T(8,128)S(1)}, bf16[256,512]{1,0:T(8,128)(2,1)S(1)}, bf16[256,512]{1,0:T(8,128)(2,1)S(1)}) custom-call(s32[4,8]{1,0:T(4,128)S(1)} %bitcast.18, bf16[8,512,128]{2,1,0:T(8,128)(2,1)S(1)} %get-tuple-element.69.adj_v, ...), custom_call_target="tpu_custom_call" | custom-call | flops 8999999488 | bytes 1 | tf_op jit(solution)/shard_map/backward_edge0/pallas_call | solution.py:403
  81.5 3.6 %collective-permute-start.11 = (bf16[256,512]{1,0:T(8,128)(2,1)S(1)}, bf16[256,512]{1,0:T(8,128)(2,1)S(1)}, u32[]{:S(2)}, u32[]{:S(2)}) collective-permute-start(bf16[256,512]{1,0:T(8,128)(2,1)S(1)} %get-tuple-element.114._), channel_id=1, source_target_pairs={{0,112},{16,0},{32,16},{48,32},{64,48},{80,64},{96,80},{112,96},{1... | collective-permute-start | bytes 786440 | tf_op jit(solution)/shard_map/ppermute | solution.py:316
  89.3 1.7 %collective-permute-start.13 = (bf16[1024,256]{1,0:T(8,128)(2,1)S(1)}, bf16[1024,256]{1,0:T(8,128)(2,1)S(1)}, u32[]{:S(2)}, u32[]{:S(2)}) collective-permute-start(bf16[1024,256]{1,0:T(8,128)(2,1)S(1)} %get-tuple-element.121), channel_id=1, source_target_pairs={{0,1},{1,0},{2,3},{3,2},{4,5},{5,4},{6,7},{7,6},{8,9},{9,8},{10,11... | collective-permute-start | bytes 1572872 | tf_op jit(solution)/shard_map/ppermute | solution.py:380
  91.0 1.6 %collective-permute-done.11.from_next = bf16[256,512]{1,0:T(8,128)(2,1)S(1)} collective-permute-done((bf16[256,512]{1,0:T(8,128)(2,1)S(1)}, bf16[256,512]{1,0:T(8,128)(2,1)S(1)}, u32[]{:S(2)}, u32[]{:S(2)}) %collective-permute-start.11) | collective-permute-done | bytes 262176 | tf_op jit(solution)/shard_map/ppermute | solution.py:316
  93.8 4.0 %collective-permute-done.14.other_1 = bf16[1024,128]{1,0:T(8,128)(2,1)S(1)} collective-permute-done((bf16[1024,128]{1,0:T(8,128)(2,1)S(1)}, bf16[1024,128]{1,0:T(8,128)(2,1)S(1)}, u32[]{:S(2)}, u32[]{:S(2)}) %collective-permute-start.14) | collective-permute-done | bytes 262176 | tf_op jit(solution)/shard_map/ppermute | solution.py:389
  99.1 23.1 %all_to_all.10.parts = bf16[64,32,256]{2,1,0:T(8,128)(2,1)S(1)} all-to-all(bf16[64,32,256]{2,1,0:T(8,128)(2,1)S(1)} %all_parts.1), channel_id=1, replica_groups=mesh['dom'=8,'dq'=8,'core'=2] {'dom','dq'}, dimensions={0} | all-to-all | bytes 2097152 | tf_op jit(solution)/shard_map/all_to_all | solution.py:383
  122.4 25.9 %all_to_all.11.half = bf16[64,48,256]{2,1,0:T(8,128)(2,1)S(1)} all-to-all(bf16[64,48,256]{2,1,0:T(8,128)(2,1)S(1)} %sum_parts.1), channel_id=1, replica_groups=mesh['dom'=8,'dq'=8,'core'=2] {'dom','dq'}, dimensions={0} | all-to-all | bytes 3145728 | tf_op jit(solution)/shard_map/all_to_all | solution.py:383
  148.3 4.9 %collective-permute-start.17 = (bf16[64,48,256]{2,1,0:T(8,128)(2,1)S(1)}, bf16[64,48,256]{2,1,0:T(8,128)(2,1)S(1)}, u32[]{:S(2)}, u32[]{:S(2)}) collective-permute-start(bf16[64,48,256]{2,1,0:T(8,128)(2,1)S(1)} %all_to_all.11.half), channel_id=1, source_target_pairs={{0,1},{1,0},{2,3},{3,2},{4,5},{5,4},{6,7},{7,6},{8,9},{9,8},{10,11... | collective-permute-start | bytes 4718600 | tf_op jit(solution)/shard_map/ppermute | solution.py:422
  153.1 1.7 %unpack_own.1 = (f32[3,512,512]{2,1,0:T(8,128)}, f32[3,512,512]{2,1,0:T(8,128)}) custom-call(bf16[64,48,256]{2,1,0:T(8,128)(2,1)S(1)} %all_to_all.11.half), custom_call_target="tpu_custom_call" | custom-call | flops 1 | bytes 1 | tf_op jit(solution)/shard_map/unpack_own/pallas_call | solution.py:427
  156.1 1.7 %unpack_other.1 = (f32[3,512,512]{2,1,0:T(8,128)}, f32[3,512,512]{2,1,0:T(8,128)}) custom-call(bf16[64,48,256]{2,1,0:T(8,128)(2,1)S(1)} %collective-permute-done.17.half, f32[3,512,512]{2,1,0:T(8,128)} %get-tuple-element.128.refs_0_, f32[3,512,512]{2,1,0:T(8,128)} %get-tuple-element.129.refs_1_), custom_call_target="tpu_custom_call", output_to_operand_aliasing={{0}: (1, {}), {1}: (2, {})} | custom-call | flops 1 | bytes 1 | tf_op jit(solution)/shard_map/unpack_other/pallas_call | solution.py:430
  (47 shorter events, 22.7 us)
Async XLA Ops:
  0.6 1.2 copy-start.1
  1.9 13.5 %collective-permute-start = (bf16[256,512]{1,0:T(8,128)(2,1)S(1)}, bf16[256,512]{1,0:T(8,128)(2,1)S(1)}, u32[]{:S(2)}, u32[]{:S(2)}) collective-permute-start(bf16[256,512]{1,0:T(8,128)(2,1)S(1)} %get-tuple-element.70), channel_id=1, source_target_pairs={{0,16},{16,32},{32,48},{48,64},{64,80},{80,96},{96,112},{112,0},{1... | collective-permute-start | bytes 786440 | tf_op jit(solution)/shard_map/ppermute | solution.py:316
  4.0 12.9 %collective-permute-start.1 = (bf16[256,512]{1,0:T(8,128)(2,1)S(1)}, bf16[256,512]{1,0:T(8,128)(2,1)S(1)}, u32[]{:S(2)}, u32[]{:S(2)}) collective-permute-start(bf16[256,512]{1,0:T(8,128)(2,1)S(1)} %get-tuple-element.71), channel_id=1, source_target_pairs={{0,112},{16,0},{32,16},{48,32},{64,48},{80,64},{96,80},{112,96},{1... | collective-permute-start | bytes 786440 | tf_op jit(solution)/shard_map/ppermute | solution.py:316
  7.6 1.2 copy-start.2
  8.8 1.4 copy-start.3
  10.2 1.4 copy-start.4
  11.6 1.2 copy-start.6
  12.9 0.7 copy-start.8
  13.5 3.5 %copy-start.7 = (s32[8,4]{0,1:T(4,128)S(1)}, s32[8,4]{0,1:T(4,128)}, u32[]{:S(2)}) copy-start(s32[8,4]{0,1:T(4,128)} %param.9) | copy-start | bytes 388
  18.8 8.4 %collective-permute-start.2 = (bf16[256,512]{1,0:T(8,128)(2,1)S(1)}, bf16[256,512]{1,0:T(8,128)(2,1)S(1)}, u32[]{:S(2)}, u32[]{:S(2)}) collective-permute-start(bf16[256,512]{1,0:T(8,128)(2,1)S(1)} %get-tuple-element.75.new_hi), channel_id=1, source_target_pairs={{0,16},{16,32},{32,48},{48,64},{64,80},{80,96},{96,112},{112,0},{1... | collective-permute-start | bytes 786440 | tf_op jit(solution)/shard_map/ppermute | solution.py:316
  20.1 12.0 %collective-permute-start.3 = (bf16[256,512]{1,0:T(8,128)(2,1)S(1)}, bf16[256,512]{1,0:T(8,128)(2,1)S(1)}, u32[]{:S(2)}, u32[]{:S(2)}) collective-permute-start(bf16[256,512]{1,0:T(8,128)(2,1)S(1)} %get-tuple-element.76.new_lo), channel_id=1, source_target_pairs={{0,112},{16,0},{32,16},{48,32},{64,48},{80,64},{96,80},{112,96},{1... | collective-permute-start | bytes 786440 | tf_op jit(solution)/shard_map/ppermute | solution.py:316
  33.9 7.4 %collective-permute-start.4 = (bf16[256,512]{1,0:T(8,128)(2,1)S(1)}, bf16[256,512]{1,0:T(8,128)(2,1)S(1)}, u32[]{:S(2)}, u32[]{:S(2)}) collective-permute-start(bf16[256,512]{1,0:T(8,128)(2,1)S(1)} %get-tuple-element.83.new_hi), channel_id=1, source_target_pairs={{0,16},{16,32},{32,48},{48,64},{64,80},{80,96},{96,112},{112,0},{1... | collective-permute-start | bytes 786440 | tf_op jit(solution)/shard_map/ppermute | solution.py:316
  35.2 10.8 %collective-permute-start.5 = (bf16[256,512]{1,0:T(8,128)(2,1)S(1)}, bf16[256,512]{1,0:T(8,128)(2,1)S(1)}, u32[]{:S(2)}, u32[]{:S(2)}) collective-permute-start(bf16[256,512]{1,0:T(8,128)(2,1)S(1)} %get-tuple-element.84.new_lo), channel_id=1, source_target_pairs={{0,112},{16,0},{32,16},{48,32},{64,48},{80,64},{96,80},{112,96},{1... | collective-permute-start | bytes 786440 | tf_op jit(solution)/shard_map/ppermute | solution.py:316
  37.6 8.4 %copy-start = (bf16[1,1024,512]{2,1,0:T(8,128)(2,1)S(1)}, bf16[1,1024,512]{2,1,0:T(8,128)(2,1)}, u32[]{:S(2)}) copy-start(bf16[1,1024,512]{2,1,0:T(8,128)(2,1)} %param.11) | copy-start | bytes 3145732
  52.3 7.3 %collective-permute-start.6 = (bf16[256,512]{1,0:T(8,128)(2,1)S(1)}, bf16[256,512]{1,0:T(8,128)(2,1)S(1)}, u32[]{:S(2)}, u32[]{:S(2)}) collective-permute-start(bf16[256,512]{1,0:T(8,128)(2,1)S(1)} %get-tuple-element.92), channel_id=1, source_target_pairs={{0,16},{16,32},{32,48},{48,64},{64,80},{80,96},{96,112},{112,0},{1... | collective-permute-start | bytes 786440 | tf_op jit(solution)/shard_map/ppermute | solution.py:316
  53.2 10.2 %collective-permute-start.7 = (bf16[256,512]{1,0:T(8,128)(2,1)S(1)}, bf16[256,512]{1,0:T(8,128)(2,1)S(1)}, u32[]{:S(2)}, u32[]{:S(2)}) collective-permute-start(bf16[256,512]{1,0:T(8,128)(2,1)S(1)} %get-tuple-element.93), channel_id=1, source_target_pairs={{0,112},{16,0},{32,16},{48,32},{64,48},{80,64},{96,80},{112,96},{1... | collective-permute-start | bytes 786440 | tf_op jit(solution)/shard_map/ppermute | solution.py:316
  65.6 13.6 %collective-permute-start.8 = (bf16[256,512]{1,0:T(8,128)(2,1)S(1)}, bf16[256,512]{1,0:T(8,128)(2,1)S(1)}, u32[]{:S(2)}, u32[]{:S(2)}) collective-permute-start(bf16[256,512]{1,0:T(8,128)(2,1)S(1)} %get-tuple-element.100), channel_id=1, source_target_pairs={{0,16},{16,32},{32,48},{48,64},{64,80},{80,96},{96,112},{112,0},{1... | collective-permute-start | bytes 786440 | tf_op jit(solution)/shard_map/ppermute | solution.py:316
  65.7 13.5 %collective-permute-start.9 = (bf16[256,512]{1,0:T(8,128)(2,1)S(1)}, bf16[256,512]{1,0:T(8,128)(2,1)S(1)}, u32[]{:S(2)}, u32[]{:S(2)}) collective-permute-start(bf16[256,512]{1,0:T(8,128)(2,1)S(1)} %get-tuple-element.101), channel_id=1, source_target_pairs={{0,112},{16,0},{32,16},{48,32},{64,48},{80,64},{96,80},{112,96},{1... | collective-permute-start | bytes 786440 | tf_op jit(solution)/shard_map/ppermute | solution.py:316
  70.6 14.5 %collective-permute-start.15 = (bf16[1024,256]{1,0:T(8,128)(2,1)S(1)}, bf16[1024,256]{1,0:T(8,128)(2,1)S(1)}, u32[]{:S(2)}, u32[]{:S(2)}) collective-permute-start(bf16[1024,256]{1,0:T(8,128)(2,1)S(1)} %get-tuple-element.125), channel_id=1, source_target_pairs={{0,1},{1,0},{2,3},{3,2},{4,5},{5,4},{6,7},{7,6},{8,9},{9,8},{10,11... | collective-permute-start | bytes 1572872 | tf_op jit(solution)/shard_map/ppermute | solution.py:380
  79.1 8.2 %collective-permute-start.12 = (bf16[1024,256]{1,0:T(8,128)(2,1)S(1)}, bf16[1024,256]{1,0:T(8,128)(2,1)S(1)}, u32[]{:S(2)}, u32[]{:S(2)}) collective-permute-start(bf16[1024,256]{1,0:T(8,128)(2,1)S(1)} %get-tuple-element.118), channel_id=1, source_target_pairs={{0,1},{1,0},{2,3},{3,2},{4,5},{5,4},{6,7},{7,6},{8,9},{9,8},{10,11... | collective-permute-start | bytes 1572872 | tf_op jit(solution)/shard_map/ppermute | solution.py:380
  81.4 9.6 %collective-permute-start.10 = (bf16[256,512]{1,0:T(8,128)(2,1)S(1)}, bf16[256,512]{1,0:T(8,128)(2,1)S(1)}, u32[]{:S(2)}, u32[]{:S(2)}) collective-permute-start(bf16[256,512]{1,0:T(8,128)(2,1)S(1)} %get-tuple-element.113), channel_id=1, source_target_pairs={{0,16},{16,32},{32,48},{48,64},{64,80},{80,96},{96,112},{112,0},{1... | collective-permute-start | bytes 786440 | tf_op jit(solution)/shard_map/ppermute | solution.py:316
  81.5 11.1 %collective-permute-start.11 = (bf16[256,512]{1,0:T(8,128)(2,1)S(1)}, bf16[256,512]{1,0:T(8,128)(2,1)S(1)}, u32[]{:S(2)}, u32[]{:S(2)}) collective-permute-start(bf16[256,512]{1,0:T(8,128)(2,1)S(1)} %get-tuple-element.114._), channel_id=1, source_target_pairs={{0,112},{16,0},{32,16},{48,32},{64,48},{80,64},{96,80},{112,96},{1... | collective-permute-start | bytes 786440 | tf_op jit(solution)/shard_map/ppermute | solution.py:316
  85.3 8.5 %collective-permute-start.16 = (bf16[1024,128]{1,0:T(8,128)(2,1)S(1)}, bf16[1024,128]{1,0:T(8,128)(2,1)S(1)}, u32[]{:S(2)}, u32[]{:S(2)}) collective-permute-start(bf16[1024,128]{1,0:T(8,128)(2,1)S(1)} %get-tuple-element.127), channel_id=1, source_target_pairs={{0,4},{2,6},{4,0},{6,2},{8,12},{10,14},{12,8},{14,10},{1,5},{3,7},... | collective-permute-start | bytes 786440 | tf_op jit(solution)/shard_map/ppermute | solution.py:389
  87.6 10.1 %collective-permute-start.14 = (bf16[1024,128]{1,0:T(8,128)(2,1)S(1)}, bf16[1024,128]{1,0:T(8,128)(2,1)S(1)}, u32[]{:S(2)}, u32[]{:S(2)}) collective-permute-start(bf16[1024,128]{1,0:T(8,128)(2,1)S(1)} %get-tuple-element.122), channel_id=1, source_target_pairs={{0,4},{2,6},{4,0},{6,2},{8,12},{10,14},{12,8},{14,10},{1,5},{3,7},... | collective-permute-start | bytes 786440 | tf_op jit(solution)/shard_map/ppermute | solution.py:389
  89.3 8.5 %collective-permute-start.13 = (bf16[1024,256]{1,0:T(8,128)(2,1)S(1)}, bf16[1024,256]{1,0:T(8,128)(2,1)S(1)}, u32[]{:S(2)}, u32[]{:S(2)}) collective-permute-start(bf16[1024,256]{1,0:T(8,128)(2,1)S(1)} %get-tuple-element.121), channel_id=1, source_target_pairs={{0,1},{1,0},{2,3},{3,2},{4,5},{5,4},{6,7},{7,6},{8,9},{9,8},{10,11... | collective-permute-start | bytes 1572872 | tf_op jit(solution)/shard_map/ppermute | solution.py:380
  97.7 1.2 copy-start.5
  148.3 7.9 %collective-permute-start.17 = (bf16[64,48,256]{2,1,0:T(8,128)(2,1)S(1)}, bf16[64,48,256]{2,1,0:T(8,128)(2,1)S(1)}, u32[]{:S(2)}, u32[]{:S(2)}) collective-permute-start(bf16[64,48,256]{2,1,0:T(8,128)(2,1)S(1)} %all_to_all.11.half), channel_id=1, source_target_pairs={{0,1},{1,0},{2,3},{3,2},{4,5},{5,4},{6,7},{7,6},{8,9},{9,8},{10,11... | collective-permute-start | bytes 4718600 | tf_op jit(solution)/shard_map/ppermute | solution.py:422
